TPU v7x, 512 devices: a whole 4x8x8 slice. The times are simulated.
512 devices in a mesh: seq: 64 (over y, z), head: 8 (over x, core).
Axes of the slice: x: 4, y: 8, z: 8, core: 2. Of those that a mesh axis runs over, the one named last changes fastest.
Arguments:
- enc_rows: bfloat16 [36864, 1024], P('seq', 'head'), may hold values from -1.5 to 1.5
- boundary_flags: int32 [36864], P('seq'), may hold values from 0 to 1, as said below
- boundary_prob: bfloat16 [36864], P('seq'), may hold values from 0.0001 to 0.99
- pad_vector: float32 [1024], replicated, may hold values from -6 to 6
- norm_gain: float32 [1024], replicated, may hold values from 0.25 to 1.75
- w_in: bfloat16 [1024, 10240], P(None, 'head'), may hold values from -0.125 to 0.125
- w_dt: bfloat16 [1024, 64], P(None, 'head'), may hold values from -0.125 to 0.125
- pad_proj: float32 [10240], P('head'), may hold values from -4 to 4
- pad_dt: float32 [64], P('head'), may hold values from -4 to 4
- dt_bias: float32 [64], P('head'), may hold values from -4 to -1
- a_log: float32 [64], P('head'), may hold values from -8.1 to -0.7
- d_skip: float32 [64], P('head'), may hold values from 0.5 to 1.5
- gate_gain: float32 [4096], P('head'), may hold values from 0.25 to 1.75
- w_out: bfloat16 [4096, 1024], P('head'), may hold values from -0.125 to 0.125
Outputs:
- decoded: bfloat16 [36864, 1024], P('seq', 'head')
Inputs may be any that keep to these rules, and one draw needn't show every extreme that they name: `boundary_flags`: exactly 9216 flags are 1; the 576 bytes of one index of seq hold at most 432 ones, and those of some index hold exactly 432. The first 18432 bytes hold no ones.
All inputs are finite; a program needn't handle non-finite values.
Results may differ from a plain program's by a relative error of at most 0.0096.
The roundings to bfloat16 on the way count: a program that leaves them out, or rounds other values in their place, can miss the bound.
Values may be sent and summed in bfloat16 or wider, within the bound.
No kernel may reach another device: no remote copies, remote signals or barrier semaphores. Data moves between devices by JAX's collectives and lax.ppermute only.
A program may use at most 64 MiB of HBM per device.

v0:
```python
import jax
import jax.numpy as jnp
from jax import lax
from jax.sharding import PartitionSpec as P

E = 2048
HEADS = 64
P_SIZE = 64
N = 128
GROUPS = 8
CH_DEV = 144
CAP = 432


eps = 1e-05
highest = lax.Precision.HIGHEST


def carried_in(part, axis, combine, identity):
    place = lax.axis_index(axis)
    gathered = jax.tree.map(lambda a: lax.all_gather(a, axis), part)
    state = jax.tree.map(lambda a, e: jnp.zeros_like(a) + jnp.asarray(e, a.dtype), part, identity)

    def one(step, state):
        return combine(
            state, jax.tree.map(lambda a: lax.dynamic_index_in_dim(a, step, 0, False), gathered)
        )

    return lax.fori_loop(0, place, one, state)


def state_block(inputs, step_sizes, b_proj, c_proj, decay_rates):
    log_decay = -decay_rates[None] * step_sizes
    running = jnp.cumsum(log_decay, axis=0)
    length = inputs.shape[0]
    lower_mask = jnp.arange(length)[:, None] >= jnp.arange(length)[None, :]
    by_head = jnp.transpose(running, (1, 2, 0))
    spread = by_head[:, :, :, None] - by_head[:, :, None, :]
    decay_mask = jnp.exp(jnp.where(lower_mask, spread, -jnp.inf))
    intersection = jnp.einsum("ign,jgn->gij", c_proj, b_proj, precision=highest)
    weights = (
        intersection[:, None] * decay_mask * jnp.transpose(step_sizes, (1, 2, 0))[:, :, None, :]
    )
    local_out = jnp.einsum("gkij,jgkp->igkp", weights, inputs, precision=highest)
    tail_weight = jnp.exp(running[-1][None] - running) * step_sizes
    local_state = jnp.einsum("jgk,jgkp,jgn->gkpn", tail_weight, inputs, b_proj, precision=highest)
    return (local_out, running, local_state, jnp.exp(running[-1]))


def carried_out(c_proj, running, state_in):
    return jnp.exp(running)[..., None] * jnp.einsum(
        "ign,gkpn->igkp", c_proj, state_in, precision=highest
    )


def normalize(rows_half, pad_vector, norm_gain):
    rows_wide = rows_half.astype(jnp.float32)
    energy = jnp.sum(rows_wide * rows_wide, axis=1) + jnp.sum(pad_vector * pad_vector)
    inverse = lax.rsqrt(energy / E + eps)
    normed = (rows_wide * inverse[:, None] * norm_gain[None, :]).astype(jnp.bfloat16)
    return (normed, inverse)


def project(normed, inverse, w_in, w_dt, pad_proj, pad_dt, dt_bias):
    projected = (
        jnp.dot(normed, w_in, preferred_element_type=jnp.float32)
        + inverse[:, None] * pad_proj[None, :]
    )
    step_raw = (
        jnp.dot(normed, w_dt, preferred_element_type=jnp.float32)
        + inverse[:, None] * pad_dt[None, :]
        + dt_bias[None, :]
    )
    return (projected, jax.nn.softplus(step_raw))


def split_columns(projected, group_count):
    rows_here = projected.shape[0]
    group_heads = HEADS // GROUPS
    inner_width = group_heads * P_SIZE
    shaped = projected.reshape(rows_here, group_count, 2 * inner_width + 2 * N)
    gate_part = shaped[:, :, :inner_width].reshape(rows_here, group_count, group_heads, P_SIZE)
    inner_part = shaped[:, :, inner_width : 2 * inner_width].reshape(
        rows_here, group_count, group_heads, P_SIZE
    )
    b_proj = shaped[:, :, 2 * inner_width : 2 * inner_width + N]
    c_proj = shaped[:, :, 2 * inner_width + N :]
    return (gate_part, inner_part, b_proj, c_proj)


def gated_norm(gate_part, ssm_out, gate_gain):
    gated = ssm_out * jax.nn.silu(gate_part)
    power = jnp.mean(gated * gated, axis=(2, 3))
    shaped_gain = gate_gain.reshape(1, gated.shape[1], gated.shape[2], gated.shape[3])
    scaled = gated * lax.rsqrt(power + eps)[:, :, None, None] * shaped_gain
    return scaled.astype(jnp.bfloat16).reshape(gated.shape[0], -1)


def compact_rows(values, boundary_flags, capacity):
    position = jnp.cumsum(boundary_flags) - 1
    target = jnp.where(boundary_flags > 0, position, capacity)
    holder = jnp.zeros((capacity + 1,) + values.shape[1:], values.dtype)
    return holder.at[target].set(values)[:capacity]


def pick_entry(table, wanted):
    source_hit = jnp.arange(table.shape[0]) == wanted
    return jnp.sum(jnp.where(source_hit, table, 0)).astype(jnp.int32)


def chain_states(earlier, later):
    return (earlier[0] * later[0], later[0][..., None, None] * earlier[1] + later[1])


def ema_weights(prob_line):
    forget = jnp.cumsum(jnp.log1p(-prob_line))
    span = prob_line.shape[0]
    lower_mask = jnp.arange(span)[:, None] >= jnp.arange(span)[None, :]
    log_gap = jnp.where(lower_mask, forget[:, None] - forget[None, :], 0.0)
    return (jnp.where(lower_mask, prob_line[None, :] * jnp.exp(log_gap), 0.0), forget)


def body(
    enc_rows,
    boundary_flags,
    boundary_prob,
    pad_vector,
    norm_gain,
    w_in,
    w_dt,
    pad_proj,
    pad_dt,
    dt_bias,
    a_log,
    d_skip,
    gate_gain,
    w_out,
):
    seq_count = lax.axis_size("seq")
    seq_index = lax.axis_index("seq")
    per_shard = CH_DEV
    width_part = enc_rows.shape[1]
    local_count = jnp.sum(boundary_flags)
    packed_rows = compact_rows(enc_rows, boundary_flags, CAP)
    packed_prob = compact_rows(boundary_prob, boundary_flags, CAP)
    all_rows, all_prob, shard_counts = (
        lax.all_gather(packed_rows, "seq", axis=0, tiled=True),
        lax.all_gather(packed_prob, "seq", axis=0, tiled=True),
        lax.all_gather(local_count[None], "seq", axis=0, tiled=True),
    )
    source_end = jnp.cumsum(shard_counts)
    shard_starts = source_end - shard_counts
    my_start = pick_entry(shard_starts, seq_index)
    targets = seq_index * per_shard + jnp.arange(per_shard)
    source = jnp.sum((source_end[None, :] <= targets[:, None]).astype(jnp.int32), axis=1)
    source_hit = jnp.arange(seq_count)[None, :] == source[:, None]
    source_begin = jnp.sum(jnp.where(source_hit, shard_starts[None, :], 0), axis=1)
    row_index = (source * CAP + targets - source_begin).astype(jnp.int32)
    my_rows = jnp.take(all_rows, row_index, axis=0)
    my_prob = jnp.take(all_prob, row_index, axis=0)
    full_rows = lax.all_gather(my_rows, "head", axis=1, tiled=True)
    normed, inverse = normalize(full_rows, pad_vector, norm_gain)
    projected, step_sizes = project(normed, inverse, w_in, w_dt, pad_proj, pad_dt, dt_bias)
    group_heads = HEADS // GROUPS
    groups_here = step_sizes.shape[1] // group_heads
    gate_part, inner_part, b_proj, c_proj = split_columns(projected, groups_here)
    step_grid = step_sizes.reshape(per_shard, groups_here, group_heads)
    decay_rates = jnp.exp(a_log).reshape(groups_here, group_heads)
    local_out, running, local_state, total_decay = state_block(
        inner_part, step_grid, b_proj, c_proj, decay_rates
    )
    identity = (jnp.ones_like(total_decay), jnp.zeros_like(local_state))
    _, state_in = carried_in((total_decay, local_state), "seq", chain_states, identity)
    ssm_out = (
        local_out
        + carried_out(c_proj, running, state_in)
        + d_skip.reshape(1, groups_here, group_heads, 1) * inner_part
    )
    mixed = gated_norm(gate_part, ssm_out, gate_gain)
    partial_sum = jnp.dot(mixed, w_out, preferred_element_type=jnp.float32)
    summed = lax.psum_scatter(partial_sum, "head", scatter_dimension=1, tiled=True)
    main_part = (my_rows.astype(jnp.float32) + summed).astype(jnp.bfloat16)
    all_main, all_weight = (
        lax.all_gather(main_part, "seq", axis=0, tiled=True),
        lax.all_gather(my_prob, "seq", axis=0, tiled=True),
    )
    all_chance = all_weight.astype(jnp.float32)
    total_rows = all_main.shape[0]
    earlier_mask = jnp.arange(total_rows) < my_start
    log_keep = jnp.where(earlier_mask, jnp.log1p(-all_chance), 0.0)
    later_keep = jnp.cumsum(log_keep[::-1])[::-1] - log_keep
    carry_weight = jnp.where(earlier_mask, all_chance * jnp.exp(later_keep), 0.0)
    main_wide = all_main.astype(jnp.float32)
    carry_row = jnp.dot(carry_weight, main_wide, precision=highest)
    padded_rows = jnp.concatenate([main_wide, jnp.zeros((CAP, width_part), jnp.float32)], axis=0)
    padded_prob = jnp.concatenate([all_chance, jnp.zeros((CAP,), jnp.float32)], axis=0)
    window_rows = lax.dynamic_slice_in_dim(padded_rows, my_start, CAP, 0)
    window_prob = lax.dynamic_slice_in_dim(padded_prob, my_start, CAP, 0)
    weights, window_forget = ema_weights(window_prob)
    smoothed = (
        jnp.dot(weights, window_rows, precision=highest)
        + jnp.exp(window_forget)[:, None] * carry_row[None, :]
    )
    with_carry = jnp.concatenate([carry_row[None, :], smoothed], axis=0)
    local_index = jnp.cumsum(boundary_flags)
    chosen_rows = jnp.take(with_carry, local_index, axis=0)
    return (enc_rows.astype(jnp.float32) + chosen_rows).astype(jnp.bfloat16)


def solution(mesh):
    in_specs = (
        P("seq", "head"),
        P("seq"),
        P("seq"),
        P(),
        P(),
        P(None, "head"),
        P(None, "head"),
        P("head"),
        P("head"),
        P("head"),
        P("head"),
        P("head"),
        P("head"),
        P("head", None),
    )
    out_specs = P("seq", "head")
    return jax.shard_map(body, mesh=mesh, in_specs=in_specs, out_specs=out_specs, check_vma=False)
```

profile of v0, /device:TPU:6, one launch (start us, length us, event | category | flops | bytes accessed | tf_op | source)
XLA Modules:
  0.0 899.3 jit_solution(7221391797481737297)
XLA Ops:
  6.6 0.8 pad_bitcast_fusion.1
  8.0 1.4 compare_select_fusion.2
  9.4 4.6 scatter_custom_fusion.1
  14.7 1.2 dynamic-slice
  15.9 1.3 dynamic-update-slice
  17.2 30.9 %all-reduce.5 = s32[64]{0:T(128)S(1)} all-reduce(s32[64]{0:T(128)S(1)} %dynamic-update-slice), channel_id=1, replica_groups=mesh['seq'=64,'head'=8] {'seq'}, use_global_device_ids=true, to_apply=%add.5 | all-reduce | flops 64 | bytes 512
  48.5 8.8 scatter_custom_fusion
  58.1 276.0 %all-reduce.6 = bf16[27648]{0:T(1024)(128)(2,1)S(1)} all-reduce(bf16[27648]{0:T(1024)(128)(2,1)S(1)} %dynamic-update-slice.1), channel_id=1, replica_groups=mesh['seq'=64,'head'=8] {'seq'}, use_global_device_ids=true, to_apply=%add.6 | all-reduce | flops 27648 | bytes 110592
  334.9 1.6 gather_fusion
  336.6 1.3 multiply_reduce_fusion.1
  337.9 0.7 exponential_negate_fusion
  338.6 4.6 gather_fusion.1
  343.3 11.5 %all_gather.32 = bf16[144,1024]{1,0:T(8,128)(2,1)S(1)} all-gather(bf16[144,128]{1,0:T(8,128)(2,1)S(1)} %broadcast_select_fusion), channel_id=1, replica_groups=mesh['seq'=64,'head'=8] {'head'}, dimensions={1}, use_global_device_ids=true | all-gather | bytes 331776 | tf_op jit(solution)/shard_map/all_gather | solution.py:161
  357.3 1.6 fusion
  358.9 1.0 fusion.57
  359.9 1.9 reshape.321
  361.8 1.3 broadcast_multiply_fusion
  363.1 2.1 fusion.19
  365.4 2.0 copy.54
  367.5 2.0 copy.55
  369.4 37.5 %all_gather.33 = f32[64,1,8]{2,1,0:T(1,128)S(1)} all-gather(f32[1,1,8]{2,1,0:T(1,128)S(1)} %copy.47), channel_id=1, replica_groups=mesh['seq'=64,'head'=8] {'seq'}, dimensions={0}, use_global_device_ids=true | all-gather | bytes 2080 | tf_op jit(solution)/shard_map/all_gather | solution.py:21
  407.2 3.6 convolution_bitcast_fusion.1
  410.9 88.0 %all-gather.9.cloned.1.call-done = f32[512,64,128]{2,1,0:T(8,128)} async-done(((f32[8,64,128]{2,1,0:T(8,128)}), f32[512,64,128]{2,1,0:T(8,128)}) %all-gather.9.cloned.1.call-update) | async-done | bytes 16777232 | tf_op jit(solution)/shard_map/all_gather | solution.py:21
  498.9 2.0 multiply_reduce_fusion
  501.2 1.2 fusion.58
  502.4 97.1 %reduce-scatter.2.cloned.1.call-done = f32[144,128]{1,0:T(8,128)} async-done(((f32[144,1024]{1,0:T(8,128)}), f32[144,128]{1,0:T(8,128)}) %reduce-scatter.2.cloned.1.call-update) | async-done | bytes 73744 | tf_op jit(solution)/shard_map/reduce_scatter | solution.py:181
  599.5 1.6 add_convert_fusion.1
  601.9 280.2 %all-reduce.7 = bf16[9216]{0:T(1024)(128)(2,1)S(1)} all-reduce(bf16[9216]{0:T(1024)(128)(2,1)S(1)} %dynamic-update-slice.2), channel_id=1, replica_groups=mesh['seq'=64,'head'=8] {'seq'}, use_global_device_ids=true, to_apply=%add.7 | all-reduce | flops 9216 | bytes 36864
  886.7 2.8 fusion.59
  889.6 0.7 convolution_add_fusion.1
  890.3 1.6 gather_fusion.2
  892.0 0.8 add_convert_fusion
  (103 shorter events, 9.1 us)
Async XLA Ops:
  6.5 350.7 %copy-start = (bf16[1024,1280]{1,0:T(8,128)(2,1)S(1)}, bf16[1024,1280]{1,0:T(8,128)(2,1)}, u32[]{:S(2)}) copy-start(bf16[1024,1280]{1,0:T(8,128)(2,1)} %param.21) | copy-start | bytes 7864324
  6.5 349.1 %copy-start.8 = (f32[1024]{0:T(1024)S(1)}, f32[1024]{0:T(1024)}, u32[]{:S(2)}) copy-start(f32[1024]{0:T(1024)} %param.20) | copy-start | bytes 12292
  6.5 349.1 %copy-start.10 = (bf16[1024,8]{0,1:T(8,128)(2,1)S(1)}, bf16[1024,8]{0,1:T(8,128)(2,1)}, u32[]{:S(2)}) copy-start(bf16[1024,8]{0,1:T(8,128)(2,1)} %param.22) | copy-start | bytes 49156
  6.5 349.1 %copy-start.12 = (f32[8]{0:T(128)S(1)}, f32[8]{0:T(128)}, u32[]{:S(2)}) copy-start(f32[8]{0:T(128)} %param.24) | copy-start | bytes 100
  6.5 349.1 %copy-start.11 = (f32[8]{0:T(128)S(1)}, f32[8]{0:T(128)}, u32[]{:S(2)}) copy-start(f32[8]{0:T(128)} %param.25) | copy-start | bytes 100
  6.5 350.7 %copy-start.7 = (f32[1280]{0:T(1024)S(1)}, f32[1280]{0:T(1024)}, u32[]{:S(2)}) copy-start(f32[1280]{0:T(1024)} %param.23) | copy-start | bytes 15364
  6.6 332.0 %all-gather.5.cloned.1.call-start = ((), (), s32[]{:S(2)}) async-start(), calls=%async_computation.1 | async-start | bytes 7188480 | tf_op jit(solution)/shard_map/all_gather | solution.py:147
  14.6 484.2 %all-gather.9.cloned.1.call-start = ((), (), s32[]{:S(2)}) async-start(), calls=%async_computation.4 | async-start | bytes 17039360 | tf_op jit(solution)/shard_map/all_gather | solution.py:21
  354.8 0.8 copy-start.3
  358.8 48.1 %copy-start.2 = (f32[144,1,1280]{2,0,1:T(8,128)}, f32[144,1,1280]{2,0,1:T(8,128)S(1)}, u32[]{:S(2)}) copy-start(f32[144,1,1280]{2,0,1:T(8,128)S(1)} %fusion) | copy-start | bytes 2211844
  358.8 6.5 copy-start.9
  365.2 234.3 %reduce-scatter.2.cloned.1.call-start = ((), (), s32[]{:S(2)}) async-start(), calls=%async_computation.2 | async-start | bytes 663552 | tf_op jit(solution)/shard_map/reduce_scatter | solution.py:181
  410.9 88.1 %copy-start.5 = (f32[144,1,512]{0,2,1:T(8,128)S(1)}, f32[144,1,512]{0,2,1:T(8,128)}, u32[]{:S(2)}) copy-start(f32[144,1,512]{0,2,1:T(8,128)} %copy.54) | copy-start | bytes 884740
  410.9 88.1 %copy-start.13 = (f32[8]{0:T(128)S(1)}, f32[8]{0:T(128)}, u32[]{:S(2)}) copy-start(f32[8]{0:T(128)} %param.27) | copy-start | bytes 100
  498.9 2.2 copy-start.4
  502.3 384.4 %all-gather.7.cloned.1.call-start = ((), (), s32[]{:S(2)}) async-start(), calls=%async_computation.3 | async-start | bytes 2396160 | tf_op jit(solution)/shard_map/all_gather | solution.py:184
  886.7 2.9 copy-start.1
  889.6 2.4 copy-start.6
Sparse Core Ops, SparseCore 0:
  14.8 99.1 all-gather.4
  365.4 133.4 all-gather.8
  502.5 97.0 reduce-scatter.1
  602.4 86.1 all-gather.6
where the time goes:
time: 903 us; the launch traced here: 899 us
  blocking collectives  636 us (70%)
  waiting for transfers between devices  185 us (20%)
  local copies, waits for them, and re-layouts  34.1 us (4%)
  between operations  16.4 us (2%)
  matrix products  14.7 us (2%)
  other arithmetic  12.5 us (1%)
    unnamed x3, blocking collectives  587 us
    reduce_scatter x1, waiting for transfers between devices, body(): lax.psum_scatter(partial_sum, 'head', scatter_dimension=1, tiled=True)  97.1 us
    all_gather x1, waiting for transfers between devices, carried_in(): gathered = jax.tree.map(lambda a: lax.all_gather(a, axis), part)  88 us
    all_gather x1, blocking collectives, carried_in(): gathered = jax.tree.map(lambda a: lax.all_gather(a, axis), part)  37.5 us
  transfers between devices with their start and end apart: 4, of which 2 were waited for; matrix products, arithmetic and copies ran while one was open for 3% of the time, Pallas kernels for 0%

commit v1 on v0

v1 whole, which is shorter than its diff:
```python
import jax
import jax.numpy as jnp
from jax import lax
from jax.sharding import Mesh
from jax.sharding import PartitionSpec as P

D = 1024
E = 2048
N = 128
HEADS_HERE = 8
P_SIZE = 64
INNER = HEADS_HERE * P_SIZE
CAP = 432
eps = 1e-05
F32 = jnp.float32
BF16 = jnp.bfloat16
highest = lax.Precision.HIGHEST


def dot(a, b, precision=None):
    return jnp.dot(a, b, preferred_element_type=F32, precision=precision)


def spread_heads(a):
    return jnp.repeat(a, P_SIZE, axis=-1)


def body(
    enc_rows,
    boundary_flags,
    boundary_prob,
    pad_vector,
    norm_gain,
    w_in,
    w_dt,
    pad_proj,
    pad_dt,
    dt_bias,
    a_log,
    d_skip,
    gate_gain,
    w_out,
):
    act = lax.axis_size("act")
    me = lax.axis_index("act")
    heads = lax.axis_size("head")
    rank = jnp.cumsum(boundary_flags)
    hit = (rank[None, :] - 1 == jnp.arange(CAP)[:, None]) & (boundary_flags > 0)[None, :]
    hit_bf = hit.astype(BF16)
    packed = dot(hit_bf, enc_rows).astype(BF16)
    prob = dot(hit_bf, boundary_prob[:, None])[:, 0]
    valid = jnp.arange(CAP) < rank[-1]

    full = lax.all_gather(packed, "head", axis=1, tiled=True)
    wide = full.astype(F32)
    energy = jnp.sum(wide * wide, axis=1) + jnp.sum(pad_vector * pad_vector)
    inverse = lax.rsqrt(energy / E + eps)
    normed = (wide * inverse[:, None] * norm_gain[None, :]).astype(BF16)
    projected = dot(normed, w_in) + inverse[:, None] * pad_proj[None, :]
    step = jax.nn.softplus(dot(normed, w_dt) + inverse[:, None] * pad_dt[None, :] + dt_bias[None, :])
    step = jnp.where(valid[:, None], step, 0.0)
    gate = projected[:, :INNER]
    x = projected[:, INNER : 2 * INNER]
    b = projected[:, 2 * INNER : 2 * INNER + N]
    c = projected[:, 2 * INNER + N :]
    running = jnp.cumsum(-jnp.exp(a_log)[None, :] * step, axis=0)
    total = running[-1]
    tail = jnp.exp(total[None, :] - running) * step
    local_state = dot(b.T, x * spread_heads(tail), highest)

    slices = local_state.reshape(act, N // act, INNER)
    logs = jnp.broadcast_to(spread_heads(total)[None, None, :], (act, 1, INNER))
    got = lax.all_to_all(jnp.concatenate([slices, logs], axis=1), "act", 0, 0)
    state = jnp.zeros_like(got[0, :-1])
    before = []
    for j in range(act):
        before.append(state)
        state = state * jnp.exp(got[j, -1])[None, :] + got[j, :-1]
    state_in = lax.all_to_all(jnp.stack(before), "act", 0, 0).reshape(N, INNER)

    lower = jnp.arange(CAP)[:, None] >= jnp.arange(CAP)[None, :]
    inter = dot(c, b.T, highest)
    outs = []
    for k in range(HEADS_HERE):
        gap = running[:, k][:, None] - running[:, k][None, :]
        w = inter * jnp.exp(jnp.where(lower, gap, -jnp.inf)) * step[:, k][None, :]
        outs.append(dot(w, x[:, k * P_SIZE : (k + 1) * P_SIZE], highest))
    ssm = jnp.concatenate(outs, axis=1)
    ssm = ssm + spread_heads(jnp.exp(running)) * dot(c, state_in.astype(F32), highest) + spread_heads(d_skip)[None, :] * x
    gated = ssm * gate / (1.0 + jnp.exp(-gate))
    power = jnp.mean(gated * gated, axis=1, keepdims=True)
    mixed = (gated * lax.rsqrt(power + eps) * gate_gain[None, :]).astype(BF16)
    partial = dot(mixed, w_out).astype(BF16)
    parts = jnp.transpose(partial.reshape(CAP, heads, -1), (1, 0, 2))
    summed = jnp.sum(lax.all_to_all(parts, "head", 0, 0).astype(F32), axis=0)
    main = (packed.astype(F32) + summed).astype(BF16)

    kept = jnp.cumsum(jnp.log1p(-prob))
    all_kept = kept[-1]
    carry = dot((prob * jnp.exp(all_kept - kept))[None, :], main.astype(F32), highest)
    sent = jnp.concatenate([carry, jnp.broadcast_to(all_kept[None, None], carry.shape)], axis=1)
    carries = lax.all_gather(sent, "act", axis=0, tiled=True)
    rows_c, logs_c = carries[:, : carry.shape[1]], carries[:, carry.shape[1]]
    earlier = jnp.arange(act) < me
    seen = jnp.where(earlier, logs_c, 0.0)
    later = jnp.cumsum(seen[::-1])[::-1] - seen
    weight = jnp.where(earlier, jnp.exp(later), 0.0)
    carry_in = jnp.sum(weight[:, None] * rows_c, axis=0)

    byte_kept = jnp.cumsum(jnp.where(boundary_flags > 0, jnp.log1p(-boundary_prob.astype(F32)), 0.0))
    covers = jnp.arange(CAP)[None, :] < rank[:, None]
    byte_gap = jnp.where(covers, byte_kept[:, None] - kept[None, :], -jnp.inf)
    w = jnp.exp(byte_gap) * prob[None, :]
    w_hi = w.astype(BF16)
    w_lo = (w - w_hi.astype(F32)).astype(BF16)
    smoothed = dot(w_hi, main) + dot(w_lo, main) + jnp.exp(byte_kept)[:, None] * carry_in[None, :]
    return (enc_rows.astype(F32) + smoothed).astype(BF16)


def solution(mesh):
    seq, heads = mesh.shape["seq"], mesh.shape["head"]
    split = Mesh(mesh.devices.reshape(2, seq // 2, heads), ("half", "act", "head"))
    seq_axes = ("half", "act")
    in_specs = (
        P(seq_axes, "head"),
        P(seq_axes),
        P(seq_axes),
        P(),
        P(),
        P(None, "head"),
        P(None, "head"),
        P("head"),
        P("head"),
        P("head"),
        P("head"),
        P("head"),
        P("head"),
        P("head", None),
    )
    return jax.shard_map(
        body, mesh=split, in_specs=in_specs, out_specs=P(seq_axes, "head"), check_vma=False
    )
```

time: 903 us -> 235 us (0.26)
  blocking collectives: 636 us -> 91.9 us
  waiting for transfers between devices: 185 us -> 14.8 us
  other arithmetic: 12.5 us -> 43.7 us
  starting transfers between devices: 0.16 us -> 25.7 us
  matrix products: 14.7 us -> 36.2 us
  between operations: 16.4 us -> 0.48 us
  local copies, waits for them, and re-layouts: 34.1 us -> 18.7 us
    unnamed x3 -> x0, blocking collectives: 587 us -> none
    reduce_scatter x1 -> x0, waiting for transfers between devices: 97.1 us -> none  [body(): lax.psum_scatter(partial_sum, 'head', scatter_dimension=1, tiled=True)]
    all_gather x3 -> x0, waiting for transfers between devices: 88 us -> none  [the longest x1 88 us: carried_in(): gathered = jax.tree.map(lambda a: lax.all_gather(a, axis), part)]
    all_gather x2, blocking collectives: 49 us -> 91.9 us  [the longest x1 75.3 us: body(): carries = lax.all_gather(sent, 'act', axis=0, tiled=True)]
    unnamed x0 -> x30, other arithmetic: none -> 31.9 us
    all_to_all x0 -> x3, starting transfers between devices: none -> 25.7 us  [the longest x1 10.6 us: body(): got = lax.all_to_all(jnp.concatenate([slices, logs], axis=1), 'act', 0, 0)]
    dot_general x9 -> x19, matrix products: 14.7 us -> 36.2 us  [dot(): return jnp.dot(a, b, preferred_element_type=F32, precision=precision)]
    all_to_all x0 -> x3, waiting for transfers between devices: none -> 14.8 us  [the longest x1 11.3 us: body(): summed = jnp.sum(lax.all_to_all(parts, 'head', 0, 0).astype(F32), axis=0)]
  transfers between devices with their start and end apart: 4 -> 3, of which waited for: 2 -> 2; matrix products, arithmetic and copies ran while one was open for 3% -> 15% of each run, Pallas kernels for 0% -> 0%
where the time goes in v1:
time: 235 us; the launch traced here: 231 us
  blocking collectives  91.9 us (39%)
  other arithmetic  43.7 us (19%)
  matrix products  36.2 us (15%)
  starting transfers between devices  25.7 us (11%)
  local copies, waits for them, and re-layouts  18.7 us (8%)
  waiting for transfers between devices  14.8 us (6%)
    all_gather x1, blocking collectives, body(): carries = lax.all_gather(sent, 'act', axis=0, tiled=True)  75.3 us
    dot_general x19, matrix products, dot(): return jnp.dot(a, b, preferred_element_type=F32, precision=precision)  36.2 us
    unnamed x30, other arithmetic  31.9 us
    all_gather x1, blocking collectives, body(): full = lax.all_gather(packed, 'head', axis=1, tiled=True)  16.7 us
    all_to_all x1, waiting for transfers between devices, body(): summed = jnp.sum(lax.all_to_all(parts, 'head', 0, 0).astype(F32), axis=0)  11.3 us
    all_to_all x1, starting transfers between devices, body(): got = lax.all_to_all(jnp.concatenate([slices, logs], axis=1), 'act', 0, 0)  10.6 us
    all_to_all x1, starting transfers between devices, body(): state_in = lax.all_to_all(jnp.stack(before), 'act', 0, 0).reshape(N, INNER)  10.2 us
    reshape x2, local copies, waits for them, and re-layouts, spread_heads(): return jnp.repeat(a, P_SIZE, axis=-1)  4.93 us
  transfers between devices with their start and end apart: 3, of which 2 were waited for; matrix products, arithmetic and copies ran while one was open for 15% of the time, Pallas kernels for 0%

profile of v1, /device:TPU:6, one launch (start us, length us, event | category | flops | bytes accessed | tf_op | source)
XLA Modules:
  0.0 231.5 jit_solution(1215879044576601866)
XLA Ops:
  6.0 16.7 %all_gather.6 = bf16[432,1024]{1,0:T(8,128)(2,1)S(1)} all-gather(bf16[432,128]{1,0:T(8,128)(2,1)S(1)} %convolution_convert_fusion.1), channel_id=1, replica_groups=mesh['half'=2,'act'=32,'head'=8] {'head'}, dimensions={1}, use_global_device_ids=true | all-gather | bytes 995328 | tf_op jit(solution)/shard_map/all_gather | solution.py:54
  30.3 2.5 %copy.56 = f32[432,512]{1,0:T(8,128)} copy(f32[432,512]{0,1:T(8,128)} %bitcast.102) | data formatting | bytes 1769472 | tf_op jit(solution)/shard_map/reshape | solution.py:25
  32.7 2.2 convolution_add_fusion
  34.9 1.4 copy-done.3
  38.3 10.6 %all-to-all-start = ((f32[32,5,512]{2,1,0:T(8,128)}), f32[32,5,512]{2,1,0:T(8,128)S(1)}, u32[]{:S(2)}, u32[]{:S(2)}) async-start(f32[32,5,512]{2,1,0:T(8,128)} %pad_maximum_fusion), calls=%async_computation | async-start | bytes 1048576 | tf_op jit(solution)/shard_map/all_to_all | solution.py:73
  48.9 2.8 %fusion.124 = f32[432,432]{1,0:T(8,128)} fusion(f32[432,1280]{1,0:T(8,128)} %copy-done.3), kind=kOutput, calls=%fused_computation.136 | convolution fusion | flops 286654464 | bytes 1188864 | tf_op jit(solution)/shard_map/dot_general | solution.py:21
  52.7 2.3 fusion.18
  55.0 2.8 %fusion.24 = f32[432,64]{1,0:T(8,128)} fusion(f32[432,432]{1,0:T(8,128)} %fusion.124, f32[432]{0:T(512)S(1)} %bitcast.171, f32[432]{0:T(512)S(1)} %bitcast.167, f32[432,1280]{1,0:T(8,128)} %copy-done.3), kind=kOutput, calls=%fused_computation.37 | convolution fusion | flops 144260352 | bytes 1222656 | tf_op jit(solution)/shard_map/dot_general | solution.py:21
  57.9 2.7 %fusion.30 = f32[432,64]{1,0:T(8,128)} fusion(f32[432,432]{1,0:T(8,128)S(1)} %copy-done.5, f32[432]{0:T(512)S(1)} %bitcast.170, f32[432]{0:T(512)S(1)} %bitcast.166, f32[432,1280]{1,0:T(8,128)} %copy-done.3), kind=kOutput, calls=%fused_computation.43 | convolution fusion | flops 144260352 | bytes 1222656 | tf_op jit(solution)/shard_map/dot_general | solution.py:21
  60.5 2.6 %fusion.36 = f32[432,64]{1,0:T(8,128)} fusion(f32[432,432]{1,0:T(8,128)S(1)} %copy-done.5, f32[432]{0:T(512)S(1)} %bitcast.169, f32[432]{0:T(512)S(1)} %bitcast.165, f32[432,1280]{1,0:T(8,128)} %copy-done.3), kind=kOutput, calls=%fused_computation.49 | convolution fusion | flops 144260352 | bytes 1222656 | tf_op jit(solution)/shard_map/dot_general | solution.py:21
  64.3 2.5 %copy.57 = f32[432,512]{1,0:T(8,128)} copy(f32[432,512]{0,1:T(8,128)} %bitcast.103) | data formatting | bytes 1769472 | tf_op jit(solution)/shard_map/reshape | solution.py:25
  68.5 2.9 %fusion.42 = f32[432,64]{1,0:T(8,128)} fusion(f32[432,432]{1,0:T(8,128)} %fusion.124, f32[432]{0:T(512)S(1)} %bitcast.164, f32[432]{0:T(512)S(1)} %bitcast.162, f32[432,1280]{1,0:T(8,128)} %copy-done.3), kind=kOutput, calls=%fused_computation.55 | convolution fusion | flops 144260352 | bytes 1222656 | tf_op jit(solution)/shard_map/dot_general | solution.py:21
  71.4 2.9 %fusion.48 = f32[432,64]{1,0:T(8,128)} fusion(f32[432,432]{1,0:T(8,128)} %fusion.124, f32[432]{0:T(512)S(1)} %bitcast.163, f32[432]{0:T(512)S(1)} %bitcast.161, f32[432,1280]{1,0:T(8,128)} %copy-done.3), kind=kOutput, calls=%fused_computation.61 | convolution fusion | flops 144260352 | bytes 1222656 | tf_op jit(solution)/shard_map/dot_general | solution.py:21
  81.1 1.3 constant_dynamic-update-slice_fusion.19
  83.8 1.3 constant_dynamic-update-slice_fusion.17
  86.4 1.3 constant_dynamic-update-slice_fusion.15
  89.1 1.3 constant_dynamic-update-slice_fusion.13
  91.7 1.3 constant_dynamic-update-slice_fusion.11
  94.4 1.3 constant_dynamic-update-slice_fusion.9
  97.0 1.3 constant_dynamic-update-slice_fusion.7
  99.7 1.3 constant_dynamic-update-slice_fusion.5
  102.3 1.3 constant_dynamic-update-slice_fusion.3
  105.0 1.3 constant_dynamic-update-slice_fusion.1
  107.7 10.2 %all-to-all-start.1 = ((f32[32,4,512]{2,1,0:T(4,128)}), f32[32,4,512]{2,1,0:T(4,128)S(1)}, u32[]{:S(2)}, u32[]{:S(2)}) async-start(f32[32,4,512]{2,1,0:T(4,128)} %constant_dynamic-update-slice_fusion), calls=%async_computation.1 | async-start | bytes 524288 | tf_op jit(solution)/shard_map/all_to_all | solution.py:79
  117.8 3.0 %fusion.54 = f32[432,64]{1,0:T(8,128)} fusion(f32[432,432]{1,0:T(8,128)} %fusion.124, f32[432]{0:T(512)S(1)} %bitcast.160, f32[432]{0:T(512)S(1)} %bitcast.158, f32[432,1280]{1,0:T(8,128)} %copy-done.3), kind=kOutput, calls=%fused_computation.67 | convolution fusion | flops 144260352 | bytes 1222656 | tf_op jit(solution)/shard_map/dot_general | solution.py:21
  120.8 2.9 %fusion.60 = f32[432,64]{1,0:T(8,128)} fusion(f32[432,432]{1,0:T(8,128)} %fusion.124, f32[432]{0:T(512)S(1)} %bitcast.159, f32[432]{0:T(512)S(1)} %bitcast.157, f32[432,1280]{1,0:T(8,128)} %copy-done.3), kind=kOutput, calls=%fused_computation.73 | convolution fusion | flops 144260352 | bytes 1222656 | tf_op jit(solution)/shard_map/dot_general | solution.py:21
  123.7 2.4 %concatenate.9 = f32[432,512]{1,0:T(8,128)} concatenate(f32[432,64]{1,0:T(8,128)} %fusion.60, f32[432,64]{1,0:T(8,128)} %fusion.54, f32[432,64]{1,0:T(8,128)} %fusion.48, f32[432,64]{1,0:T(8,128)} %fusion.42, f32[432,64]{1,0:T(8,128)} %fusion.36, f32[432,64]{1,0:T(8,128)} %fusion.30, f32[432,64]{1,0:T(8,128)S(1)} %copy-done.7, f32[432,64]{1,0:T(8,128)S(1)} %fusion.18), dimensions={1} | concatenate | bytes 1769472 | tf_op jit(solution)/shard_map/concatenate | solution.py:88
  126.0 3.5 %all-to-all-done.1 = f32[32,4,512]{2,1,0:T(4,128)S(1)} async-done(((f32[32,4,512]{2,1,0:T(4,128)}), f32[32,4,512]{2,1,0:T(4,128)S(1)}, u32[]{:S(2)}, u32[]{:S(2)}) %all-to-all-start.1) | async-done | bytes 262176 | tf_op jit(solution)/shard_map/all_to_all | solution.py:79
  129.7 3.4 %multiply_reduce_fusion = (f32[432]{0:T(512)S(1)}, f32[432,512]{1,0:T(8,128)S(1)}) fusion(f32[432,1280]{1,0:T(8,128)} %copy-done.3, f32[512]{0:T(512)S(1)} %mul.1066, f32[432,512]{1,0:T(8,128)} %concatenate.9, f32[432,512]{1,0:T(8,128)} %copy.57, f32[128,512]{1,0:T(8,128)S(1)} %reshape.3303), kind=kOutput, calls=%fused_computation.28 | convolution fusion | flops 341950016 | bytes 4910784 | tf_op jit(solution)/shard_map/dot_general | solution.py:21
  134.8 4.9 %all-to-all-start.2 = ((bf16[8,432,128]{2,1,0:T(8,128)(2,1)}), bf16[8,432,128]{2,1,0:T(8,128)(2,1)S(1)}, u32[]{:S(2)}, u32[]{:S(2)}) async-start(bf16[8,432,128]{2,1,0:T(8,128)(2,1)} %bitcast.100), calls=%async_computation.2 | async-start | bytes 1769472 | tf_op jit(solution)/shard_map/all_to_all | solution.py:95
  140.6 11.3 %all-to-all-done.2 = bf16[8,432,128]{2,1,0:T(8,128)(2,1)S(1)} async-done(((bf16[8,432,128]{2,1,0:T(8,128)(2,1)}), bf16[8,432,128]{2,1,0:T(8,128)(2,1)S(1)}, u32[]{:S(2)}, u32[]{:S(2)}) %all-to-all-start.2) | async-done | bytes 884768 | tf_op jit(solution)/shard_map/all_to_all | solution.py:95
  153.8 75.3 %all-gather = f32[32,1,256]{2,1,0:T(1,128)S(1)} all-gather(f32[1,1,256]{2,1,0:T(1,128)S(1)} %pad_bitcast_fusion.4), channel_id=1, replica_groups=mesh['half'=2,'act'=32,'head'=8] {'act'}, dimensions={0}, use_global_device_ids=true | all-gather | bytes 33792 | tf_op jit(solution)/shard_map/all_gather | solution.py:102
  (154 shorter events, 46.3 us)
Async XLA Ops:
  0.0 32.7 %copy-start = (bf16[1024,1280]{1,0:T(8,128)(2,1)S(1)}, bf16[1024,1280]{1,0:T(8,128)(2,1)}, u32[]{:S(2)}) copy-start(bf16[1024,1280]{1,0:T(8,128)(2,1)} %param.19) | copy-start | bytes 7864324
  0.0 22.9 %copy-start.16 = (f32[1024]{0:T(1024)S(1)}, f32[1024]{0:T(1024)}, u32[]{:S(2)}) copy-start(f32[1024]{0:T(1024)} %param.17) | copy-start | bytes 12292
  0.0 24.3 %copy-start.27 = (f32[8]{0:T(128)S(1)}, f32[8]{0:T(128)}, u32[]{:S(2)}) copy-start(f32[8]{0:T(128)} %param.24) | copy-start | bytes 100
  0.0 25.0 %copy-start.26 = (f32[1024]{0:T(1024)S(1)}, f32[1024]{0:T(1024)}, u32[]{:S(2)}) copy-start(f32[1024]{0:T(1024)} %param.18) | copy-start | bytes 12292
  0.0 25.0 %copy-start.25 = (bf16[1024,8]{0,1:T(8,128)(2,1)S(1)}, bf16[1024,8]{0,1:T(8,128)(2,1)}, u32[]{:S(2)}) copy-start(bf16[1024,8]{0,1:T(8,128)(2,1)} %param.20) | copy-start | bytes 49156
  0.0 25.0 %copy-start.21 = (f32[8]{0:T(128)S(1)}, f32[8]{0:T(128)}, u32[]{:S(2)}) copy-start(f32[8]{0:T(128)} %param.22) | copy-start | bytes 100
  0.0 25.0 %copy-start.20 = (f32[8]{0:T(128)S(1)}, f32[8]{0:T(128)}, u32[]{:S(2)}) copy-start(f32[8]{0:T(128)} %param.23) | copy-start | bytes 100
  2.1 3.3 %copy-start.14 = (s32[576]{0:T(1024)}, s32[576]{0:T(1024)S(1)}, u32[]{:S(2)}) copy-start(s32[576]{0:T(1024)S(1)} %get-tuple-element.90) | copy-start | bytes 6916
  4.0 1.3 copy-start.18
  5.3 0.6 copy-start.6
  24.3 1.8 copy-start.22
  25.1 1.0 copy-start.9
  27.7 0.6 copy-start.11
  32.7 3.6 %copy-start.1 = (f32[432,512]{1,0:T(8,128)S(1)}, f32[432,512]{1,0:T(8,128)}, u32[]{:S(2)}) copy-start(f32[432,512]{1,0:T(8,128)} %copy.56) | copy-start | bytes 2654212
  34.9 1.4 copy-start.3
  36.3 0.8 copy-start.12
  37.1 14.6 %copy-start.10 = (bf16[576]{0:T(1024)(128)(2,1)S(1)}, bf16[576]{0:T(1024)(128)(2,1)}, u32[]{:S(2)}) copy-start(bf16[576]{0:T(1024)(128)(2,1)} %param.16) | copy-start | bytes 3460
  37.1 14.6 %copy-start.15 = (s32[576]{0:T(1024)S(1)}, s32[576]{0:T(1024)}, u32[]{:S(2)}) copy-start(s32[576]{0:T(1024)} %copy-done.14) | copy-start | bytes 6916
  37.1 14.6 %copy-start.19 = (pred[576]{0:T(1024)(128)(4,1)S(1)}, pred[576]{0:T(1024)(128)(4,1)}, u32[]{:S(2)}) copy-start(pred[576]{0:T(1024)(128)(4,1)} %copy-done.18) | copy-start | bytes 1732
  38.3 36.0 %all-to-all-start = ((f32[32,5,512]{2,1,0:T(8,128)}), f32[32,5,512]{2,1,0:T(8,128)S(1)}, u32[]{:S(2)}, u32[]{:S(2)}) async-start(f32[32,5,512]{2,1,0:T(8,128)} %pad_maximum_fusion), calls=%async_computation | async-start | bytes 1048576 | tf_op jit(solution)/shard_map/all_to_all | solution.py:73
  52.5 5.3 %copy-start.5 = (f32[432,432]{1,0:T(8,128)S(1)}, f32[432,432]{1,0:T(8,128)}, u32[]{:S(2)}) copy-start(f32[432,432]{1,0:T(8,128)} %fusion.124) | copy-start | bytes 2239492
  57.9 5.3 %copy-start.8 = (f32[576]{0:T(1024)S(1)}, f32[576]{0:T(1024)}, u32[]{:S(2)}) copy-start(f32[576]{0:T(1024)} %get-tuple-element.5) | copy-start | bytes 6916
  63.1 3.6 %copy-start.23 = (f32[8]{0:T(128)S(1)}, f32[8]{0:T(128)}, u32[]{:S(2)}) copy-start(f32[8]{0:T(128)} %param.25) | copy-start | bytes 100
  74.3 6.8 %copy-start.2 = (f32[32,5,512]{2,1,0:T(8,128)}, f32[32,5,512]{2,1,0:T(8,128)S(1)}, u32[]{:S(2)}) copy-start(f32[32,5,512]{2,1,0:T(8,128)S(1)} %all-to-all-done) | copy-start | bytes 983044
  107.7 21.9 %all-to-all-start.1 = ((f32[32,4,512]{2,1,0:T(4,128)}), f32[32,4,512]{2,1,0:T(4,128)S(1)}, u32[]{:S(2)}, u32[]{:S(2)}) async-start(f32[32,4,512]{2,1,0:T(4,128)} %constant_dynamic-update-slice_fusion), calls=%async_computation.1 | async-start | bytes 524288 | tf_op jit(solution)/shard_map/all_to_all | solution.py:79
  117.8 5.8 %copy-start.7 = (f32[432,64]{1,0:T(8,128)S(1)}, f32[432,64]{1,0:T(8,128)}, u32[]{:S(2)}) copy-start(f32[432,64]{1,0:T(8,128)} %fusion.24) | copy-start | bytes 331780
  129.6 3.4 %copy-start.4 = (bf16[512,1024]{1,0:T(8,128)(2,1)S(1)}, bf16[512,1024]{1,0:T(8,128)(2,1)}, u32[]{:S(2)}) copy-start(bf16[512,1024]{1,0:T(8,128)(2,1)} %param.27) | copy-start | bytes 3145732
  129.7 3.4 %copy-start.17 = (f32[512]{0:T(512)S(1)}, f32[512]{0:T(512)}, u32[]{:S(2)}) copy-start(f32[512]{0:T(512)} %param.26) | copy-start | bytes 6148
  134.8 95.0 %copy-start.13 = (s32[576]{0:T(1024)S(1)}, s32[576]{0:T(1024)}, u32[]{:S(2)}) copy-start(s32[576]{0:T(1024)} %get-tuple-element.89) | copy-start | bytes 6916
  134.8 17.1 %all-to-all-start.2 = ((bf16[8,432,128]{2,1,0:T(8,128)(2,1)}), bf16[8,432,128]{2,1,0:T(8,128)(2,1)S(1)}, u32[]{:S(2)}, u32[]{:S(2)}) async-start(bf16[8,432,128]{2,1,0:T(8,128)(2,1)} %bitcast.100), calls=%async_computation.2 | async-start | bytes 1769472 | tf_op jit(solution)/shard_map/all_to_all | solution.py:95
  152.0 78.3 %copy-start.24 = (bf16[576,128]{1,0:T(8,128)(2,1)S(1)}, bf16[576,128]{1,0:T(8,128)(2,1)}, u32[]{:S(2)}) copy-start(bf16[576,128]{1,0:T(8,128)(2,1)} %param.14) | copy-start | bytes 442372

commit v2 on v1

v2 whole, which is shorter than its diff:
```python
import jax
import jax.numpy as jnp
from jax import lax
from jax.experimental import pallas as pl
from jax.experimental.pallas import tpu as pltpu
from jax.sharding import Mesh
from jax.sharding import PartitionSpec as P

D = 1024
E = 2048
N = 128
HEADS_HERE = 8
P_SIZE = 64
INNER = HEADS_HERE * P_SIZE
COLS = 2 * INNER + 2 * N
CAP = 432
BYTES = 576
WIDTH = 128
CHUNKS = ((0, 128), (128, 128), (256, 128), (384, 48))
X_CHIPS = 4
LOW = -1e30
eps = 1e-05
F32 = jnp.float32
BF16 = jnp.bfloat16


def dot(a, b, contract=((1,), (0,))):
    return lax.dot_general(a, b, (contract, ((), ())), preferred_element_type=F32)


def halves(a):
    hi = a.astype(BF16)
    return hi, (a - hi.astype(F32)).astype(BF16)


def thirds(a):
    hi = a.astype(BF16)
    rest = a - hi.astype(F32)
    mid = rest.astype(BF16)
    return hi, mid, (rest - mid.astype(F32)).astype(BF16)


def dot3(a, b, contract=((1,), (0,))):
    a_hi, a_lo = halves(a)
    b_hi, b_lo = halves(b)
    return dot(a_hi, b_hi, contract) + dot(a_hi, b_lo, contract) + dot(a_lo, b_hi, contract)


def iota(shape, dim):
    return lax.broadcasted_iota(jnp.int32, shape, dim)


def spread_heads(a):
    owner = (iota((2 * HEADS_HERE, INNER), 1) // P_SIZE) == (
        iota((2 * HEADS_HERE, INNER), 0) % HEADS_HERE
    )
    hi, lo = halves(a)
    return dot(jnp.concatenate([hi, lo], axis=1), owner.astype(BF16))


def select_kernel(flags_ref, enc_ref, packed_ref):
    flags = flags_ref[...]
    upper = (iota((BYTES, BYTES), 0) <= iota((BYTES, BYTES), 1)).astype(BF16)
    rank = dot(flags.astype(F32).astype(BF16), upper)
    place = jnp.where(flags > 0, rank.astype(jnp.int32) - 1, -1)
    hit = (iota((CAP, BYTES), 0) == place).astype(F32).astype(BF16)
    packed_ref[...] = dot(hit, enc_ref[...]).astype(BF16)


def weights_kernel(flags_ref, prob_ref, w_hi_ref, w_lo_ref, carry_ref, kept_ref, decay_ref):
    flags = flags_ref[...].astype(F32)
    prob = prob_ref[...].astype(F32)
    logs = jnp.where(flags > 0, jnp.log1p(-prob), 0.0)
    before = iota((BYTES, BYTES), 1) <= iota((BYTES, BYTES), 0)
    same = iota((BYTES, BYTES), 1) == iota((BYTES, BYTES), 0)

    def column(mask, row):
        return jnp.sum(jnp.where(mask, row, 0.0), axis=1, keepdims=True)

    rank = column(before, flags)
    kept = column(before, logs)
    flag = column(same, flags)
    chance = column(same, prob)
    place = iota((BYTES, CAP), 1).astype(F32)
    hit = (place == rank - 1.0) & (flag > 0)
    kept_k = jnp.sum(jnp.where(hit, kept, 0.0), axis=0, keepdims=True)
    prob_k = jnp.sum(jnp.where(hit, chance, 0.0), axis=0, keepdims=True)
    gap = jnp.where(place < rank, kept - kept_k, LOW)
    hi, lo = halves(jnp.exp(gap) * prob_k)
    w_hi_ref[...] = hi
    w_lo_ref[...] = lo
    total = jnp.sum(logs, axis=1, keepdims=True)
    count = jnp.sum(flags, axis=1, keepdims=True)
    real = iota((1, CAP), 1).astype(F32) < count
    carry_ref[...] = jnp.exp(jnp.where(real, total - kept_k, LOW)) * prob_k
    kept_ref[...] = jnp.broadcast_to(total, (1, WIDTH))
    decay_ref[...] = jnp.exp(kept)


def project_kernel(
    r0, r1, r2, r3, s0, s1, s2, s3,
    flags_ref, pad_ref, gain_ref, w_in_ref, w_dt_ref, pad_proj_ref, pad_dt_ref, bias_ref, a_log_ref,
    proj_ref, step_ref, run_ref, run_t_ref, pieces_ref, normed_ref,
):
    x = lax.axis_index("x")
    core = lax.axis_index("core")
    blocks = (r0, r1, r2, r3, s0, s1, s2, s3)
    energy = jnp.zeros((CAP, WIDTH), F32)
    for block in blocks:
        wide = block[...].astype(F32)
        energy = energy + wide * wide
    pad = pad_ref[...]
    power = jnp.sum(energy, axis=1, keepdims=True) + jnp.sum(pad * pad)
    inverse = lax.rsqrt(power / E + eps)
    for i, block in enumerate(blocks):
        shift, other = i % X_CHIPS, i // X_CHIPS
        chip = lax.rem(x + (X_CHIPS - shift), X_CHIPS)
        owner = chip * 2 + (core if other == 0 else 1 - core)
        gain = gain_ref[pl.ds(owner, 1), :]
        lanes = pl.ds(pl.multiple_of(owner * WIDTH, WIDTH), WIDTH)
        normed_ref[:, lanes] = (block[...].astype(F32) * inverse * gain).astype(BF16)

    def tile(t, carry):
        lanes = pl.ds(pl.multiple_of(t * 256, 256), 256)
        proj_ref[:, lanes] = dot(normed_ref[...], w_in_ref[:, lanes]) + inverse * pad_proj_ref[:, lanes]
        return carry

    lax.fori_loop(0, COLS // 256, tile, 0)
    raw = dot(normed_ref[...], w_dt_ref[...]) + inverse * pad_dt_ref[...] + bias_ref[...]
    soft = jnp.maximum(raw, 0.0) + jnp.log1p(jnp.exp(-jnp.abs(raw)))
    count = jnp.sum(flags_ref[...].astype(F32), axis=1, keepdims=True)
    real = iota((CAP, HEADS_HERE), 0).astype(F32) < count
    step = jnp.where(real, soft, 0.0)
    step_ref[...] = step
    logs = -jnp.exp(a_log_ref[...]) * step
    split = jnp.concatenate(thirds(logs), axis=1)
    lower = (iota((CAP, CAP), 1) <= iota((CAP, CAP), 0)).astype(BF16)
    upper = (iota((CAP, CAP), 0) <= iota((CAP, CAP), 1)).astype(BF16)
    sums = dot(lower, split)
    h = HEADS_HERE
    run = sums[:, :h] + sums[:, h : 2 * h] + sums[:, 2 * h :]
    sums_t = dot(split, upper, ((0,), (0,)))
    run_t_ref[...] = sums_t[:h] + sums_t[h : 2 * h] + sums_t[2 * h :]
    run_ref[...] = run
    total = run[CAP - 1 :, :]
    tail = jnp.exp(total - run) * step
    weighted = proj_ref[:, INNER : 2 * INNER] * spread_heads(tail)
    state = dot3(proj_ref[:, 2 * INNER : 2 * INNER + N], weighted, ((0,), (0,)))
    total_wide = spread_heads(jnp.broadcast_to(total, (8, h)))[0:1, :]
    spare = jnp.concatenate(
        [total_wide[:, i * WIDTH : (i + 1) * WIDTH] for i in range(INNER // WIDTH)], axis=0
    )
    act = pieces_ref.shape[0]
    per = N // act
    for d in range(act):
        pieces_ref[d, :, :INNER] = state[d * per : (d + 1) * per, :]
        if per >= 4:
            pieces_ref[d, 0:4, INNER:] = spare
            if per > 4:
                pieces_ref[d, 4:, INNER:] = jnp.zeros((per - 4, WIDTH), F32)


def local_kernel(proj_ref, step_ref, run_ref, run_t_ref, skip_ref, out_ref):
    state = jnp.zeros((N, INNER), F32)
    skip = spread_heads(jnp.broadcast_to(skip_ref[...], (8, HEADS_HERE)))[0:1, :]
    start_run = jnp.zeros((1, HEADS_HERE), F32)
    for start, length in CHUNKS:
        rows = slice(start, start + length)
        x = proj_ref[rows, INNER : 2 * INNER]
        b = proj_ref[rows, 2 * INNER : 2 * INNER + N]
        c = proj_ref[rows, 2 * INNER + N :]
        run = run_ref[rows, :]
        step = step_ref[rows, :]
        end_run = run[length - 1 :, :]
        scaled = (x * spread_heads(step)).astype(BF16)
        inter = dot3(c, b, ((1,), (1,)))
        lower = iota((length, length), 0) >= iota((length, length), 1)
        outs = []
        for k in range(HEADS_HERE):
            gap = run[:, k : k + 1] - run_t_ref[k : k + 1, rows]
            w = inter * jnp.exp(jnp.where(lower, gap, LOW))
            outs.append(dot(w.astype(BF16), scaled[:, k * P_SIZE : (k + 1) * P_SIZE]))
        y = jnp.concatenate(outs, axis=1) + skip * x
        if start > 0:
            y = y + spread_heads(jnp.exp(run - start_run)) * dot3(c, state)
        out_ref[rows, :] = y
        if start + length < CAP:
            weighted = x * spread_heads(step * jnp.exp(end_run - run))
            kept = spread_heads(jnp.broadcast_to(jnp.exp(end_run - start_run), (8, HEADS_HERE)))
            state = state * kept[0:1, :] + dot3(b, weighted, ((0,), (0,)))
        start_run = end_run


def scan_kernel(got_ref, before_ref):
    act, per, _ = got_ref.shape
    state = jnp.zeros((per, INNER), F32)
    for j in range(act):
        before_ref[j] = state
        keep = jnp.exp(got_ref[j, 0:4, INNER:])
        keep = jnp.concatenate([keep[i : i + 1, :] for i in range(INNER // WIDTH)], axis=1)
        state = state * keep + got_ref[j, :, :INNER]


def output_kernel(proj_ref, run_ref, local_ref, state_ref, gain_ref, w_out_ref, kept_ref, sent_ref, full_ref):
    core = lax.axis_index("core")
    act, per, _ = state_ref.shape
    for d in range(act):
        full_ref[d * per : (d + 1) * per, :] = state_ref[d]
    c = proj_ref[:, 2 * INNER + N :]
    ssm = local_ref[...] + spread_heads(jnp.exp(run_ref[...])) * dot3(c, full_ref[...])
    gate = proj_ref[:, :INNER]
    gated = ssm * gate / (1.0 + jnp.exp(-gate))
    power = jnp.mean(gated * gated, axis=1, keepdims=True)
    mixed = (gated * lax.rsqrt(power + eps) * gain_ref[...]).astype(BF16)
    for i in range(X_CHIPS):
        pair = dot(mixed, w_out_ref[:, i * 2 * WIDTH : (i + 1) * 2 * WIDTH])
        first, second = pair[:, :WIDTH], pair[:, WIDTH:]
        kept_ref[i] = jnp.where(core == 0, first, second)
        sent_ref[i] = jnp.where(core == 0, second, first).astype(BF16)


def main_kernel(packed_ref, parts_ref, carry_ref, kept_ref, main_ref, sent_ref):
    summed = packed_ref[...].astype(F32)
    added = parts_ref[0].astype(F32)
    for i in range(1, X_CHIPS):
        added = added + parts_ref[i].astype(F32)
    main = (summed + added).astype(BF16)
    main_ref[...] = main
    split = jnp.concatenate([jnp.broadcast_to(p, (8, CAP)) for p in thirds(carry_ref[...])], axis=0)
    sums = dot(split, main)
    carry = sums[0:1] + sums[8:9] + sums[16:17]
    row = jnp.concatenate([carry, kept_ref[...]], axis=0)
    sent_ref[...] = jnp.broadcast_to(row[None], sent_ref.shape)


def decode_kernel(enc_ref, w_hi_ref, w_lo_ref, main_ref, decay_ref, carries_ref, out_ref):
    me = lax.axis_index("act")
    act = carries_ref.shape[0]
    carry = jnp.zeros((1, WIDTH), F32)
    for j in range(act):
        after = carry * jnp.exp(carries_ref[j, 1:2, :]) + carries_ref[j, 0:1, :]
        carry = jnp.where(j < me, after, carry)
    main = main_ref[...]
    smoothed = dot(w_hi_ref[...], main) + dot(w_lo_ref[...], main) + decay_ref[...] * carry
    out_ref[...] = (enc_ref[...].astype(F32) + smoothed).astype(BF16)


def shape(dims, dtype=F32):
    return jax.ShapeDtypeStruct(dims, dtype)


def call(kernel, outs, name, scratch=(), flops=0, transcendentals=0, nbytes=0):
    return pl.pallas_call(
        kernel,
        out_shape=outs,
        name=name,
        scratch_shapes=scratch,
        compiler_params=pltpu.CompilerParams(vmem_limit_bytes=40 * 2**20),
        cost_estimate=pl.CostEstimate(
            flops=flops, transcendentals=transcendentals, bytes_accessed=nbytes
        ),
    )


def body(
    enc_rows,
    boundary_flags,
    boundary_prob,
    pad_vector,
    norm_gain,
    w_in,
    w_dt,
    pad_proj,
    pad_dt,
    dt_bias,
    a_log,
    d_skip,
    gate_gain,
    w_out,
):
    act = lax.axis_size("act")
    row = lambda a: a.reshape(1, -1)
    flags, prob = row(boundary_flags), row(boundary_prob)
    packed = call(select_kernel, shape((CAP, WIDTH), BF16), "select", flops=10**8)(flags, enc_rows)

    around = [packed] + [
        lax.ppermute(packed, "x", [(i, (i + s) % X_CHIPS) for i in range(X_CHIPS)])
        for s in range(1, X_CHIPS)
    ]
    across = [lax.ppermute(a, "core", [(0, 1), (1, 0)]) for a in around]

    w_hi, w_lo, carry_w, kept, decay = call(
        weights_kernel,
        (
            shape((BYTES, CAP), BF16),
            shape((BYTES, CAP), BF16),
            shape((1, CAP)),
            shape((1, WIDTH)),
            shape((BYTES, 1)),
        ),
        "weights",
        transcendentals=BYTES * CAP,
        flops=BYTES * CAP * 30,
        nbytes=10**6,
    )(flags, prob)

    proj, step, run, run_t, pieces = call(
        project_kernel,
        (
            shape((CAP, COLS)),
            shape((CAP, HEADS_HERE)),
            shape((CAP, HEADS_HERE)),
            shape((HEADS_HERE, CAP)),
            shape((act, N // act, INNER + WIDTH)),
        ),
        "project",
        scratch=[pltpu.VMEM((CAP, D), BF16)],
        flops=2 * CAP * D * COLS,
        nbytes=8 * 10**6,
    )(
        *around, *across, flags, pad_vector.reshape(-1, WIDTH), norm_gain.reshape(-1, WIDTH), w_in, w_dt,
        row(pad_proj), row(pad_dt), row(dt_bias), row(a_log),
    )

    got = lax.all_to_all(pieces, "act", 0, 0)
    local = call(
        local_kernel, shape((CAP, INNER)), "local", flops=10**9, transcendentals=CAP * 1024, nbytes=3 * 10**6
    )(proj, step, run, run_t, row(d_skip))
    before = call(scan_kernel, shape((act, N // act, INNER)), "scan", nbytes=6 * 10**5)(got)
    state_in = lax.all_to_all(before, "act", 0, 0)

    own, sent = call(
        output_kernel,
        (shape((X_CHIPS, CAP, WIDTH)), shape((X_CHIPS, CAP, WIDTH), BF16)),
        "output",
        scratch=[pltpu.VMEM((N, INNER), F32)],
        flops=2 * CAP * INNER * D,
        nbytes=6 * 10**6,
    )(proj, run, local, state_in, row(gate_gain), w_out)

    pair = (own + lax.ppermute(sent, "core", [(0, 1), (1, 0)]).astype(F32)).astype(BF16)
    parts = lax.all_to_all(pair, "x", 0, 0)
    main, carry = call(
        main_kernel, (shape((CAP, WIDTH), BF16), shape((act, 2, WIDTH))), "main", nbytes=6 * 10**5
    )(packed, parts, carry_w, kept)
    carries = lax.all_to_all(carry, "act", 0, 0)
    return call(
        decode_kernel, shape((BYTES, WIDTH), BF16), "decode", flops=2 * 10**8, nbytes=2 * 10**6
    )(enc_rows, w_hi, w_lo, main, decay, carries)


def solution(mesh):
    seq = mesh.shape["seq"]
    split = Mesh(
        mesh.devices.reshape(2, seq // 2, X_CHIPS, 2), ("half", "act", "x", "core")
    )
    by_seq, by_head = ("half", "act"), ("x", "core")
    in_specs = (
        P(by_seq, by_head),
        P(by_seq),
        P(by_seq),
        P(),
        P(),
        P(None, by_head),
        P(None, by_head),
        P(by_head),
        P(by_head),
        P(by_head),
        P(by_head),
        P(by_head),
        P(by_head),
        P(by_head, None),
    )
    return jax.shard_map(
        body, mesh=split, in_specs=in_specs, out_specs=P(by_seq, by_head), check_vma=False
    )
```

time: 235 us -> 115 us (0.49)
  blocking collectives: 91.9 us -> 38.2 us
  other arithmetic: 43.7 us -> 0.86 us
  matrix products: 36.2 us -> 0 us
  Pallas kernels: 0 us -> 12.6 us
  starting transfers between devices: 25.7 us -> 34.2 us
  local copies, waits for them, and re-layouts: 18.7 us -> 13.2 us
    all_gather x2 -> x0, blocking collectives: 91.9 us -> none  [the longest x1 75.3 us: body(): carries = lax.all_gather(sent, 'act', axis=0, tiled=True)]
    all_to_all x0 -> x2, blocking collectives: none -> 38.2 us  [the longest x1 23.6 us: body(): got = lax.all_to_all(pieces, 'act', 0, 0)]
    dot_general x19 -> x0, matrix products: 36.2 us -> none  [dot(): return jnp.dot(a, b, preferred_element_type=F32, precision=precision)]
    unnamed x30 -> x0, other arithmetic: 31.9 us -> none
    ppermute x0 -> x8, starting transfers between devices: none -> 23.2 us  [the longest x3 12.4 us: body(): lax.ppermute(packed, 'x', [(i, (i + s) % X_CHIPS) for i in range(X_CHIPS)])]
    all_to_all x3 -> x2, starting transfers between devices: 25.7 us -> 11.1 us  [the longest x1 6.66 us: body(): parts = lax.all_to_all(pair, 'x', 0, 0)]
    pallas_call x0 -> x8, Pallas kernels: none -> 12.6 us  [the longest x1 4.59 us: body(): call(project_kernel, (shape((CAP, COLS)), shape((CAP, HEADS_HERE)), shape...]
    unnamed x60 -> x43, local copies, waits for them, and re-layouts: 4.02 us -> 11.8 us
  transfers between devices with their start and end apart: 3 -> 10, of which waited for: 2 -> 3; matrix products, arithmetic and copies ran while one was open for 15% -> 1% of each run, Pallas kernels for 0% -> 3%
where the time goes in v2:
time: 115 us; the launch traced here: 114 us
  blocking collectives  38.2 us (33%)
  starting transfers between devices  34.2 us (30%)
  waiting for transfers between devices  14.2 us (12%)
  local copies, waits for them, and re-layouts  13.2 us (11%)
  Pallas kernels  12.6 us (11%)
    all_to_all x1, blocking collectives, body(): got = lax.all_to_all(pieces, 'act', 0, 0)  23.6 us
    all_to_all x1, blocking collectives, body(): carries = lax.all_to_all(carry, 'act', 0, 0)  14.6 us
    ppermute x3, starting transfers between devices, body(): lax.ppermute(packed, 'x', [(i, (i + s) % X_CHIPS) for i in range(X_CHIPS)])  12.4 us
    unnamed x43, local copies, waits for them, and re-layouts  11.8 us
    ppermute x4, starting transfers between devices, body(): across = [lax.ppermute(a, 'core', [(0, 1), (1, 0)]) for a in around]  8.65 us
    all_to_all x1, starting transfers between devices, body(): parts = lax.all_to_all(pair, 'x', 0, 0)  6.66 us
    all_to_all x1, waiting for transfers between devices, body(): state_in = lax.all_to_all(before, 'act', 0, 0)  6.58 us
    all_to_all x1, waiting for transfers between devices, body(): parts = lax.all_to_all(pair, 'x', 0, 0)  5.87 us
  transfers between devices with their start and end apart: 10, of which 3 were waited for; matrix products, arithmetic and copies ran while one was open for 1% of the time, Pallas kernels for 3%

profile of v2, /device:TPU:6, one launch (start us, length us, event | category | flops | bytes accessed | tf_op | source)
XLA Modules:
  0.0 113.6 jit_solution(9059396649259595957)
XLA Ops:
  0.0 0.7 reshape.30.flags_ref
  0.7 0.9 copy-done.6
  2.1 7.8 %collective-permute-start = (bf16[432,128]{1,0:T(8,128)(2,1)S(1)}, bf16[432,128]{1,0:T(8,128)(2,1)S(1)}, u32[]{:S(2)}, u32[]{:S(2)}) collective-permute-start(bf16[432,128]{1,0:T(8,128)(2,1)S(1)} %select.1.r0.packed_ref), channel_id=1, source_target_pairs={{0,2},{2,4},{4,6},{6,0},{1,3},{3,5},{5,7},{7,1},{8,10},{10,12},{12... | collective-permute-start | bytes 331784 | tf_op jit(solution)/shard_map/ppermute | solution.py:287
  9.9 1.9 %collective-permute-start.1 = (bf16[432,128]{1,0:T(8,128)(2,1)S(1)}, bf16[432,128]{1,0:T(8,128)(2,1)S(1)}, u32[]{:S(2)}, u32[]{:S(2)}) collective-permute-start(bf16[432,128]{1,0:T(8,128)(2,1)S(1)} %select.1.r0.packed_ref), channel_id=1, source_target_pairs={{0,4},{2,6},{4,0},{6,2},{1,5},{3,7},{5,1},{7,3},{8,12},{10,14},{12... | collective-permute-start | bytes 331784 | tf_op jit(solution)/shard_map/ppermute | solution.py:287
  11.8 2.8 %collective-permute-start.2 = (bf16[432,128]{1,0:T(8,128)(2,1)S(1)}, bf16[432,128]{1,0:T(8,128)(2,1)S(1)}, u32[]{:S(2)}, u32[]{:S(2)}) collective-permute-start(bf16[432,128]{1,0:T(8,128)(2,1)S(1)} %select.1.r0.packed_ref), channel_id=1, source_target_pairs={{0,6},{2,0},{4,2},{6,4},{1,7},{3,1},{5,3},{7,5},{8,14},{10,8},{12,... | collective-permute-start | bytes 331784 | tf_op jit(solution)/shard_map/ppermute | solution.py:287
  14.6 1.9 %collective-permute-start.3 = (bf16[432,128]{1,0:T(8,128)(2,1)S(1)}, bf16[432,128]{1,0:T(8,128)(2,1)S(1)}, u32[]{:S(2)}, u32[]{:S(2)}) collective-permute-start(bf16[432,128]{1,0:T(8,128)(2,1)S(1)} %select.1.r0.packed_ref), channel_id=1, source_target_pairs={{0,1},{1,0},{2,3},{3,2},{4,5},{5,4},{6,7},{7,6},{8,9},{9,8},{10,11... | collective-permute-start | bytes 331784 | tf_op jit(solution)/shard_map/ppermute | solution.py:290
  16.5 2.4 %collective-permute-start.4 = (bf16[432,128]{1,0:T(8,128)(2,1)S(1)}, bf16[432,128]{1,0:T(8,128)(2,1)S(1)}, u32[]{:S(2)}, u32[]{:S(2)}) collective-permute-start(bf16[432,128]{1,0:T(8,128)(2,1)S(1)} %collective-permute-done.r1), channel_id=1, source_target_pairs={{0,1},{1,0},{2,3},{3,2},{4,5},{5,4},{6,7},{7,6},{8,9},{9,8},{10,11... | collective-permute-start | bytes 331784 | tf_op jit(solution)/shard_map/ppermute | solution.py:290
  19.0 1.9 %collective-permute-start.5 = (bf16[432,128]{1,0:T(8,128)(2,1)S(1)}, bf16[432,128]{1,0:T(8,128)(2,1)S(1)}, u32[]{:S(2)}, u32[]{:S(2)}) collective-permute-start(bf16[432,128]{1,0:T(8,128)(2,1)S(1)} %collective-permute-done.1.r2), channel_id=1, source_target_pairs={{0,1},{1,0},{2,3},{3,2},{4,5},{5,4},{6,7},{7,6},{8,9},{9,8},{10,11... | collective-permute-start | bytes 331784 | tf_op jit(solution)/shard_map/ppermute | solution.py:290
  20.9 2.4 %collective-permute-start.6 = (bf16[432,128]{1,0:T(8,128)(2,1)S(1)}, bf16[432,128]{1,0:T(8,128)(2,1)S(1)}, u32[]{:S(2)}, u32[]{:S(2)}) collective-permute-start(bf16[432,128]{1,0:T(8,128)(2,1)S(1)} %collective-permute-done.2.r3), channel_id=1, source_target_pairs={{0,1},{1,0},{2,3},{3,2},{4,5},{5,4},{6,7},{7,6},{8,9},{9,8},{10,11... | collective-permute-start | bytes 331784 | tf_op jit(solution)/shard_map/ppermute | solution.py:290
  23.3 0.9 copy.15.w_dt_ref
  24.2 0.7 reshape.34.pad_proj_ref
  25.0 1.7 %copy-done.11 = bf16[1024,1280]{1,0:T(8,128)(2,1)S(1)} copy-done((bf16[1024,1280]{1,0:T(8,128)(2,1)S(1)}, bf16[1024,1280]{1,0:T(8,128)(2,1)}, u32[]{:S(2)}) %copy-start.11) | copy-done | bytes 2621464
  30.0 4.6 %project.1 = (f32[432,1280]{1,0:T(8,128)S(1)}, f32[432,8]{1,0:T(8,128)S(1)}, f32[432,8]{1,0:T(8,128)S(1)}, f32[8,432]{1,0:T(8,128)S(1)}, f32[32,4,640]{2,1,0:T(4,128)S(1)}) custom-call(bf16[432,128]{1,0:T(8,128)(2,1)S(1)} %select.1.r0.packed_ref, bf16[432,128]{1,0:T(8,128)(2,1)S(1)} %collective-permute-done.r1, ...), custom_call_target="tpu_custom_call" | custom-call | flops 1132462080 | bytes 8000000 | tf_op jit(solution)/shard_map/project/pallas_call | solution.py:307
  34.7 23.6 %all_to_all.20.got_ref = f32[32,4,640]{2,1,0:T(4,128)S(1)} all-to-all(f32[32,4,640]{2,1,0:T(4,128)S(1)} %get-tuple-element.25), channel_id=1, replica_groups=mesh['half'=2,'act'=32,'x'=4,'core'=2] {'act'}, dimensions={0} | all-to-all | bytes 655360 | tf_op jit(solution)/shard_map/all_to_all | solution.py:325
  58.3 0.8 scan.1
  59.1 4.4 %all-to-all-start.1 = ((f32[32,4,512]{2,1,0:T(4,128)}), f32[32,4,512]{2,1,0:T(4,128)S(1)}, u32[]{:S(2)}, u32[]{:S(2)}) async-start(f32[32,4,512]{2,1,0:T(4,128)} %scan.1), calls=%async_computation.1 | async-start | bytes 524288 | tf_op jit(solution)/shard_map/all_to_all | solution.py:330
  63.5 0.9 copy-done.4
  64.5 0.9 copy-done.19
  65.4 2.7 %local.1.local_ref = f32[432,512]{1,0:T(8,128)S(1)} custom-call(f32[432,1280]{1,0:T(8,128)S(1)} %get-tuple-element.21.proj_ref, f32[432,8]{1,0:T(8,128)S(1)} %copy-done.19, f32[432,8]{1,0:T(8,128)S(1)} %copy-done.4, f32[8,432]{1,0:T(8,128)S(1)} %get-tuple-element.24.run_t_ref, f32[1,8]{1,0:T(1,128)S(1)} %bitcast.13), custom_call_target="tpu_custom_call" | custom-call | flops 1000000000 | bytes 3000000 | tf_op jit(solution)/shard_map/local/pallas_call | solution.py:326
  68.1 0.9 copy-done.1
  69.0 6.6 %all-to-all-done.1.state_ref = f32[32,4,512]{2,1,0:T(4,128)S(1)} async-done(((f32[32,4,512]{2,1,0:T(4,128)}), f32[32,4,512]{2,1,0:T(4,128)S(1)}, u32[]{:S(2)}, u32[]{:S(2)}) %all-to-all-start.1) | async-done | bytes 262176 | tf_op jit(solution)/shard_map/all_to_all | solution.py:330
  75.6 1.2 %copy-done.2 = f32[432,512]{1,0:T(8,128)S(1)} copy-done((f32[432,512]{1,0:T(8,128)S(1)}, f32[432,512]{1,0:T(8,128)}, u32[]{:S(2)}) %copy-start.2) | copy-done | bytes 884760
  76.8 0.9 copy-done.5
  77.7 1.5 %output.1 = (f32[4,432,128]{2,1,0:T(8,128)S(1)}, bf16[4,432,128]{2,1,0:T(8,128)(2,1)S(1)}) custom-call(f32[432,1280]{1,0:T(8,128)S(1)} %get-tuple-element.21.proj_ref, f32[432,8]{1,0:T(8,128)S(1)} %copy-done.5, f32[432,512]{1,0:T(8,128)S(1)} %copy-done.2, f32[32,4,512]{2,1,0:T(4,128)S(1)} %all-to-all-done.1.state_ref, f32[1,512]{1,0:T(1,128)S(1)} %bitcast.7, ...), custom_call_target="tpu_custom_call" | custom-call | flops 452984832 | bytes 6000000 | tf_op jit(solution)/shard_map/output/pallas_call | solution.py:332
  79.2 2.1 %collective-permute-start.7 = (bf16[4,432,128]{2,1,0:T(8,128)(2,1)S(1)}, bf16[4,432,128]{2,1,0:T(8,128)(2,1)S(1)}, u32[]{:S(2)}, u32[]{:S(2)}) collective-permute-start(bf16[4,432,128]{2,1,0:T(8,128)(2,1)S(1)} %get-tuple-element.27), channel_id=1, source_target_pairs={{0,1},{1,0},{2,3},{3,2},{4,5},{5,4},{6,7},{7,6},{8,9},{9,8},{10,11... | collective-permute-start | bytes 1327112 | tf_op jit(solution)/shard_map/ppermute | solution.py:341
  81.2 1.8 %collective-permute-done.7 = bf16[4,432,128]{2,1,0:T(8,128)(2,1)S(1)} collective-permute-done((bf16[4,432,128]{2,1,0:T(8,128)(2,1)S(1)}, bf16[4,432,128]{2,1,0:T(8,128)(2,1)S(1)}, u32[]{:S(2)}, u32[]{:S(2)}) %collective-permute-start.7) | collective-permute-done | bytes 442400 | tf_op jit(solution)/shard_map/ppermute | solution.py:341
  83.0 0.9 add_convert_fusion
  83.9 6.7 %all-to-all-start.2 = ((bf16[4,432,128]{2,1,0:T(8,128)(2,1)}), bf16[4,432,128]{2,1,0:T(8,128)(2,1)S(1)}, u32[]{:S(2)}, u32[]{:S(2)}) async-start(bf16[4,432,128]{2,1,0:T(8,128)(2,1)} %add_convert_fusion), calls=%async_computation.2 | async-start | bytes 884736 | tf_op jit(solution)/shard_map/all_to_all | solution.py:342
  90.5 1.2 %weights.1 = (bf16[576,432]{1,0:T(8,128)(2,1)S(1)}, bf16[576,432]{1,0:T(8,128)(2,1)S(1)}, f32[1,432]{1,0:T(1,128)S(1)}, f32[1,128]{1,0:T(1,128)S(1)}, f32[576,1]{1,0:T(8,128)S(1)}) custom-call(s32[1,576]{1,0:T(1,128)S(1)} %reshape.30.flags_ref, bf16[1,576]{1,0:T(2,128)(2,1)S(1)} %reshape.31.prob_ref), custom_call_target="tpu_custom_call" | custom-call | flops 7464960 | bytes 1000000 | tf_op jit(solution)/shard_map/weights/pallas_call | solution.py:292
  91.8 5.9 %all-to-all-done.2.parts_ref = bf16[4,432,128]{2,1,0:T(8,128)(2,1)S(1)} async-done(((bf16[4,432,128]{2,1,0:T(8,128)(2,1)}), bf16[4,432,128]{2,1,0:T(8,128)(2,1)S(1)}, u32[]{:S(2)}, u32[]{:S(2)}) %all-to-all-start.2) | async-done | bytes 442400 | tf_op jit(solution)/shard_map/all_to_all | solution.py:342
  97.8 14.6 %all_to_all.21.carries_ref = f32[32,2,128]{2,1,0:T(2,128)S(1)} all-to-all(f32[32,2,128]{2,1,0:T(2,128)S(1)} %get-tuple-element.32), channel_id=1, replica_groups=mesh['half'=2,'act'=32,'x'=4,'core'=2] {'act'}, dimensions={0} | all-to-all | bytes 65536 | tf_op jit(solution)/shard_map/all_to_all | solution.py:346
  112.4 1.1 decode.1
  (45 shorter events, 4.1 us)
Async XLA Ops:
  0.7 0.9 copy-start.6
  2.1 32.5 %copy-start.8 = (bf16[432,128]{1,0:T(8,128)(2,1)}, bf16[432,128]{1,0:T(8,128)(2,1)S(1)}, u32[]{:S(2)}) copy-start(bf16[432,128]{1,0:T(8,128)(2,1)S(1)} %select.1.r0.packed_ref) | copy-start | bytes 331780
  2.1 14.4 %collective-permute-start = (bf16[432,128]{1,0:T(8,128)(2,1)S(1)}, bf16[432,128]{1,0:T(8,128)(2,1)S(1)}, u32[]{:S(2)}, u32[]{:S(2)}) collective-permute-start(bf16[432,128]{1,0:T(8,128)(2,1)S(1)} %select.1.r0.packed_ref), channel_id=1, source_target_pairs={{0,2},{2,4},{4,6},{6,0},{1,3},{3,5},{5,7},{7,1},{8,10},{10,12},{12... | collective-permute-start | bytes 331784 | tf_op jit(solution)/shard_map/ppermute | solution.py:287
  9.9 9.1 %collective-permute-start.1 = (bf16[432,128]{1,0:T(8,128)(2,1)S(1)}, bf16[432,128]{1,0:T(8,128)(2,1)S(1)}, u32[]{:S(2)}, u32[]{:S(2)}) collective-permute-start(bf16[432,128]{1,0:T(8,128)(2,1)S(1)} %select.1.r0.packed_ref), channel_id=1, source_target_pairs={{0,4},{2,6},{4,0},{6,2},{1,5},{3,7},{5,1},{7,3},{8,12},{10,14},{12... | collective-permute-start | bytes 331784 | tf_op jit(solution)/shard_map/ppermute | solution.py:287
  11.8 9.1 %collective-permute-start.2 = (bf16[432,128]{1,0:T(8,128)(2,1)S(1)}, bf16[432,128]{1,0:T(8,128)(2,1)S(1)}, u32[]{:S(2)}, u32[]{:S(2)}) collective-permute-start(bf16[432,128]{1,0:T(8,128)(2,1)S(1)} %select.1.r0.packed_ref), channel_id=1, source_target_pairs={{0,6},{2,0},{4,2},{6,4},{1,7},{3,1},{5,3},{7,5},{8,14},{10,8},{12,... | collective-permute-start | bytes 331784 | tf_op jit(solution)/shard_map/ppermute | solution.py:287
  14.6 10.3 %collective-permute-start.3 = (bf16[432,128]{1,0:T(8,128)(2,1)S(1)}, bf16[432,128]{1,0:T(8,128)(2,1)S(1)}, u32[]{:S(2)}, u32[]{:S(2)}) collective-permute-start(bf16[432,128]{1,0:T(8,128)(2,1)S(1)} %select.1.r0.packed_ref), channel_id=1, source_target_pairs={{0,1},{1,0},{2,3},{3,2},{4,5},{5,4},{6,7},{7,6},{8,9},{9,8},{10,11... | collective-permute-start | bytes 331784 | tf_op jit(solution)/shard_map/ppermute | solution.py:290
  16.5 8.4 %collective-permute-start.4 = (bf16[432,128]{1,0:T(8,128)(2,1)S(1)}, bf16[432,128]{1,0:T(8,128)(2,1)S(1)}, u32[]{:S(2)}, u32[]{:S(2)}) collective-permute-start(bf16[432,128]{1,0:T(8,128)(2,1)S(1)} %collective-permute-done.r1), channel_id=1, source_target_pairs={{0,1},{1,0},{2,3},{3,2},{4,5},{5,4},{6,7},{7,6},{8,9},{9,8},{10,11... | collective-permute-start | bytes 331784 | tf_op jit(solution)/shard_map/ppermute | solution.py:290
  19.0 6.0 %collective-permute-start.5 = (bf16[432,128]{1,0:T(8,128)(2,1)S(1)}, bf16[432,128]{1,0:T(8,128)(2,1)S(1)}, u32[]{:S(2)}, u32[]{:S(2)}) collective-permute-start(bf16[432,128]{1,0:T(8,128)(2,1)S(1)} %collective-permute-done.1.r2), channel_id=1, source_target_pairs={{0,1},{1,0},{2,3},{3,2},{4,5},{5,4},{6,7},{7,6},{8,9},{9,8},{10,11... | collective-permute-start | bytes 331784 | tf_op jit(solution)/shard_map/ppermute | solution.py:290
  20.9 4.0 %collective-permute-start.6 = (bf16[432,128]{1,0:T(8,128)(2,1)S(1)}, bf16[432,128]{1,0:T(8,128)(2,1)S(1)}, u32[]{:S(2)}, u32[]{:S(2)}) collective-permute-start(bf16[432,128]{1,0:T(8,128)(2,1)S(1)} %collective-permute-done.2.r3), channel_id=1, source_target_pairs={{0,1},{1,0},{2,3},{3,2},{4,5},{5,4},{6,7},{7,6},{8,9},{9,8},{10,11... | collective-permute-start | bytes 331784 | tf_op jit(solution)/shard_map/ppermute | solution.py:290
  24.9 1.7 %copy-start.11 = (bf16[1024,1280]{1,0:T(8,128)(2,1)S(1)}, bf16[1024,1280]{1,0:T(8,128)(2,1)}, u32[]{:S(2)}) copy-start(bf16[1024,1280]{1,0:T(8,128)(2,1)} %w_in_ref.1) | copy-start | bytes 7864324
  26.7 0.7 copy-start.12
  27.4 0.7 copy-start.13
  28.1 0.7 copy-start.14
  28.7 0.7 copy-start.15
  29.4 0.7 copy-start.16
  30.0 33.5 %copy-start.17 = (f32[8]{0:T(128)S(1)}, f32[8]{0:T(128)}, u32[]{:S(2)}) copy-start(f32[8]{0:T(128)} %param.25) | copy-start | bytes 100
  34.6 23.6 %copy-start.3 = (f32[432,8]{1,0:T(8,128)}, f32[432,8]{1,0:T(8,128)S(1)}, u32[]{:S(2)}) copy-start(f32[432,8]{1,0:T(8,128)S(1)} %get-tuple-element.22.run_ref) | copy-start | bytes 41476
  34.7 23.6 %copy-start.18 = (f32[432,8]{1,0:T(8,128)}, f32[432,8]{1,0:T(8,128)S(1)}, u32[]{:S(2)}) copy-start(f32[432,8]{1,0:T(8,128)S(1)} %get-tuple-element.23.step_ref) | copy-start | bytes 41476
  34.7 40.9 %copy-start = (bf16[512,1024]{1,0:T(8,128)(2,1)S(1)}, bf16[512,1024]{1,0:T(8,128)(2,1)}, u32[]{:S(2)}) copy-start(bf16[512,1024]{1,0:T(8,128)(2,1)} %w_out_ref.1) | copy-start | bytes 3145732
  34.7 40.9 %copy-start.10 = (f32[512]{0:T(512)S(1)}, f32[512]{0:T(512)}, u32[]{:S(2)}) copy-start(f32[512]{0:T(512)} %param.26) | copy-start | bytes 6148
  59.1 16.5 %all-to-all-start.1 = ((f32[32,4,512]{2,1,0:T(4,128)}), f32[32,4,512]{2,1,0:T(4,128)S(1)}, u32[]{:S(2)}, u32[]{:S(2)}) async-start(f32[32,4,512]{2,1,0:T(4,128)} %scan.1), calls=%async_computation.1 | async-start | bytes 524288 | tf_op jit(solution)/shard_map/all_to_all | solution.py:330
  63.5 0.9 copy-start.4
  64.5 0.9 copy-start.19
  68.1 0.9 copy-start.1
  75.6 1.2 %copy-start.2 = (f32[432,512]{1,0:T(8,128)S(1)}, f32[432,512]{1,0:T(8,128)}, u32[]{:S(2)}) copy-start(f32[432,512]{1,0:T(8,128)} %copy-done.1) | copy-start | bytes 2654212
  76.8 0.9 copy-start.5
  77.7 12.8 %copy-start.20 = (bf16[576]{0:T(1024)(128)(2,1)S(1)}, bf16[576]{0:T(1024)(128)(2,1)}, u32[]{:S(2)}) copy-start(bf16[576]{0:T(1024)(128)(2,1)} %param.16) | copy-start | bytes 3460
  79.2 18.5 %copy-start.9 = (bf16[432,128]{1,0:T(8,128)(2,1)S(1)}, bf16[432,128]{1,0:T(8,128)(2,1)}, u32[]{:S(2)}) copy-start(bf16[432,128]{1,0:T(8,128)(2,1)} %copy-done.8) | copy-start | bytes 331780
  79.2 33.3 %copy-start.7 = (bf16[576,128]{1,0:T(8,128)(2,1)S(1)}, bf16[576,128]{1,0:T(8,128)(2,1)}, u32[]{:S(2)}) copy-start(bf16[576,128]{1,0:T(8,128)(2,1)} %enc_ref.3) | copy-start | bytes 442372
  79.2 3.8 %collective-permute-start.7 = (bf16[4,432,128]{2,1,0:T(8,128)(2,1)S(1)}, bf16[4,432,128]{2,1,0:T(8,128)(2,1)S(1)}, u32[]{:S(2)}, u32[]{:S(2)}) collective-permute-start(bf16[4,432,128]{2,1,0:T(8,128)(2,1)S(1)} %get-tuple-element.27), channel_id=1, source_target_pairs={{0,1},{1,0},{2,3},{3,2},{4,5},{5,4},{6,7},{7,6},{8,9},{9,8},{10,11... | collective-permute-start | bytes 1327112 | tf_op jit(solution)/shard_map/ppermute | solution.py:341
  83.9 13.8 %all-to-all-start.2 = ((bf16[4,432,128]{2,1,0:T(8,128)(2,1)}), bf16[4,432,128]{2,1,0:T(8,128)(2,1)S(1)}, u32[]{:S(2)}, u32[]{:S(2)}) async-start(bf16[4,432,128]{2,1,0:T(8,128)(2,1)} %add_convert_fusion), calls=%async_computation.2 | async-start | bytes 884736 | tf_op jit(solution)/shard_map/all_to_all | solution.py:342

commit v3 on v2

--- a/solution.py
+++ b/solution.py
@@ -18,6 +18,7 @@
 WIDTH = 128
 CHUNKS = ((0, 128), (128, 128), (256, 128), (384, 48))
 X_CHIPS = 4
+Z_CHIPS = 8
 LOW = -1e30
 eps = 1e-05
 F32 = jnp.float32
@@ -67,7 +68,14 @@
     packed_ref[...] = dot(hit, enc_ref[...]).astype(BF16)
 
 
-def weights_kernel(flags_ref, prob_ref, w_hi_ref, w_lo_ref, carry_ref, kept_ref, decay_ref):
+def weights_kernel(*refs):
+    flags_ref, prob_ref = refs[:2]
+    staged = (len(refs) - 8) // 2
+    given, (w_hi_ref, w_lo_ref, carry_ref, kept_ref, decay_ref) = refs[2 : 2 + staged], refs[2 + staged : 7 + staged]
+    held, sems = refs[7 + staged : 7 + 2 * staged], refs[-1]
+    copies = [pltpu.make_async_copy(a, b, sems.at[i]) for i, (a, b) in enumerate(zip(given, held))]
+    for copy in copies:
+        copy.start()
     flags = flags_ref[...].astype(F32)
     prob = prob_ref[...].astype(F32)
     logs = jnp.where(flags > 0, jnp.log1p(-prob), 0.0)
@@ -95,19 +103,25 @@
     carry_ref[...] = jnp.exp(jnp.where(real, total - kept_k, LOW)) * prob_k
     kept_ref[...] = jnp.broadcast_to(total, (1, WIDTH))
     decay_ref[...] = jnp.exp(kept)
+    for copy in copies:
+        copy.wait()
+
+
+def stack_kernel(r0, r1, r2, r3, out_ref):
+    for i, block in enumerate((r0, r1, r2, r3)):
+        out_ref[i] = block[...]
 
 
 def project_kernel(
-    r0, r1, r2, r3, s0, s1, s2, s3,
-    flags_ref, pad_ref, gain_ref, w_in_ref, w_dt_ref, pad_proj_ref, pad_dt_ref, bias_ref, a_log_ref,
+    near_ref, far_ref, flags_ref, pad_ref, gain_ref, w_in_ref, w_dt_ref, pad_proj_ref, pad_dt_ref, bias_ref, a_log_ref,
     proj_ref, step_ref, run_ref, run_t_ref, pieces_ref, normed_ref,
 ):
     x = lax.axis_index("x")
     core = lax.axis_index("core")
-    blocks = (r0, r1, r2, r3, s0, s1, s2, s3)
+    blocks = [ref[i] for ref in (near_ref, far_ref) for i in range(X_CHIPS)]
     energy = jnp.zeros((CAP, WIDTH), F32)
     for block in blocks:
-        wide = block[...].astype(F32)
+        wide = block.astype(F32)
         energy = energy + wide * wide
     pad = pad_ref[...]
     power = jnp.sum(energy, axis=1, keepdims=True) + jnp.sum(pad * pad)
@@ -118,7 +132,7 @@
         owner = chip * 2 + (core if other == 0 else 1 - core)
         gain = gain_ref[pl.ds(owner, 1), :]
         lanes = pl.ds(pl.multiple_of(owner * WIDTH, WIDTH), WIDTH)
-        normed_ref[:, lanes] = (block[...].astype(F32) * inverse * gain).astype(BF16)
+        normed_ref[:, lanes] = (block.astype(F32) * inverse * gain).astype(BF16)
 
     def tile(t, carry):
         lanes = pl.ds(pl.multiple_of(t * 256, 256), 256)
@@ -126,7 +140,7 @@
         return carry
 
     lax.fori_loop(0, COLS // 256, tile, 0)
-    raw = dot(normed_ref[...], w_dt_ref[...]) + inverse * pad_dt_ref[...] + bias_ref[...]
+    raw = dot(normed_ref[...], w_dt_ref[...], ((1,), (1,))) + inverse * pad_dt_ref[...] + bias_ref[...]
     soft = jnp.maximum(raw, 0.0) + jnp.log1p(jnp.exp(-jnp.abs(raw)))
     count = jnp.sum(flags_ref[...].astype(F32), axis=1, keepdims=True)
     real = iota((CAP, HEADS_HERE), 0).astype(F32) < count
@@ -150,14 +164,12 @@
     spare = jnp.concatenate(
         [total_wide[:, i * WIDTH : (i + 1) * WIDTH] for i in range(INNER // WIDTH)], axis=0
     )
-    act = pieces_ref.shape[0]
-    per = N // act
-    for d in range(act):
+    parts = pieces_ref.shape[0]
+    per = N // parts
+    for d in range(parts):
         pieces_ref[d, :, :INNER] = state[d * per : (d + 1) * per, :]
-        if per >= 4:
-            pieces_ref[d, 0:4, INNER:] = spare
-            if per > 4:
-                pieces_ref[d, 4:, INNER:] = jnp.zeros((per - 4, WIDTH), F32)
+        pieces_ref[d, 0:4, INNER:] = spare
+        pieces_ref[d, 4:, INNER:] = jnp.zeros((per - 4, WIDTH), F32)
 
 
 def local_kernel(proj_ref, step_ref, run_ref, run_t_ref, skip_ref, out_ref):
@@ -191,14 +203,31 @@
         start_run = end_run
 
 
-def scan_kernel(got_ref, before_ref):
-    act, per, _ = got_ref.shape
-    state = jnp.zeros((per, INNER), F32)
-    for j in range(act):
+def keep_of(logs):
+    keep = jnp.exp(logs)
+    return jnp.concatenate([keep[i : i + 1, :] for i in range(INNER // WIDTH)], axis=1)
+
+
+def total_kernel(got_ref, total_ref):
+    state, logs = got_ref[0, :, :INNER], got_ref[0, :, INNER:]
+    for j in range(1, got_ref.shape[0]):
+        more = got_ref[j, :, INNER:]
+        state = state * keep_of(more[0:4]) + got_ref[j, :, :INNER]
+        logs = logs + more
+    for i in range(total_ref.shape[0]):
+        total_ref[i, :, :INNER] = state
+        total_ref[i, :, INNER:] = logs
+
+
+def scan_kernel(got_ref, rows_ref, before_ref):
+    y = lax.axis_index("y")
+    state = jnp.zeros(before_ref.shape[1:], F32)
+    for j in range(rows_ref.shape[0]):
+        after = state * keep_of(rows_ref[j, 0:4, INNER:]) + rows_ref[j, :, :INNER]
+        state = jnp.where(j < y, after, state)
+    for j in range(got_ref.shape[0]):
         before_ref[j] = state
-        keep = jnp.exp(got_ref[j, 0:4, INNER:])
-        keep = jnp.concatenate([keep[i : i + 1, :] for i in range(INNER // WIDTH)], axis=1)
-        state = state * keep + got_ref[j, :, :INNER]
+        state = state * keep_of(got_ref[j, 0:4, INNER:]) + got_ref[j, :, :INNER]
 
 
 def output_kernel(proj_ref, run_ref, local_ref, state_ref, gain_ref, w_out_ref, kept_ref, sent_ref, full_ref):
@@ -219,12 +248,17 @@
         sent_ref[i] = jnp.where(core == 0, second, first).astype(BF16)
 
 
-def main_kernel(packed_ref, parts_ref, carry_ref, kept_ref, main_ref, sent_ref):
-    summed = packed_ref[...].astype(F32)
-    added = parts_ref[0].astype(F32)
-    for i in range(1, X_CHIPS):
-        added = added + parts_ref[i].astype(F32)
-    main = (summed + added).astype(BF16)
+def pair_kernel(packed_ref, own_ref, got_ref, keep_ref, s1, s2, s3):
+    x = lax.axis_index("x")
+    keep_ref[...] = packed_ref[...].astype(F32) + (own_ref[x] + got_ref[x].astype(F32))
+    for s, out_ref in enumerate((s1, s2, s3), start=1):
+        chip = lax.rem(x + s, X_CHIPS)
+        out_ref[...] = (own_ref[chip] + got_ref[chip].astype(F32)).astype(BF16)
+
+
+def main_kernel(keep_ref, r1, r2, r3, carry_ref, kept_ref, main_ref, sent_ref):
+    added = r1[...].astype(F32) + r2[...].astype(F32) + r3[...].astype(F32)
+    main = (keep_ref[...] + added).astype(BF16)
     main_ref[...] = main
     split = jnp.concatenate([jnp.broadcast_to(p, (8, CAP)) for p in thirds(carry_ref[...])], axis=0)
     sums = dot(split, main)
@@ -233,13 +267,22 @@
     sent_ref[...] = jnp.broadcast_to(row[None], sent_ref.shape)
 
 
-def decode_kernel(enc_ref, w_hi_ref, w_lo_ref, main_ref, decay_ref, carries_ref, out_ref):
-    me = lax.axis_index("act")
-    act = carries_ref.shape[0]
+def carry_kernel(got_ref, sent_ref):
+    carry, logs = got_ref[0, 0:1, :], got_ref[0, 1:2, :]
+    for j in range(1, got_ref.shape[0]):
+        more = got_ref[j, 1:2, :]
+        carry = carry * jnp.exp(more) + got_ref[j, 0:1, :]
+        logs = logs + more
+    row = jnp.concatenate([carry, logs], axis=0)
+    sent_ref[...] = jnp.broadcast_to(row[None], sent_ref.shape)
+
+
+def decode_kernel(enc_ref, w_hi_ref, w_lo_ref, main_ref, decay_ref, row_ref, rows_ref, out_ref):
     carry = jnp.zeros((1, WIDTH), F32)
-    for j in range(act):
-        after = carry * jnp.exp(carries_ref[j, 1:2, :]) + carries_ref[j, 0:1, :]
-        carry = jnp.where(j < me, after, carry)
+    for ref, place in ((rows_ref, lax.axis_index("y")), (row_ref, lax.axis_index("z"))):
+        for j in range(ref.shape[0]):
+            after = carry * jnp.exp(ref[j, 1:2, :]) + ref[j, 0:1, :]
+            carry = jnp.where(j < place, after, carry)
     main = main_ref[...]
     smoothed = dot(w_hi_ref[...], main) + dot(w_lo_ref[...], main) + decay_ref[...] * carry
     out_ref[...] = (enc_ref[...].astype(F32) + smoothed).astype(BF16)
@@ -249,17 +292,23 @@
     return jax.ShapeDtypeStruct(dims, dtype)
 
 
-def call(kernel, outs, name, scratch=(), flops=0, transcendentals=0, nbytes=0):
+def call(kernel, outs, name, in_specs=None, scratch=(), vmem=12, flops=0, transcendentals=0, nbytes=0):
+    more = {} if in_specs is None else {"in_specs": in_specs}
     return pl.pallas_call(
         kernel,
         out_shape=outs,
         name=name,
         scratch_shapes=scratch,
-        compiler_params=pltpu.CompilerParams(vmem_limit_bytes=40 * 2**20),
+        compiler_params=pltpu.CompilerParams(vmem_limit_bytes=vmem * 2**20),
         cost_estimate=pl.CostEstimate(
             flops=flops, transcendentals=transcendentals, bytes_accessed=nbytes
         ),
-    )
+        **more,
+    )
+
+
+def over_chips(a, s):
+    return lax.ppermute(a, "x", [(i, (i + s) % X_CHIPS) for i in range(X_CHIPS)])
 
 
 def body(
@@ -278,31 +327,39 @@
     gate_gain,
     w_out,
 ):
-    act = lax.axis_size("act")
+    y_size, z_size = lax.axis_size("y"), lax.axis_size("z")
     row = lambda a: a.reshape(1, -1)
     flags, prob = row(boundary_flags), row(boundary_prob)
     packed = call(select_kernel, shape((CAP, WIDTH), BF16), "select", flops=10**8)(flags, enc_rows)
 
-    around = [packed] + [
-        lax.ppermute(packed, "x", [(i, (i + s) % X_CHIPS) for i in range(X_CHIPS)])
-        for s in range(1, X_CHIPS)
+    around = [over_chips(packed, s) for s in range(1, X_CHIPS)]
+    near = call(stack_kernel, shape((X_CHIPS, CAP, WIDTH), BF16), "stack", nbytes=10**6)(packed, *around)
+    far = lax.ppermute(near, "core", [(0, 1), (1, 0)])
+
+    given = [
+        w_in, w_out, w_dt.T, pad_vector.reshape(-1, WIDTH), norm_gain.reshape(-1, WIDTH), row(pad_proj),
+        row(pad_dt), row(dt_bias), row(a_log), row(d_skip), row(gate_gain),
     ]
-    across = [lax.ppermute(a, "core", [(0, 1), (1, 0)]) for a in around]
-
-    w_hi, w_lo, carry_w, kept, decay = call(
+    any_spec, vmem_spec = pl.BlockSpec(memory_space=pl.ANY), pl.BlockSpec(memory_space=pltpu.VMEM)
+    w_hi, w_lo, carry_w, kept, decay, *held = call(
         weights_kernel,
-        (
+        [
             shape((BYTES, CAP), BF16),
             shape((BYTES, CAP), BF16),
             shape((1, CAP)),
             shape((1, WIDTH)),
             shape((BYTES, 1)),
-        ),
+        ]
+        + [shape(a.shape, a.dtype) for a in given],
         "weights",
+        in_specs=[vmem_spec] * 2 + [any_spec] * len(given),
+        scratch=[pltpu.SemaphoreType.DMA((len(given),))],
+        vmem=16,
         transcendentals=BYTES * CAP,
         flops=BYTES * CAP * 30,
-        nbytes=10**6,
-    )(flags, prob)
+        nbytes=5 * 10**6,
+    )(flags, prob, *given)
+    w_in, w_out, w_dt, pad_vector, norm_gain, pad_proj, pad_dt, dt_bias, a_log, d_skip, gate_gain = held
 
     proj, step, run, run_t, pieces = call(
         project_kernel,
@@ -311,50 +368,58 @@
             shape((CAP, HEADS_HERE)),
             shape((CAP, HEADS_HERE)),
             shape((HEADS_HERE, CAP)),
-            shape((act, N // act, INNER + WIDTH)),
+            shape((z_size, N // z_size, INNER + WIDTH)),
         ),
         "project",
         scratch=[pltpu.VMEM((CAP, D), BF16)],
+        vmem=20,
         flops=2 * CAP * D * COLS,
         nbytes=8 * 10**6,
-    )(
-        *around, *across, flags, pad_vector.reshape(-1, WIDTH), norm_gain.reshape(-1, WIDTH), w_in, w_dt,
-        row(pad_proj), row(pad_dt), row(dt_bias), row(a_log),
-    )
-
-    got = lax.all_to_all(pieces, "act", 0, 0)
+    )(near, far, flags, pad_vector, norm_gain, w_in, w_dt, pad_proj, pad_dt, dt_bias, a_log)
+
+    got = lax.all_to_all(pieces, "z", 0, 0)
+    totals = call(total_kernel, shape((y_size,) + pieces.shape[1:]), "total", nbytes=4 * 10**5)(got)
+    rows = lax.all_to_all(totals, "y", 0, 0)
     local = call(
         local_kernel, shape((CAP, INNER)), "local", flops=10**9, transcendentals=CAP * 1024, nbytes=3 * 10**6
-    )(proj, step, run, run_t, row(d_skip))
-    before = call(scan_kernel, shape((act, N // act, INNER)), "scan", nbytes=6 * 10**5)(got)
-    state_in = lax.all_to_all(before, "act", 0, 0)
+    )(proj, step, run, run_t, d_skip)
+    before = call(scan_kernel, shape((z_size, N // z_size, INNER)), "scan", nbytes=6 * 10**5)(got, rows)
+    state_in = lax.all_to_all(before, "z", 0, 0)
 
     own, sent = call(
         output_kernel,
         (shape((X_CHIPS, CAP, WIDTH)), shape((X_CHIPS, CAP, WIDTH), BF16)),
         "output",
         scratch=[pltpu.VMEM((N, INNER), F32)],
+        vmem=16,
         flops=2 * CAP * INNER * D,
         nbytes=6 * 10**6,
-    )(proj, run, local, state_in, row(gate_gain), w_out)
-
-    pair = (own + lax.ppermute(sent, "core", [(0, 1), (1, 0)]).astype(F32)).astype(BF16)
-    parts = lax.all_to_all(pair, "x", 0, 0)
+    )(proj, run, local, state_in, gate_gain, w_out)
+
+    got_sums = lax.ppermute(sent, "core", [(0, 1), (1, 0)])
+    block = shape((CAP, WIDTH), BF16)
+    keep, *parts = call(
+        pair_kernel, (shape((CAP, WIDTH)), block, block, block), "pair", nbytes=2 * 10**6
+    )(packed, own, got_sums)
+    parts = [over_chips(a, s) for s, a in enumerate(parts, start=1)]
     main, carry = call(
-        main_kernel, (shape((CAP, WIDTH), BF16), shape((act, 2, WIDTH))), "main", nbytes=6 * 10**5
-    )(packed, parts, carry_w, kept)
-    carries = lax.all_to_all(carry, "act", 0, 0)
+        main_kernel, (block, shape((z_size, 2, WIDTH))), "main", nbytes=6 * 10**5
+    )(keep, *parts, carry_w, kept)
+    row_carries = lax.all_to_all(carry, "z", 0, 0)
+    row_total = call(carry_kernel, shape((y_size, 2, WIDTH)), "carry")(row_carries)
+    all_carries = lax.all_to_all(row_total, "y", 0, 0)
     return call(
         decode_kernel, shape((BYTES, WIDTH), BF16), "decode", flops=2 * 10**8, nbytes=2 * 10**6
-    )(enc_rows, w_hi, w_lo, main, decay, carries)
+    )(enc_rows, w_hi, w_lo, main, decay, row_carries, all_carries)
 
 
 def solution(mesh):
     seq = mesh.shape["seq"]
     split = Mesh(
-        mesh.devices.reshape(2, seq // 2, X_CHIPS, 2), ("half", "act", "x", "core")
-    )
-    by_seq, by_head = ("half", "act"), ("x", "core")
+        mesh.devices.reshape(2, seq // 2 // Z_CHIPS, Z_CHIPS, X_CHIPS, 2),
+        ("half", "y", "z", "x", "core"),
+    )
+    by_seq, by_head = ("half", "y", "z"), ("x", "core")
     in_specs = (
         P(by_seq, by_head),
         P(by_seq),

time: 115 us -> 131 us (1.14)
  blocking collectives: 38.2 us -> 50.3 us
  local copies, waits for them, and re-layouts: 13.2 us -> 18.6 us
  starting transfers between devices: 34.2 us -> 29.7 us
  waiting for transfers between devices: 14.2 us -> 17.6 us
    all_to_all x2 -> x4, blocking collectives: 38.2 us -> 50.3 us  [the longest x1 19.3 us: body(): got = lax.all_to_all(pieces, 'z', 0, 0)]
    ppermute x8, waiting for transfers between devices: 1.78 us -> 12.5 us  [the longest x6 10.7 us: over_chips(): lax.ppermute(a, 'x', [(i, (i + s) % X_CHIPS) for i in range(X_CHIPS)])]
    all_to_all x2 -> x1, starting transfers between devices: 11.1 us -> 3.41 us  [body(): state_in = lax.all_to_all(before, 'z', 0, 0)]
    all_to_all x2 -> x1, waiting for transfers between devices: 12.4 us -> 5.15 us  [body(): state_in = lax.all_to_all(before, 'z', 0, 0)]
    unnamed x43 -> x54, local copies, waits for them, and re-layouts: 11.8 us -> 16.5 us
    ppermute x8, starting transfers between devices: 23.2 us -> 26.3 us  [the longest x6 22.5 us: over_chips(): lax.ppermute(a, 'x', [(i, (i + s) % X_CHIPS) for i in range(X_CHIPS)])]
    pallas_call x3 -> x7, Pallas kernels: 2.25 us -> 2.81 us  [the longest x1 1.67 us: body(): call(weights_kernel, [shape((BYTES, CAP), BF16), shape((BYTES, CAP), BF16...]
  transfers between devices with their start and end apart: 10 -> 9, of which waited for: 3 -> 6; matrix products, arithmetic and copies ran while one was open for 1% -> 1% of each run, Pallas kernels for 3% -> 3%
where the time goes in v3:
time: 131 us; the launch traced here: 130 us
  blocking collectives  50.3 us (38%)
  starting transfers between devices  29.7 us (23%)
  local copies, waits for them, and re-layouts  18.6 us (14%)
  waiting for transfers between devices  17.6 us (13%)
  Pallas kernels  13.1 us (10%)
    ppermute x6, starting transfers between devices, over_chips(): lax.ppermute(a, 'x', [(i, (i + s) % X_CHIPS) for i in range(X_CHIPS)])  22.5 us
    all_to_all x1, blocking collectives, body(): got = lax.all_to_all(pieces, 'z', 0, 0)  19.3 us
    unnamed x54, local copies, waits for them, and re-layouts  16.5 us
    all_to_all x1, blocking collectives, body(): rows = lax.all_to_all(totals, 'y', 0, 0)  11.6 us
    ppermute x6, waiting for transfers between devices, over_chips(): lax.ppermute(a, 'x', [(i, (i + s) % X_CHIPS) for i in range(X_CHIPS)])  10.7 us
    all_to_all x1, blocking collectives, body(): row_carries = lax.all_to_all(carry, 'z', 0, 0)  10.1 us
    all_to_all x1, blocking collectives, body(): all_carries = lax.all_to_all(row_total, 'y', 0, 0)  9.4 us
    all_to_all x1, waiting for transfers between devices, body(): state_in = lax.all_to_all(before, 'z', 0, 0)  5.15 us
  transfers between devices with their start and end apart: 9, of which 6 were waited for; matrix products, arithmetic and copies ran while one was open for 1% of the time, Pallas kernels for 3%

profile of v3, /device:TPU:6, one launch (start us, length us, event | category | flops | bytes accessed | tf_op | source)
XLA Modules:
  0.0 129.6 jit_solution(13825322927074435990)
XLA Ops:
  0.7 0.9 copy-done.15
  2.1 2.7 %collective-permute-start.2 = (bf16[432,128]{1,0:T(8,128)(2,1)S(1)}, bf16[432,128]{1,0:T(8,128)(2,1)S(1)}, u32[]{:S(2)}, u32[]{:S(2)}) collective-permute-start(bf16[432,128]{1,0:T(8,128)(2,1)S(1)} %select.1.r0.packed_ref), channel_id=1, source_target_pairs={{0,6},{2,0},{4,2},{6,4},{1,7},{3,1},{5,3},{7,5},{8,14},{10,8},{12,... | collective-permute-start | bytes 331784 | tf_op jit(solution)/shard_map/ppermute | solution.py:311
  4.9 8.4 %collective-permute-start.1 = (bf16[432,128]{1,0:T(8,128)(2,1)S(1)}, bf16[432,128]{1,0:T(8,128)(2,1)S(1)}, u32[]{:S(2)}, u32[]{:S(2)}) collective-permute-start(bf16[432,128]{1,0:T(8,128)(2,1)S(1)} %select.1.r0.packed_ref), channel_id=1, source_target_pairs={{0,4},{2,6},{4,0},{6,2},{1,5},{3,7},{5,1},{7,3},{8,12},{10,14},{12... | collective-permute-start | bytes 331784 | tf_op jit(solution)/shard_map/ppermute | solution.py:311
  13.3 1.9 %collective-permute-start = (bf16[432,128]{1,0:T(8,128)(2,1)S(1)}, bf16[432,128]{1,0:T(8,128)(2,1)S(1)}, u32[]{:S(2)}, u32[]{:S(2)}) collective-permute-start(bf16[432,128]{1,0:T(8,128)(2,1)S(1)} %select.1.r0.packed_ref), channel_id=1, source_target_pairs={{0,2},{2,4},{4,6},{6,0},{1,3},{3,5},{5,7},{7,1},{8,10},{10,12},{12... | collective-permute-start | bytes 331784 | tf_op jit(solution)/shard_map/ppermute | solution.py:311
  16.0 3.9 %collective-permute-done.r1 = bf16[432,128]{1,0:T(8,128)(2,1)S(1)} collective-permute-done((bf16[432,128]{1,0:T(8,128)(2,1)S(1)}, bf16[432,128]{1,0:T(8,128)(2,1)S(1)}, u32[]{:S(2)}, u32[]{:S(2)}) %collective-permute-start) | collective-permute-done | bytes 110624 | tf_op jit(solution)/shard_map/ppermute | solution.py:311
  20.0 1.9 %collective-permute-start.3 = (bf16[4,432,128]{2,1,0:T(8,128)(2,1)S(1)}, bf16[4,432,128]{2,1,0:T(8,128)(2,1)S(1)}, u32[]{:S(2)}, u32[]{:S(2)}) collective-permute-start(bf16[4,432,128]{2,1,0:T(8,128)(2,1)S(1)} %stack.1.near_ref), channel_id=1, source_target_pairs={{0,1},{1,0},{2,3},{3,2},{4,5},{5,4},{6,7},{7,6},{8,9},{9,8},{10,11... | collective-permute-start | bytes 1327112 | tf_op jit(solution)/shard_map/ppermute | solution.py:337
  23.3 1.7 %copy-done = bf16[1024,1280]{1,0:T(8,128)(2,1)S(1)} copy-done((bf16[1024,1280]{1,0:T(8,128)(2,1)S(1)}, bf16[1024,1280]{1,0:T(8,128)(2,1)}, u32[]{:S(2)}) %copy-start) | copy-done | bytes 2621464
  25.0 1.2 copy-done.1
  31.6 1.7 %weights.1 = (bf16[576,432]{1,0:T(8,128)(2,1)S(1)}, bf16[576,432]{1,0:T(8,128)(2,1)S(1)}, f32[1,432]{1,0:T(1,128)S(1)}, f32[1,128]{1,0:T(1,128)S(1)}, f32[576,1]...) custom-call(s32[1,576]{1,0:T(1,128)S(1)} %reshape.30.refs_0_.flags_r, ...), custom_call_target="tpu_custom_call" | custom-call | flops 7464960 | bytes 5000000 | tf_op jit(solution)/shard_map/weights/pallas_call | solution.py:344
  34.1 0.8 copy-done.6
  35.7 4.5 %project.1 = (f32[432,1280]{1,0:T(8,128)S(1)}, f32[432,8]{1,0:T(8,128)S(1)}, f32[432,8]{1,0:T(8,128)S(1)}, f32[8,432]{1,0:T(8,128)S(1)}, f32[8,16,640]{2,1,0:T(8,128)S(1)}) custom-call(bf16[4,432,128]{2,1,0:T(8,128)(2,1)S(1)} %stack.1.near_ref, bf16[4,432,128]{2,1,0:T(8,128)(2,1)S(1)} %collective-permute-done.3.far_ref, ...), custom_call_target="tpu_custom_call" | custom-call | flops 1132462080 | bytes 8000000 | tf_op jit(solution)/shard_map/project/pallas_call | solution.py:364
  40.2 19.3 %all_to_all.25.got_ref = f32[8,16,640]{2,1,0:T(8,128)S(1)} all-to-all(f32[8,16,640]{2,1,0:T(8,128)S(1)} %get-tuple-element.49), channel_id=1, replica_groups=mesh['half'=2,'y'=4,'z'=8,'x'=4,'core'=2] {'z'}, dimensions={0} | all-to-all | bytes 655360 | tf_op jit(solution)/shard_map/all_to_all | solution.py:380
  59.5 11.6 %all_to_all.26.rows_ref = f32[4,16,640]{2,1,0:T(8,128)S(1)} all-to-all(f32[4,16,640]{2,1,0:T(8,128)S(1)} %total.1), channel_id=1, replica_groups=mesh['half'=2,'y'=4,'z'=8,'x'=4,'core'=2] {'y'}, dimensions={0} | all-to-all | bytes 327680 | tf_op jit(solution)/shard_map/all_to_all | solution.py:382
  71.8 3.4 %all-to-all-start.2 = ((f32[8,16,512]{2,1,0:T(8,128)}), f32[8,16,512]{2,1,0:T(8,128)S(1)}, u32[]{:S(2)}, u32[]{:S(2)}) async-start(f32[8,16,512]{2,1,0:T(8,128)} %scan.1), calls=%async_computation.2 | async-start | bytes 524288 | tf_op jit(solution)/shard_map/all_to_all | solution.py:387
  75.3 0.9 copy-done.13
  76.2 0.9 copy-done.26
  77.1 2.7 %local.1.local_ref = f32[432,512]{1,0:T(8,128)S(1)} custom-call(f32[432,1280]{1,0:T(8,128)S(1)} %get-tuple-element.44.proj_ref, f32[432,8]{1,0:T(8,128)S(1)} %copy-done.26, f32[432,8]{1,0:T(8,128)S(1)} %copy-done.13, f32[8,432]{1,0:T(8,128)S(1)} %get-tuple-element.47.run_t_ref, f32[1,8]{1,0:T(1,128)S(1)} %get-tuple-element.48.skip_ref), custom_call_target="tpu_custom_call" | custom-call | flops 1000000000 | bytes 3000000 | tf_op jit(solution)/shard_map/local/pallas_call | solution.py:383
  79.8 0.9 copy-done.2
  80.8 5.2 %all-to-all-done.2.state_ref = f32[8,16,512]{2,1,0:T(8,128)S(1)} async-done(((f32[8,16,512]{2,1,0:T(8,128)}), f32[8,16,512]{2,1,0:T(8,128)S(1)}, u32[]{:S(2)}, u32[]{:S(2)}) %all-to-all-start.2) | async-done | bytes 262176 | tf_op jit(solution)/shard_map/all_to_all | solution.py:387
  85.9 1.2 copy-done.3
  87.1 0.9 copy-done.14
  88.0 1.4 %output.1 = (f32[4,432,128]{2,1,0:T(8,128)S(1)}, bf16[4,432,128]{2,1,0:T(8,128)(2,1)S(1)}) custom-call(f32[432,1280]{1,0:T(8,128)S(1)} %get-tuple-element.44.proj_ref, f32[432,8]{1,0:T(8,128)S(1)} %copy-done.14, f32[432,512]{1,0:T(8,128)S(1)} %copy-done.3, f32[8,16,512]{2,1,0:T(8,128)S(1)} %all-to-all-done.2.state_ref, ...), custom_call_target="tpu_custom_call" | custom-call | flops 452984832 | bytes 6000000 | tf_op jit(solution)/shard_map/output/pallas_call | solution.py:389
  89.5 1.9 %collective-permute-start.4 = (bf16[4,432,128]{2,1,0:T(8,128)(2,1)S(1)}, bf16[4,432,128]{2,1,0:T(8,128)(2,1)S(1)}, u32[]{:S(2)}, u32[]{:S(2)}) collective-permute-start(bf16[4,432,128]{2,1,0:T(8,128)(2,1)S(1)} %get-tuple-element.53), channel_id=1, source_target_pairs={{0,1},{1,0},{2,3},{3,2},{4,5},{5,4},{6,7},{7,6},{8,9},{9,8},{10,11... | collective-permute-start | bytes 1327112 | tf_op jit(solution)/shard_map/ppermute | solution.py:399
  91.4 1.8 %collective-permute-done.4.got_ref = bf16[4,432,128]{2,1,0:T(8,128)(2,1)S(1)} collective-permute-done((bf16[4,432,128]{2,1,0:T(8,128)(2,1)S(1)}, bf16[4,432,128]{2,1,0:T(8,128)(2,1)S(1)}, u32[]{:S(2)}, u32[]{:S(2)}) %collective-permute-start.4) | collective-permute-done | bytes 442400 | tf_op jit(solution)/shard_map/ppermute | solution.py:399
  93.3 4.7 %collective-permute-start.5 = (bf16[432,128]{1,0:T(8,128)(2,1)S(1)}, bf16[432,128]{1,0:T(8,128)(2,1)S(1)}, u32[]{:S(2)}, u32[]{:S(2)}) collective-permute-start(bf16[432,128]{1,0:T(8,128)(2,1)S(1)} %get-tuple-element.55), channel_id=1, source_target_pairs={{0,2},{2,4},{4,6},{6,0},{1,3},{3,5},{5,7},{7,1},{8,10},{10,12},{12... | collective-permute-start | bytes 331784 | tf_op jit(solution)/shard_map/ppermute | solution.py:311
  98.0 2.7 %collective-permute-start.6 = (bf16[432,128]{1,0:T(8,128)(2,1)S(1)}, bf16[432,128]{1,0:T(8,128)(2,1)S(1)}, u32[]{:S(2)}, u32[]{:S(2)}) collective-permute-start(bf16[432,128]{1,0:T(8,128)(2,1)S(1)} %get-tuple-element.56), channel_id=1, source_target_pairs={{0,4},{2,6},{4,0},{6,2},{1,5},{3,7},{5,1},{7,3},{8,12},{10,14},{12... | collective-permute-start | bytes 331784 | tf_op jit(solution)/shard_map/ppermute | solution.py:311
  100.8 2.0 %collective-permute-start.7 = (bf16[432,128]{1,0:T(8,128)(2,1)S(1)}, bf16[432,128]{1,0:T(8,128)(2,1)S(1)}, u32[]{:S(2)}, u32[]{:S(2)}) collective-permute-start(bf16[432,128]{1,0:T(8,128)(2,1)S(1)} %get-tuple-element.57), channel_id=1, source_target_pairs={{0,6},{2,0},{4,2},{6,4},{1,7},{3,1},{5,3},{7,5},{8,14},{10,8},{12,... | collective-permute-start | bytes 331784 | tf_op jit(solution)/shard_map/ppermute | solution.py:311
  102.8 4.0 %collective-permute-done.6.r2 = bf16[432,128]{1,0:T(8,128)(2,1)S(1)} collective-permute-done((bf16[432,128]{1,0:T(8,128)(2,1)S(1)}, bf16[432,128]{1,0:T(8,128)(2,1)S(1)}, u32[]{:S(2)}, u32[]{:S(2)}) %collective-permute-start.6) | collective-permute-done | bytes 110624 | tf_op jit(solution)/shard_map/ppermute | solution.py:311
  106.7 2.0 %collective-permute-done.7.r3 = bf16[432,128]{1,0:T(8,128)(2,1)S(1)} collective-permute-done((bf16[432,128]{1,0:T(8,128)(2,1)S(1)}, bf16[432,128]{1,0:T(8,128)(2,1)S(1)}, u32[]{:S(2)}, u32[]{:S(2)}) %collective-permute-start.7) | collective-permute-done | bytes 110624 | tf_op jit(solution)/shard_map/ppermute | solution.py:311
  108.9 10.1 %all_to_all.27.got_ref.row_ref = f32[8,2,128]{2,1,0:T(2,128)S(1)} all-to-all(f32[8,2,128]{2,1,0:T(2,128)S(1)} %get-tuple-element.62), channel_id=1, replica_groups=mesh['half'=2,'y'=4,'z'=8,'x'=4,'core'=2] {'z'}, dimensions={0} | all-to-all | bytes 16384 | tf_op jit(solution)/shard_map/all_to_all | solution.py:408
  119.0 9.4 %all_to_all.28.rows_ref = f32[4,2,128]{2,1,0:T(2,128)S(1)} all-to-all(f32[4,2,128]{2,1,0:T(2,128)S(1)} %carry.1), channel_id=1, replica_groups=mesh['half'=2,'y'=4,'z'=8,'x'=4,'core'=2] {'y'}, dimensions={0} | all-to-all | bytes 8192 | tf_op jit(solution)/shard_map/all_to_all | solution.py:410
  128.5 1.1 decode.1
  (59 shorter events, 11.5 us)
Async XLA Ops:
  0.7 0.9 copy-start.15
  2.1 21.2 %copy-start.8 = (bf16[432,128]{1,0:T(8,128)(2,1)}, bf16[432,128]{1,0:T(8,128)(2,1)S(1)}, u32[]{:S(2)}) copy-start(bf16[432,128]{1,0:T(8,128)(2,1)S(1)} %select.1.r0.packed_ref) | copy-start | bytes 331780
  2.1 13.1 %collective-permute-start.2 = (bf16[432,128]{1,0:T(8,128)(2,1)S(1)}, bf16[432,128]{1,0:T(8,128)(2,1)S(1)}, u32[]{:S(2)}, u32[]{:S(2)}) collective-permute-start(bf16[432,128]{1,0:T(8,128)(2,1)S(1)} %select.1.r0.packed_ref), channel_id=1, source_target_pairs={{0,6},{2,0},{4,2},{6,4},{1,7},{3,1},{5,3},{7,5},{8,14},{10,8},{12,... | collective-permute-start | bytes 331784 | tf_op jit(solution)/shard_map/ppermute | solution.py:311
  4.9 11.1 %collective-permute-start.1 = (bf16[432,128]{1,0:T(8,128)(2,1)S(1)}, bf16[432,128]{1,0:T(8,128)(2,1)S(1)}, u32[]{:S(2)}, u32[]{:S(2)}) collective-permute-start(bf16[432,128]{1,0:T(8,128)(2,1)S(1)} %select.1.r0.packed_ref), channel_id=1, source_target_pairs={{0,4},{2,6},{4,0},{6,2},{1,5},{3,7},{5,1},{7,3},{8,12},{10,14},{12... | collective-permute-start | bytes 331784 | tf_op jit(solution)/shard_map/ppermute | solution.py:311
  13.3 6.6 %collective-permute-start = (bf16[432,128]{1,0:T(8,128)(2,1)S(1)}, bf16[432,128]{1,0:T(8,128)(2,1)S(1)}, u32[]{:S(2)}, u32[]{:S(2)}) collective-permute-start(bf16[432,128]{1,0:T(8,128)(2,1)S(1)} %select.1.r0.packed_ref), channel_id=1, source_target_pairs={{0,2},{2,4},{4,6},{6,0},{1,3},{3,5},{5,7},{7,1},{8,10},{10,12},{12... | collective-permute-start | bytes 331784 | tf_op jit(solution)/shard_map/ppermute | solution.py:311
  20.0 15.7 %collective-permute-start.3 = (bf16[4,432,128]{2,1,0:T(8,128)(2,1)S(1)}, bf16[4,432,128]{2,1,0:T(8,128)(2,1)S(1)}, u32[]{:S(2)}, u32[]{:S(2)}) collective-permute-start(bf16[4,432,128]{2,1,0:T(8,128)(2,1)S(1)} %stack.1.near_ref), channel_id=1, source_target_pairs={{0,1},{1,0},{2,3},{3,2},{4,5},{5,4},{6,7},{7,6},{8,9},{9,8},{10,11... | collective-permute-start | bytes 1327112 | tf_op jit(solution)/shard_map/ppermute | solution.py:337
  23.3 1.7 %copy-start = (bf16[1024,1280]{1,0:T(8,128)(2,1)S(1)}, bf16[1024,1280]{1,0:T(8,128)(2,1)}, u32[]{:S(2)}) copy-start(bf16[1024,1280]{1,0:T(8,128)(2,1)} %refs_2_.1) | copy-start | bytes 7864324
  25.0 1.2 copy-start.1
  26.2 0.7 copy-start.17
  27.0 0.7 copy-start.18
  27.6 0.7 copy-start.19
  28.3 0.7 copy-start.20
  33.3 0.8 copy-start.4
  34.1 0.8 copy-start.6
  34.9 0.7 copy-start.10
  40.2 19.3 %copy-start.25 = (f32[432,8]{1,0:T(8,128)}, f32[432,8]{1,0:T(8,128)S(1)}, u32[]{:S(2)}) copy-start(f32[432,8]{1,0:T(8,128)S(1)} %get-tuple-element.46.step_ref) | copy-start | bytes 41476
  40.2 30.9 %copy-start.12 = (f32[432,8]{1,0:T(8,128)}, f32[432,8]{1,0:T(8,128)S(1)}, u32[]{:S(2)}) copy-start(f32[432,8]{1,0:T(8,128)S(1)} %get-tuple-element.45.run_ref) | copy-start | bytes 41476
  71.8 14.1 %all-to-all-start.2 = ((f32[8,16,512]{2,1,0:T(8,128)}), f32[8,16,512]{2,1,0:T(8,128)S(1)}, u32[]{:S(2)}, u32[]{:S(2)}) async-start(f32[8,16,512]{2,1,0:T(8,128)} %scan.1), calls=%async_computation.2 | async-start | bytes 524288 | tf_op jit(solution)/shard_map/all_to_all | solution.py:387
  75.3 0.9 copy-start.13
  76.2 0.9 copy-start.26
  79.8 0.9 copy-start.2
  85.9 1.2 copy-start.3
  87.1 0.9 copy-start.14
  88.0 5.2 %copy-start.9 = (bf16[432,128]{1,0:T(8,128)(2,1)S(1)}, bf16[432,128]{1,0:T(8,128)(2,1)}, u32[]{:S(2)}) copy-start(bf16[432,128]{1,0:T(8,128)(2,1)} %copy-done.8) | copy-start | bytes 331780
  88.0 40.4 %copy-start.5 = (bf16[576,432]{1,0:T(8,128)(2,1)S(1)}, bf16[576,432]{1,0:T(8,128)(2,1)}, u32[]{:S(2)}) copy-start(bf16[576,432]{1,0:T(8,128)(2,1)} %copy-done.4) | copy-start | bytes 1492996
  88.0 40.4 %copy-start.7 = (bf16[576,432]{1,0:T(8,128)(2,1)S(1)}, bf16[576,432]{1,0:T(8,128)(2,1)}, u32[]{:S(2)}) copy-start(bf16[576,432]{1,0:T(8,128)(2,1)} %copy-done.6) | copy-start | bytes 1492996
  88.0 40.4 %copy-start.11 = (f32[576,1]{1,0:T(8,128)S(1)}, f32[576,1]{1,0:T(8,128)}, u32[]{:S(2)}) copy-start(f32[576,1]{1,0:T(8,128)} %copy-done.10) | copy-start | bytes 6916
  88.0 40.4 %copy-start.16 = (bf16[576,128]{1,0:T(8,128)(2,1)S(1)}, bf16[576,128]{1,0:T(8,128)(2,1)}, u32[]{:S(2)}) copy-start(bf16[576,128]{1,0:T(8,128)(2,1)} %enc_ref.3) | copy-start | bytes 442372
  89.5 3.7 %collective-permute-start.4 = (bf16[4,432,128]{2,1,0:T(8,128)(2,1)S(1)}, bf16[4,432,128]{2,1,0:T(8,128)(2,1)S(1)}, u32[]{:S(2)}, u32[]{:S(2)}) collective-permute-start(bf16[4,432,128]{2,1,0:T(8,128)(2,1)S(1)} %get-tuple-element.53), channel_id=1, source_target_pairs={{0,1},{1,0},{2,3},{3,2},{4,5},{5,4},{6,7},{7,6},{8,9},{9,8},{10,11... | collective-permute-start | bytes 1327112 | tf_op jit(solution)/shard_map/ppermute | solution.py:399
  93.3 9.5 %collective-permute-start.5 = (bf16[432,128]{1,0:T(8,128)(2,1)S(1)}, bf16[432,128]{1,0:T(8,128)(2,1)S(1)}, u32[]{:S(2)}, u32[]{:S(2)}) collective-permute-start(bf16[432,128]{1,0:T(8,128)(2,1)S(1)} %get-tuple-element.55), channel_id=1, source_target_pairs={{0,2},{2,4},{4,6},{6,0},{1,3},{3,5},{5,7},{7,1},{8,10},{10,12},{12... | collective-permute-start | bytes 331784 | tf_op jit(solution)/shard_map/ppermute | solution.py:311
  98.0 8.7 %collective-permute-start.6 = (bf16[432,128]{1,0:T(8,128)(2,1)S(1)}, bf16[432,128]{1,0:T(8,128)(2,1)S(1)}, u32[]{:S(2)}, u32[]{:S(2)}) collective-permute-start(bf16[432,128]{1,0:T(8,128)(2,1)S(1)} %get-tuple-element.56), channel_id=1, source_target_pairs={{0,4},{2,6},{4,0},{6,2},{1,5},{3,7},{5,1},{7,3},{8,12},{10,14},{12... | collective-permute-start | bytes 331784 | tf_op jit(solution)/shard_map/ppermute | solution.py:311
  100.8 8.0 %collective-permute-start.7 = (bf16[432,128]{1,0:T(8,128)(2,1)S(1)}, bf16[432,128]{1,0:T(8,128)(2,1)S(1)}, u32[]{:S(2)}, u32[]{:S(2)}) collective-permute-start(bf16[432,128]{1,0:T(8,128)(2,1)S(1)} %get-tuple-element.57), channel_id=1, source_target_pairs={{0,6},{2,0},{4,2},{6,4},{1,7},{3,1},{5,3},{7,5},{8,14},{10,8},{12,... | collective-permute-start | bytes 331784 | tf_op jit(solution)/shard_map/ppermute | solution.py:311
  (4 other events, 2.6 us)

commit v4 on v2

v4 whole, which is shorter than its diff:
```python
import jax
import jax.numpy as jnp
from jax import lax
from jax.experimental import pallas as pl
from jax.experimental.pallas import tpu as pltpu
from jax.sharding import Mesh
from jax.sharding import PartitionSpec as P

D = 1024
E = 2048
N = 128
HEADS_HERE = 8
P_SIZE = 64
INNER = HEADS_HERE * P_SIZE
COLS = 2 * INNER + 2 * N
CAP = 432
HEAD_PARTS = 8
BYTES = 576
WIDTH = 128
CHUNKS = ((0, 128), (128, 128), (256, 128), (384, 48))
LOW = -1e30
XBC = INNER + 2 * N
VMEM_LIMIT = 60 * 2**20
eps = 1e-05
F32 = jnp.float32
BF16 = jnp.bfloat16


def dot(a, b, contract=((1,), (0,))):
    return lax.dot_general(a, b, (contract, ((), ())), preferred_element_type=F32)


def halves(a):
    hi = a.astype(BF16)
    return hi, (a - hi.astype(F32)).astype(BF16)


def thirds(a):
    hi = a.astype(BF16)
    rest = a - hi.astype(F32)
    mid = rest.astype(BF16)
    return hi, mid, (rest - mid.astype(F32)).astype(BF16)


def dot3(a, b, contract=((1,), (0,))):
    a_hi, a_lo = halves(a)
    b_hi, b_lo = halves(b)
    return dot(a_hi, b_hi, contract) + dot(a_hi, b_lo, contract) + dot(a_lo, b_hi, contract)


def iota(shape, dim):
    return lax.broadcasted_iota(jnp.int32, shape, dim)


def spread_heads(a):
    owner = (iota((2 * HEADS_HERE, INNER), 1) // P_SIZE) == (
        iota((2 * HEADS_HERE, INNER), 0) % HEADS_HERE
    )
    hi, lo = halves(a)
    return dot(jnp.concatenate([hi, lo], axis=1), owner.astype(BF16))


def line(ref):
    return ref[...].reshape(1, ref.shape[0])


def select_kernel(flags_ref, enc_ref, packed_ref):
    flags = line(flags_ref)
    upper = (iota((BYTES, BYTES), 0) <= iota((BYTES, BYTES), 1)).astype(BF16)
    rank = dot(flags.astype(F32).astype(BF16), upper)
    place = jnp.where(flags > 0, rank.astype(jnp.int32) - 1, -1)
    hit = (iota((CAP, BYTES), 0) == place).astype(F32).astype(BF16)
    packed_ref[...] = dot(hit, enc_ref[...]).astype(BF16)


def weights_kernel(flags_ref, prob_ref, w_hi_ref, w_lo_ref, carry_ref, kept_ref, decay_ref):
    flags = line(flags_ref).astype(F32)
    prob = prob_ref[...].astype(F32).reshape(1, BYTES)
    logs = jnp.where(flags > 0, jnp.log1p(-prob), 0.0)
    before = iota((BYTES, BYTES), 1) <= iota((BYTES, BYTES), 0)
    same = iota((BYTES, BYTES), 1) == iota((BYTES, BYTES), 0)

    def column(mask, row):
        return jnp.sum(jnp.where(mask, row, 0.0), axis=1, keepdims=True)

    rank = column(before, flags)
    kept = column(before, logs)
    flag = column(same, flags)
    chance = column(same, prob)
    place = iota((BYTES, CAP), 1).astype(F32)
    hit = (place == rank - 1.0) & (flag > 0)
    kept_k = jnp.sum(jnp.where(hit, kept, 0.0), axis=0, keepdims=True)
    prob_k = jnp.sum(jnp.where(hit, chance, 0.0), axis=0, keepdims=True)
    gap = jnp.where(place < rank, kept - kept_k, LOW)
    hi, lo = halves(jnp.exp(gap) * prob_k)
    w_hi_ref[...] = hi
    w_lo_ref[...] = lo
    total = jnp.sum(logs, axis=1, keepdims=True)
    count = jnp.sum(flags, axis=1, keepdims=True)
    real = iota((1, CAP), 1).astype(F32) < count
    carry_ref[...] = jnp.exp(jnp.where(real, total - kept_k, LOW)) * prob_k
    kept_ref[...] = jnp.broadcast_to(total, (1, WIDTH))
    decay_ref[...] = jnp.exp(kept)


def log_decays(step, a_log_ref):
    return -jnp.exp(line(a_log_ref)) * step


def sum_thirds(sums, axis):
    h = HEADS_HERE
    if axis == 0:
        return sums[:h] + sums[h : 2 * h] + sums[2 * h :]
    return sums[:, :h] + sums[:, h : 2 * h] + sums[:, 2 * h :]


def project_kernel(
    rows_ref, flags_ref, pad_ref, gain_ref, w_in_ref, w_dt_ref, pad_proj_ref, pad_dt_ref, bias_ref, a_log_ref,
    xbc_ref, normed_ref, inverse_ref, step_ref, run_ref, pieces_ref, w_ref, sems,
):
    tiles = range(XBC // 256)
    copies = [
        pltpu.make_async_copy(
            w_in_ref.at[:, INNER + 256 * t : INNER + 256 * (t + 1)], w_ref.at[t], sems.at[t]
        )
        for t in tiles
    ]
    for copy in copies:
        copy.start()
    energy = jnp.zeros((CAP, WIDTH), F32)
    for i in range(HEAD_PARTS):
        wide = rows_ref[:, i * WIDTH : (i + 1) * WIDTH].astype(F32)
        energy = energy + wide * wide
    pad = line(pad_ref)
    power = jnp.sum(energy, axis=1, keepdims=True) + jnp.sum(pad * pad)
    inverse = lax.rsqrt(power / E + eps)
    inverse_ref[...] = inverse
    gain = line(gain_ref)
    for i in range(HEAD_PARTS):
        lanes = slice(i * WIDTH, (i + 1) * WIDTH)
        normed_ref[:, lanes] = (rows_ref[:, lanes].astype(F32) * inverse * gain[:, lanes]).astype(BF16)
    h = HEADS_HERE
    raw = dot(normed_ref[...], w_dt_ref[...], ((1,), (1,))) + inverse * line(pad_dt_ref) + line(bias_ref)
    soft = jnp.maximum(raw, 0.0) + jnp.log1p(jnp.exp(-jnp.abs(raw)))
    count = jnp.sum(line(flags_ref).astype(F32), axis=1, keepdims=True)
    step = jnp.where(iota((CAP, h), 0).astype(F32) < count, soft, 0.0)
    step_ref[...] = step
    split = jnp.concatenate(thirds(log_decays(step, a_log_ref)), axis=1)
    lower = (iota((CAP, CAP), 1) <= iota((CAP, CAP), 0)).astype(BF16)
    run = sum_thirds(dot(lower, split), 1)
    run_ref[...] = run
    total = run[CAP - 1 :, :]
    tail = spread_heads(jnp.exp(total - run) * step)
    pad_proj = line(pad_proj_ref)
    for t in tiles:
        copies[t].wait()
        lanes = slice(256 * t, 256 * (t + 1))
        offset = inverse * pad_proj[:, INNER + 256 * t : INNER + 256 * (t + 1)]
        xbc_ref[:, lanes] = dot(normed_ref[...], w_ref[t]) + offset
    state = dot3(xbc_ref[:, INNER : INNER + N], xbc_ref[:, :INNER] * tail, ((0,), (0,)))
    total_wide = spread_heads(jnp.broadcast_to(total, (8, h)))[0:1, :]
    spare = jnp.concatenate(
        [total_wide[:, i * WIDTH : (i + 1) * WIDTH] for i in range(INNER // WIDTH)], axis=0
    )
    parts = pieces_ref.shape[0]
    per = N // parts
    for d in range(parts):
        pieces_ref[d, :, :INNER] = state[d * per : (d + 1) * per, :]
        pieces_ref[d, 0:4, INNER:] = spare
        if per > 4:
            pieces_ref[d, 4:, INNER:] = jnp.zeros((per - 4, WIDTH), F32)


def local_kernel(
    xbc_ref, normed_ref, inverse_ref, step_ref, run_ref, w_in_ref, pad_proj_ref, a_log_ref, skip_ref,
    out_ref, silu_ref, w_ref, sems,
):
    copies = [
        pltpu.make_async_copy(w_in_ref.at[:, 256 * t : 256 * (t + 1)], w_ref.at[t], sems.at[t])
        for t in range(INNER // 256)
    ]
    for copy in copies:
        copy.start()
    split = jnp.concatenate(thirds(log_decays(step_ref[...], a_log_ref)), axis=1)
    upper = (iota((CAP, CAP), 0) <= iota((CAP, CAP), 1)).astype(BF16)
    run_t = sum_thirds(dot(split, upper, ((0,), (0,))), 0)
    state = jnp.zeros((N, INNER), F32)
    skip = spread_heads(jnp.broadcast_to(line(skip_ref), (8, HEADS_HERE)))[0:1, :]
    start_run = jnp.zeros((1, HEADS_HERE), F32)
    for start, length in CHUNKS:
        rows = slice(start, start + length)
        x = xbc_ref[rows, :INNER]
        b = xbc_ref[rows, INNER : INNER + N]
        c = xbc_ref[rows, INNER + N :]
        run = run_ref[rows, :]
        step = step_ref[rows, :]
        end_run = run[length - 1 :, :]
        scaled = (x * spread_heads(step)).astype(BF16)
        inter = dot3(c, b, ((1,), (1,)))
        lower = iota((length, length), 0) >= iota((length, length), 1)
        outs = []
        for k in range(HEADS_HERE):
            gap = run[:, k : k + 1] - run_t[k : k + 1, rows]
            w = inter * jnp.exp(jnp.where(lower, gap, LOW))
            outs.append(dot(w.astype(BF16), scaled[:, k * P_SIZE : (k + 1) * P_SIZE]))
        y = jnp.concatenate(outs, axis=1) + skip * x
        if start > 0:
            y = y + spread_heads(jnp.exp(run - start_run)) * dot3(c, state)
        out_ref[rows, :] = y
        if start + length < CAP:
            weighted = x * spread_heads(step * jnp.exp(end_run - run))
            kept = spread_heads(jnp.broadcast_to(jnp.exp(end_run - start_run), (8, HEADS_HERE)))
            state = state * kept[0:1, :] + dot3(b, weighted, ((0,), (0,)))
        start_run = end_run
    pad_proj = line(pad_proj_ref)
    for t in range(INNER // 256):
        copies[t].wait()
        lanes = slice(256 * t, 256 * (t + 1))
        gate = dot(normed_ref[...], w_ref[t]) + inverse_ref[...] * pad_proj[:, lanes]
        silu_ref[:, lanes] = gate / (1.0 + jnp.exp(-gate))


def scan_kernel(got_ref, before_ref):
    act, per, _ = got_ref.shape
    state = jnp.zeros((per, INNER), F32)
    for j in range(act):
        before_ref[j] = state
        keep = jnp.exp(got_ref[j, 0:4, INNER:])
        keep = jnp.concatenate([keep[i : i + 1, :] for i in range(INNER // WIDTH)], axis=1)
        state = state * keep + got_ref[j, :, :INNER]


def output_kernel(
    run_ref, state_ref, gain_ref, xbc_ref, local_ref, silu_ref, w_out_ref,
    out_ref, full_ref, c_ref, local_v, silu_v, w_ref, sems,
):
    copies = [
        pltpu.make_async_copy(given, held, sems.at[i])
        for i, (given, held) in enumerate(
            (
                (xbc_ref.at[:, INNER + N :], c_ref),
                (local_ref, local_v),
                (silu_ref, silu_v),
                (w_out_ref, w_ref),
            )
        )
    ]
    for copy in copies:
        copy.start()
    parts, per, _ = state_ref.shape
    for d in range(parts):
        full_ref[d * per : (d + 1) * per, :] = state_ref[d]
    decay = spread_heads(jnp.exp(run_ref[...]))
    copies[0].wait()
    carried = decay * dot3(c_ref[...], full_ref[...])
    copies[1].wait()
    copies[2].wait()
    gated = (local_v[...] + carried) * silu_v[...]
    power = jnp.mean(gated * gated, axis=1, keepdims=True)
    mixed = (gated * lax.rsqrt(power + eps) * line(gain_ref)).astype(BF16)
    copies[3].wait()
    for i in range(HEAD_PARTS // 2):
        pair = dot(mixed, w_ref[:, i * 2 * WIDTH : (i + 1) * 2 * WIDTH]).astype(BF16)
        out_ref[2 * i] = pair[:, :WIDTH]
        out_ref[2 * i + 1] = pair[:, WIDTH:]


def main_kernel(packed_ref, parts_ref, carry_ref, kept_ref, main_ref, sent_ref):
    summed = packed_ref[...].astype(F32)
    added = parts_ref[0].astype(F32)
    for i in range(1, HEAD_PARTS):
        added = added + parts_ref[i].astype(F32)
    main = (summed + added).astype(BF16)
    main_ref[...] = main
    split = jnp.concatenate([jnp.broadcast_to(p, (8, CAP)) for p in thirds(carry_ref[...])], axis=0)
    sums = dot(split, main)
    carry = sums[0:1] + sums[8:9] + sums[16:17]
    row = jnp.concatenate([carry, kept_ref[...]], axis=0)
    sent_ref[...] = jnp.broadcast_to(row[None], sent_ref.shape)


def decode_kernel(enc_ref, w_hi_ref, w_lo_ref, main_ref, decay_ref, carries_ref, out_ref):
    me = lax.axis_index("act")
    act = carries_ref.shape[0]
    carry = jnp.zeros((1, WIDTH), F32)
    for j in range(act):
        after = carry * jnp.exp(carries_ref[j, 1:2, :]) + carries_ref[j, 0:1, :]
        carry = jnp.where(j < me, after, carry)
    main = main_ref[...]
    smoothed = dot(w_hi_ref[...], main) + dot(w_lo_ref[...], main) + decay_ref[...] * carry
    out_ref[...] = (enc_ref[...].astype(F32) + smoothed).astype(BF16)


def shape(dims, dtype=F32):
    return jax.ShapeDtypeStruct(dims, dtype)


def call(kernel, outs, name, specs=None, scratch=(), flops=0, transcendentals=0, nbytes=0):
    more = {} if specs is None else {"in_specs": specs}
    return pl.pallas_call(
        kernel,
        out_shape=outs,
        name=name,
        scratch_shapes=scratch,
        compiler_params=pltpu.CompilerParams(vmem_limit_bytes=VMEM_LIMIT),
        cost_estimate=pl.CostEstimate(
            flops=flops, transcendentals=transcendentals, bytes_accessed=nbytes
        ),
        **more,
    )


def body(
    enc_rows,
    boundary_flags,
    boundary_prob,
    pad_vector,
    norm_gain,
    w_in,
    w_dt,
    pad_proj,
    pad_dt,
    dt_bias,
    a_log,
    d_skip,
    gate_gain,
    w_out,
):
    act = lax.axis_size("act")
    held, apart = pl.BlockSpec(), pl.BlockSpec(memory_space=pltpu.HBM)
    packed = call(select_kernel, shape((CAP, WIDTH), BF16), "select", flops=10**8)(boundary_flags, enc_rows)
    rows = lax.all_gather(packed, "head", axis=1, tiled=True)

    w_hi, w_lo, carry_w, kept, decay = call(
        weights_kernel,
        (
            shape((BYTES, CAP), BF16),
            shape((BYTES, CAP), BF16),
            shape((1, CAP)),
            shape((1, WIDTH)),
            shape((BYTES, 1)),
        ),
        "weights",
        transcendentals=BYTES * CAP,
        flops=BYTES * CAP * 30,
        nbytes=10**6,
    )(boundary_flags, boundary_prob)

    xbc, normed, inverse, step, run, pieces = call(
        project_kernel,
        (
            shape((CAP, XBC)),
            shape((CAP, D), BF16),
            shape((CAP, 1)),
            shape((CAP, HEADS_HERE)),
            shape((CAP, HEADS_HERE)),
            shape((act, N // act, INNER + WIDTH)),
        ),
        "project",
        specs=[held] * 4 + [apart] + [held] * 5,
        scratch=[pltpu.VMEM((XBC // 256, D, 256), BF16), pltpu.SemaphoreType.DMA((XBC // 256,))],
        flops=2 * CAP * D * XBC,
        nbytes=8 * 10**6,
    )(rows, boundary_flags, pad_vector, norm_gain, w_in, w_dt.T, pad_proj, pad_dt, dt_bias, a_log)

    got = lax.all_to_all(pieces, "act", 0, 0)
    local, silu = call(
        local_kernel,
        (shape((CAP, INNER)), shape((CAP, INNER))),
        "local",
        specs=[held] * 5 + [apart] + [held] * 3,
        scratch=[pltpu.VMEM((INNER // 256, D, 256), BF16), pltpu.SemaphoreType.DMA((INNER // 256,))],
        flops=2 * 10**9,
        transcendentals=CAP * 2048,
        nbytes=6 * 10**6,
    )(xbc, normed, inverse, step, run, w_in, pad_proj, a_log, d_skip)
    before = call(scan_kernel, shape((act, N // act, INNER)), "scan", nbytes=6 * 10**5)(got)
    state_in = lax.all_to_all(before, "act", 0, 0)

    partial = call(
        output_kernel,
        shape((HEAD_PARTS, CAP, WIDTH), BF16),
        "output",
        specs=[held] * 3 + [apart] * 4,
        scratch=[
            pltpu.VMEM((N, INNER), F32),
            pltpu.VMEM((CAP, N), F32),
            pltpu.VMEM((CAP, INNER), F32),
            pltpu.VMEM((CAP, INNER), F32),
            pltpu.VMEM((INNER, D), BF16),
            pltpu.SemaphoreType.DMA((4,)),
        ],
        flops=2 * CAP * INNER * D,
        nbytes=6 * 10**6,
    )(run, state_in, gate_gain, xbc, local, silu, w_out)

    parts = lax.all_to_all(partial, "head", 0, 0)
    main, carry = call(
        main_kernel, (shape((CAP, WIDTH), BF16), shape((act, 2, WIDTH))), "main", nbytes=6 * 10**5
    )(packed, parts, carry_w, kept)
    carries = lax.all_to_all(carry, "act", 0, 0)
    return call(
        decode_kernel, shape((BYTES, WIDTH), BF16), "decode", flops=2 * 10**8, nbytes=2 * 10**6
    )(enc_rows, w_hi, w_lo, main, decay, carries)


def solution(mesh):
    seq, heads = mesh.shape["seq"], mesh.shape["head"]
    split = Mesh(mesh.devices.reshape(2, seq // 2, heads), ("half", "act", "head"))
    by_seq, by_head = ("half", "act"), "head"
    in_specs = (
        P(by_seq, by_head),
        P(by_seq),
        P(by_seq),
        P(),
        P(),
        P(None, by_head),
        P(None, by_head),
        P(by_head),
        P(by_head),
        P(by_head),
        P(by_head),
        P(by_head),
        P(by_head),
        P(by_head, None),
    )
    return jax.shard_map(
        body, mesh=split, in_specs=in_specs, out_specs=P(by_seq, by_head), check_vma=False
    )
```

time: 115 us -> 113 us (0.983)
  starting transfers between devices: 34.2 us -> 9.71 us
  blocking collectives: 38.2 us -> 56.9 us
  Pallas kernels: 12.6 us -> 28.6 us
  local copies, waits for them, and re-layouts: 13.2 us -> 1.62 us
    ppermute x8 -> x0, starting transfers between devices: 23.2 us -> none  [the longest x3 12.4 us: body(): lax.ppermute(packed, 'x', [(i, (i + s) % X_CHIPS) for i in range(X_CHIPS)])]
    all_gather x0 -> x1, blocking collectives: none -> 18 us  [body(): rows = lax.all_gather(packed, 'head', axis=1, tiled=True)]
    unnamed x43 -> x4, local copies, waits for them, and re-layouts: 11.8 us -> 1.62 us
    pallas_call x3, Pallas kernels: 8.71 us -> 17.3 us  [the longest x1 6.69 us: body(): call(local_kernel, (shape((CAP, INNER)), shape((CAP, INNER))), 'local', s...]
    all_to_all x1, waiting for transfers between devices: 5.87 us -> 9.23 us  [body(): parts = lax.all_to_all(partial, 'head', 0, 0)]
    pallas_call x1, Pallas kernels: 0.21 us -> 2.05 us  [body(): call(main_kernel, (shape((CAP, WIDTH), BF16), shape((act, 2, WIDTH))), 'm...]
    all_to_all x1, starting transfers between devices: 6.66 us -> 4.84 us  [body(): parts = lax.all_to_all(partial, 'head', 0, 0)]
    ppermute x8 -> x0, waiting for transfers between devices: 1.78 us -> none  [the longest x1 1.76 us: body(): lax.ppermute(sent, 'core', [(0, 1), (1, 0)]).astype(F32)]
  transfers between devices with their start and end apart: 10 -> 2, of which waited for: 3 -> 2; matrix products, arithmetic and copies ran while one was open for 1% -> 0% of each run, Pallas kernels for 3% -> 9%
where the time goes in v4:
time: 113 us; the launch traced here: 111 us
  blocking collectives  56.9 us (50%)
  Pallas kernels  28.6 us (25%)
  waiting for transfers between devices  14.6 us (13%)
  starting transfers between devices  9.71 us (9%)
  local copies, waits for them, and re-layouts  1.62 us (1%)
    all_to_all x1, blocking collectives, body(): got = lax.all_to_all(pieces, 'act', 0, 0)  23.8 us
    all_gather x1, blocking collectives, body(): rows = lax.all_gather(packed, 'head', axis=1, tiled=True)  18 us
    all_to_all x1, blocking collectives, body(): carries = lax.all_to_all(carry, 'act', 0, 0)  15.1 us
    all_to_all x1, waiting for transfers between devices, body(): parts = lax.all_to_all(partial, 'head', 0, 0)  9.23 us
    pallas_call x1, Pallas kernels, body(): call(local_kernel, (shape((CAP, INNER)), shape((CAP, INNER))), 'local', s...  6.69 us
    pallas_call x1, Pallas kernels, body(): call(project_kernel, (shape((CAP, XBC)), shape((CAP, D), BF16), shape((CA...  6.08 us
    all_to_all x1, waiting for transfers between devices, body(): state_in = lax.all_to_all(before, 'act', 0, 0)  5.35 us
    all_to_all x1, starting transfers between devices, body(): state_in = lax.all_to_all(before, 'act', 0, 0)  4.87 us
  transfers between devices with their start and end apart: 2, of which 2 were waited for; matrix products, arithmetic and copies ran while one was open for 0% of the time, Pallas kernels for 9%

profile of v4, /device:TPU:6, one launch (start us, length us, event | category | flops | bytes accessed | tf_op | source)
XLA Modules:
  0.0 111.5 jit_solution(7785510551006977344)
XLA Ops:
  0.0 2.1 %select.1.packed_ref = bf16[432,128]{1,0:T(8,128)(2,1)} custom-call(s32[576]{0:T(1024)} %flags_ref.5, bf16[576,128]{1,0:T(8,128)(2,1)} %enc_ref.3), custom_call_target="tpu_custom_call" | custom-call | flops 100000000 | tf_op jit(solution)/shard_map/select/pallas_call | solution.py:331
  2.1 18.0 %all_gather.3.rows_ref = bf16[432,1024]{1,0:T(8,128)(2,1)} all-gather(bf16[432,128]{1,0:T(8,128)(2,1)} %select.1.packed_ref), channel_id=1, replica_groups=mesh['half'=2,'act'=32,'head'=8] {'head'}, dimensions={1}, use_global_device_ids=true | all-gather | bytes 995328 | tf_op jit(solution)/shard_map/all_gather | solution.py:332
  20.1 6.1 %project.1 = (f32[432,768]{1,0:T(8,128)}, bf16[432,1024]{1,0:T(8,128)(2,1)}, f32[432,1]{1,0:T(8,128)}, f32[432,8]{1,0:T(8,128)}, f32[432,8]{1,0:T(8,128)}, /*index=5*/f32[32,4,640]{2,1,0:T(4,128)}) custom-call(bf16[432,1024]{1,0:T(8,128)(2,1)} %all_gather.3.rows_ref, s32[576]{0:T(1024)} %flags_ref.5, f32[1024]{0:T(1024)} %pad_ref.1, f32[1024]{0:T(1024)} %gain_ref.2, ...), custom_call_target="tpu_custom_call" | custom-call | flops 679477248 | bytes 8000000 | tf_op jit(solution)/shard_map/project/pallas_call | solution.py:349
  26.1 23.8 %all_to_all.20.got_ref = f32[32,4,640]{2,1,0:T(4,128)} all-to-all(f32[32,4,640]{2,1,0:T(4,128)} %get-tuple-element.23), channel_id=1, replica_groups=mesh['half'=2,'act'=32,'head'=8] {'act'}, dimensions={0} | all-to-all | bytes 655360 | tf_op jit(solution)/shard_map/all_to_all | solution.py:366
  50.0 1.8 %scan.1 = f32[32,4,512]{2,1,0:T(4,128)} custom-call(f32[32,4,640]{2,1,0:T(4,128)} %all_to_all.20.got_ref), custom_call_target="tpu_custom_call" | custom-call | bytes 600000 | tf_op jit(solution)/shard_map/scan/pallas_call | solution.py:377
  51.7 4.9 %all-to-all-start.1 = ((f32[32,4,512]{2,1,0:T(4,128)}), f32[32,4,512]{2,1,0:T(4,128)S(1)}, u32[]{:S(2)}, u32[]{:S(2)}) async-start(f32[32,4,512]{2,1,0:T(4,128)} %scan.1), calls=%async_computation.1 | async-start | bytes 524288 | tf_op jit(solution)/shard_map/all_to_all | solution.py:378
  56.6 6.7 %local.1 = (f32[432,512]{1,0:T(8,128)}, f32[432,512]{1,0:T(8,128)}) custom-call(f32[432,768]{1,0:T(8,128)} %get-tuple-element.24.xbc_ref, bf16[432,1024]{1,0:T(8,128)(2,1)} %get-tuple-element.25.normed_ref, f32[432,1]{1,0:T(8,128)} %get-tuple-element.26.inverse_ref, f32[432,8]{1,0:T(8,128)} %get-tuple-element.27.step_ref, ...), custom_call_target="tpu_custom_call" | custom-call | flops 2000000000 | bytes 6000000 | tf_op jit(solution)/shard_map/local/pallas_call | solution.py:367
  63.3 5.4 %all-to-all-done.1.state_ref = f32[32,4,512]{2,1,0:T(4,128)S(1)} async-done(((f32[32,4,512]{2,1,0:T(4,128)}), f32[32,4,512]{2,1,0:T(4,128)S(1)}, u32[]{:S(2)}, u32[]{:S(2)}) %all-to-all-start.1) | async-done | bytes 262176 | tf_op jit(solution)/shard_map/all_to_all | solution.py:378
  68.6 0.0 copy-start.1
  68.6 0.7 copy-done.1
  69.3 4.5 %output.1 = bf16[8,432,128]{2,1,0:T(8,128)(2,1)} custom-call(f32[432,8]{1,0:T(8,128)} %get-tuple-element.22.run_ref, f32[32,4,512]{2,1,0:T(4,128)} %copy-done.1, f32[512]{0:T(512)} %gain_ref.3, f32[432,768]{1,0:T(8,128)} %get-tuple-element.24.xbc_ref, f32[432,512]{1,0:T(8,128)} %get-tuple-element.28.local_ref, f32[432,512]{1,0:T(8,128)} %get-tuple-element.29.silu_ref, ...), custom_call_target="tpu_custom_call" | custom-call | flops 452984832 | bytes 6000000 | tf_op jit(solution)/shard_map/output/pallas_call | solution.py:380
  73.9 4.8 %all-to-all-start.2 = ((bf16[8,432,128]{2,1,0:T(8,128)(2,1)}), bf16[8,432,128]{2,1,0:T(8,128)(2,1)S(1)}, u32[]{:S(2)}, u32[]{:S(2)}) async-start(bf16[8,432,128]{2,1,0:T(8,128)(2,1)} %output.1), calls=%async_computation.2 | async-start | bytes 1769472 | tf_op jit(solution)/shard_map/all_to_all | solution.py:397
  78.7 2.9 %weights.1 = (bf16[576,432]{1,0:T(8,128)(2,1)}, bf16[576,432]{1,0:T(8,128)(2,1)}, f32[1,432]{1,0:T(1,128)}, f32[1,128]{1,0:T(1,128)}, f32[576,1]{1,0:T(8,128)}) custom-call(s32[576]{0:T(1024)} %flags_ref.5, bf16[576]{0:T(1024)(128)(2,1)} %prob_ref.1), custom_call_target="tpu_custom_call" | custom-call | flops 7464960 | bytes 1000000 | tf_op jit(solution)/shard_map/weights/pallas_call | solution.py:334
  81.6 9.2 %all-to-all-done.2.parts_ref = bf16[8,432,128]{2,1,0:T(8,128)(2,1)S(1)} async-done(((bf16[8,432,128]{2,1,0:T(8,128)(2,1)}), bf16[8,432,128]{2,1,0:T(8,128)(2,1)S(1)}, u32[]{:S(2)}, u32[]{:S(2)}) %all-to-all-start.2) | async-done | bytes 884768 | tf_op jit(solution)/shard_map/all_to_all | solution.py:397
  90.8 0.0 copy-start
  90.9 0.9 copy-done
  91.8 2.0 %main.1 = (bf16[432,128]{1,0:T(8,128)(2,1)}, f32[32,2,128]{2,1,0:T(2,128)}) custom-call(bf16[432,128]{1,0:T(8,128)(2,1)} %select.1.packed_ref, bf16[8,432,128]{2,1,0:T(8,128)(2,1)} %copy-done, f32[1,432]{1,0:T(1,128)} %get-tuple-element.30.carry_ref, f32[1,128]{1,0:T(1,128)} %get-tuple-element.31.kept_ref), custom_call_target="tpu_custom_call" | custom-call | bytes 600000 | tf_op jit(solution)/shard_map/main/pallas_call | solution.py:398
  93.8 15.1 %all_to_all.21.carries_ref = f32[32,2,128]{2,1,0:T(2,128)} all-to-all(f32[32,2,128]{2,1,0:T(2,128)} %get-tuple-element.34), channel_id=1, replica_groups=mesh['half'=2,'act'=32,'head'=8] {'act'}, dimensions={0} | all-to-all | bytes 65536 | tf_op jit(solution)/shard_map/all_to_all | solution.py:401
  108.9 2.5 %decode.1 = bf16[576,128]{1,0:T(8,128)(2,1)} custom-call(bf16[576,128]{1,0:T(8,128)(2,1)} %enc_ref.3, bf16[576,432]{1,0:T(8,128)(2,1)} %get-tuple-element.20.w_hi_ref, bf16[576,432]{1,0:T(8,128)(2,1)} %get-tuple-element.21.w_lo_ref, bf16[432,128]{1,0:T(8,128)(2,1)} %get-tuple-element.32.main_ref, f32[576,1]{1,0:T(8,128)} %get-tuple-element.33.decay_ref, ...), custom_call_target="tpu_custom_call" | custom-call | flops 200000000 | bytes 2000000 | tf_op jit(solution)/shard_map/decode/pallas_call | solution.py:402
Async XLA Ops:
  51.7 16.9 %all-to-all-start.1 = ((f32[32,4,512]{2,1,0:T(4,128)}), f32[32,4,512]{2,1,0:T(4,128)S(1)}, u32[]{:S(2)}, u32[]{:S(2)}) async-start(f32[32,4,512]{2,1,0:T(4,128)} %scan.1), calls=%async_computation.1 | async-start | bytes 524288 | tf_op jit(solution)/shard_map/all_to_all | solution.py:378
  68.6 0.7 copy-start.1
  73.9 17.0 %all-to-all-start.2 = ((bf16[8,432,128]{2,1,0:T(8,128)(2,1)}), bf16[8,432,128]{2,1,0:T(8,128)(2,1)S(1)}, u32[]{:S(2)}, u32[]{:S(2)}) async-start(bf16[8,432,128]{2,1,0:T(8,128)(2,1)} %output.1), calls=%async_computation.2 | async-start | bytes 1769472 | tf_op jit(solution)/shard_map/all_to_all | solution.py:397
  90.8 0.9 copy-start

commit v5 on v4

--- a/solution.py
+++ b/solution.py
@@ -20,7 +20,7 @@
 CHUNKS = ((0, 128), (128, 128), (256, 128), (384, 48))
 LOW = -1e30
 XBC = INNER + 2 * N
-VMEM_LIMIT = 60 * 2**20
+VMEM_LIMIT = 24 * 2**20
 eps = 1e-05
 F32 = jnp.float32
 BF16 = jnp.bfloat16
@@ -64,7 +64,21 @@
     return ref[...].reshape(1, ref.shape[0])
 
 
-def select_kernel(flags_ref, enc_ref, packed_ref):
+def fetch(given, held, sems):
+    copies = [pltpu.make_async_copy(a, b, sems.at[i]) for i, (a, b) in enumerate(zip(given, held))]
+    for copy in copies:
+        copy.start()
+    return copies
+
+
+def arrived(copies):
+    for copy in copies:
+        copy.wait()
+
+
+def select_kernel(flags_hbm, enc_hbm, packed_ref, flags_ref, enc_ref, sems):
+    copies = fetch((flags_hbm, enc_hbm), (flags_ref, enc_ref), sems)
+    arrived(copies)
     flags = line(flags_ref)
     upper = (iota((BYTES, BYTES), 0) <= iota((BYTES, BYTES), 1)).astype(BF16)
     rank = dot(flags.astype(F32).astype(BF16), upper)
@@ -115,9 +129,13 @@
 
 
 def project_kernel(
-    rows_ref, flags_ref, pad_ref, gain_ref, w_in_ref, w_dt_ref, pad_proj_ref, pad_dt_ref, bias_ref, a_log_ref,
-    xbc_ref, normed_ref, inverse_ref, step_ref, run_ref, pieces_ref, w_ref, sems,
+    rows_ref, w_in_ref, *refs,
 ):
+    given, refs = refs[:8], refs[8:]
+    (xbc_ref, normed_ref, inverse_ref, step_ref, run_ref, pieces_ref), refs = refs[:6], refs[6:]
+    held, (w_ref, sems, small_sems) = refs[:8], refs[8:]
+    flags_ref, pad_ref, gain_ref, w_dt_ref, pad_proj_ref, pad_dt_ref, bias_ref, a_log_ref = held
+    small = fetch(given, held, small_sems)
     tiles = range(XBC // 256)
     copies = [
         pltpu.make_async_copy(
@@ -131,6 +149,7 @@
     for i in range(HEAD_PARTS):
         wide = rows_ref[:, i * WIDTH : (i + 1) * WIDTH].astype(F32)
         energy = energy + wide * wide
+    arrived(small)
     pad = line(pad_ref)
     power = jnp.sum(energy, axis=1, keepdims=True) + jnp.sum(pad * pad)
     inverse = lax.rsqrt(power / E + eps)
@@ -171,16 +190,14 @@
             pieces_ref[d, 4:, INNER:] = jnp.zeros((per - 4, WIDTH), F32)
 
 
-def local_kernel(
-    xbc_ref, normed_ref, inverse_ref, step_ref, run_ref, w_in_ref, pad_proj_ref, a_log_ref, skip_ref,
-    out_ref, silu_ref, w_ref, sems,
-):
-    copies = [
-        pltpu.make_async_copy(w_in_ref.at[:, 256 * t : 256 * (t + 1)], w_ref.at[t], sems.at[t])
-        for t in range(INNER // 256)
-    ]
-    for copy in copies:
-        copy.start()
+def local_kernel(*refs):
+    given, w_in_ref, (out_ref, silu_ref), held, (w_ref, sems) = refs[:8], refs[8], refs[9:11], refs[11:19], refs[19:]
+    xbc_ref, normed_ref, inverse_ref, step_ref, run_ref, pad_proj_ref, a_log_ref, skip_ref = held
+    tiles = range(INNER // 256)
+    pieces = [w_in_ref.at[:, 256 * t : 256 * (t + 1)] for t in tiles]
+    copies = fetch(given + tuple(pieces), held + tuple(w_ref.at[t] for t in tiles), sems)
+    arrived(copies[:8])
+    copies = copies[8:]
     split = jnp.concatenate(thirds(log_decays(step_ref[...], a_log_ref)), axis=1)
     upper = (iota((CAP, CAP), 0) <= iota((CAP, CAP), 1)).astype(BF16)
     run_t = sum_thirds(dot(split, upper, ((0,), (0,))), 0)
@@ -206,7 +223,7 @@
         y = jnp.concatenate(outs, axis=1) + skip * x
         if start > 0:
             y = y + spread_heads(jnp.exp(run - start_run)) * dot3(c, state)
-        out_ref[rows, :] = y
+        out_ref[rows, :] = y.astype(BF16)
         if start + length < CAP:
             weighted = x * spread_heads(step * jnp.exp(end_run - run))
             kept = spread_heads(jnp.broadcast_to(jnp.exp(end_run - start_run), (8, HEADS_HERE)))
@@ -217,7 +234,7 @@
         copies[t].wait()
         lanes = slice(256 * t, 256 * (t + 1))
         gate = dot(normed_ref[...], w_ref[t]) + inverse_ref[...] * pad_proj[:, lanes]
-        silu_ref[:, lanes] = gate / (1.0 + jnp.exp(-gate))
+        silu_ref[:, lanes] = (gate / (1.0 + jnp.exp(-gate))).astype(BF16)
 
 
 def scan_kernel(got_ref, before_ref):
@@ -231,34 +248,24 @@
 
 
 def output_kernel(
-    run_ref, state_ref, gain_ref, xbc_ref, local_ref, silu_ref, w_out_ref,
-    out_ref, full_ref, c_ref, local_v, silu_v, w_ref, sems,
+    state_ref, c_hbm, run_hbm, local_hbm, silu_hbm, gain_hbm, w_out_hbm,
+    out_ref, full_ref, c_ref, run_ref, local_ref, silu_ref, gain_ref, w_ref, sems,
 ):
-    copies = [
-        pltpu.make_async_copy(given, held, sems.at[i])
-        for i, (given, held) in enumerate(
-            (
-                (xbc_ref.at[:, INNER + N :], c_ref),
-                (local_ref, local_v),
-                (silu_ref, silu_v),
-                (w_out_ref, w_ref),
-            )
-        )
-    ]
-    for copy in copies:
-        copy.start()
+    copies = fetch(
+        (c_hbm.at[:, INNER + N :], run_hbm, local_hbm, silu_hbm, gain_hbm, w_out_hbm),
+        (c_ref, run_ref, local_ref, silu_ref, gain_ref, w_ref),
+        sems,
+    )
     parts, per, _ = state_ref.shape
     for d in range(parts):
         full_ref[d * per : (d + 1) * per, :] = state_ref[d]
-    decay = spread_heads(jnp.exp(run_ref[...]))
-    copies[0].wait()
-    carried = decay * dot3(c_ref[...], full_ref[...])
-    copies[1].wait()
-    copies[2].wait()
-    gated = (local_v[...] + carried) * silu_v[...]
+    arrived(copies[:2])
+    carried = spread_heads(jnp.exp(run_ref[...])) * dot3(c_ref[...], full_ref[...])
+    arrived(copies[2:5])
+    gated = (local_ref[...].astype(F32) + carried) * silu_ref[...].astype(F32)
     power = jnp.mean(gated * gated, axis=1, keepdims=True)
     mixed = (gated * lax.rsqrt(power + eps) * line(gain_ref)).astype(BF16)
-    copies[3].wait()
+    arrived(copies[5:])
     for i in range(HEAD_PARTS // 2):
         pair = dot(mixed, w_ref[:, i * 2 * WIDTH : (i + 1) * 2 * WIDTH]).astype(BF16)
         out_ref[2 * i] = pair[:, :WIDTH]
@@ -279,7 +286,8 @@
     sent_ref[...] = jnp.broadcast_to(row[None], sent_ref.shape)
 
 
-def decode_kernel(enc_ref, w_hi_ref, w_lo_ref, main_ref, decay_ref, carries_ref, out_ref):
+def decode_kernel(enc_hbm, w_hi_ref, w_lo_ref, main_ref, decay_ref, carries_ref, out_ref, enc_ref, sems):
+    copies = fetch((enc_hbm,), (enc_ref,), sems)
     me = lax.axis_index("act")
     act = carries_ref.shape[0]
     carry = jnp.zeros((1, WIDTH), F32)
@@ -288,6 +296,7 @@
         carry = jnp.where(j < me, after, carry)
     main = main_ref[...]
     smoothed = dot(w_hi_ref[...], main) + dot(w_lo_ref[...], main) + decay_ref[...] * carry
+    arrived(copies)
     out_ref[...] = (enc_ref[...].astype(F32) + smoothed).astype(BF16)
 
 
@@ -297,7 +306,7 @@
 
 def call(kernel, outs, name, specs=None, scratch=(), flops=0, transcendentals=0, nbytes=0):
     more = {} if specs is None else {"in_specs": specs}
-    return pl.pallas_call(
+    run = pl.pallas_call(
         kernel,
         out_shape=outs,
         name=name,
@@ -307,6 +316,14 @@
             flops=flops, transcendentals=transcendentals, bytes_accessed=nbytes
         ),
         **more,
+    )
+    if specs is None:
+        return run
+    return lambda *args: run(
+        *[
+            pltpu.with_memory_space_constraint(a, pltpu.HBM) if spec.memory_space == pltpu.HBM else a
+            for a, spec in zip(args, specs)
+        ]
     )
 
 
@@ -328,7 +345,15 @@
 ):
     act = lax.axis_size("act")
     held, apart = pl.BlockSpec(), pl.BlockSpec(memory_space=pltpu.HBM)
-    packed = call(select_kernel, shape((CAP, WIDTH), BF16), "select", flops=10**8)(boundary_flags, enc_rows)
+    dma = pltpu.SemaphoreType.DMA
+    packed = call(
+        select_kernel,
+        shape((CAP, WIDTH), BF16),
+        "select",
+        specs=[apart] * 2,
+        scratch=[pltpu.VMEM((BYTES,), jnp.int32), pltpu.VMEM((BYTES, WIDTH), BF16), dma((2,))],
+        flops=10**8,
+    )(boundary_flags, enc_rows)
     rows = lax.all_gather(packed, "head", axis=1, tiled=True)
 
     w_hi, w_lo, carry_w, kept, decay = call(
@@ -346,6 +371,7 @@
         nbytes=10**6,
     )(boundary_flags, boundary_prob)
 
+    small = [boundary_flags, pad_vector, norm_gain, w_dt.T, pad_proj, pad_dt, dt_bias, a_log]
     xbc, normed, inverse, step, run, pieces = call(
         project_kernel,
         (
@@ -357,23 +383,26 @@
             shape((act, N // act, INNER + WIDTH)),
         ),
         "project",
-        specs=[held] * 4 + [apart] + [held] * 5,
-        scratch=[pltpu.VMEM((XBC // 256, D, 256), BF16), pltpu.SemaphoreType.DMA((XBC // 256,))],
+        specs=[held] + [apart] * (1 + len(small)),
+        scratch=[pltpu.VMEM(a.shape, a.dtype) for a in small]
+        + [pltpu.VMEM((XBC // 256, D, 256), BF16), dma((XBC // 256,)), dma((len(small),))],
         flops=2 * CAP * D * XBC,
         nbytes=8 * 10**6,
-    )(rows, boundary_flags, pad_vector, norm_gain, w_in, w_dt.T, pad_proj, pad_dt, dt_bias, a_log)
+    )(rows, w_in, *small)
 
     got = lax.all_to_all(pieces, "act", 0, 0)
+    needed = [xbc, normed, inverse, step, run, pad_proj, a_log, d_skip]
     local, silu = call(
         local_kernel,
-        (shape((CAP, INNER)), shape((CAP, INNER))),
+        (shape((CAP, INNER), BF16), shape((CAP, INNER), BF16)),
         "local",
-        specs=[held] * 5 + [apart] + [held] * 3,
-        scratch=[pltpu.VMEM((INNER // 256, D, 256), BF16), pltpu.SemaphoreType.DMA((INNER // 256,))],
+        specs=[apart] * (len(needed) + 1),
+        scratch=[pltpu.VMEM(a.shape, a.dtype) for a in needed]
+        + [pltpu.VMEM((INNER // 256, D, 256), BF16), dma((len(needed) + INNER // 256,))],
         flops=2 * 10**9,
         transcendentals=CAP * 2048,
         nbytes=6 * 10**6,
-    )(xbc, normed, inverse, step, run, w_in, pad_proj, a_log, d_skip)
+    )(*needed, w_in)
     before = call(scan_kernel, shape((act, N // act, INNER)), "scan", nbytes=6 * 10**5)(got)
     state_in = lax.all_to_all(before, "act", 0, 0)
 
@@ -381,18 +410,20 @@
         output_kernel,
         shape((HEAD_PARTS, CAP, WIDTH), BF16),
         "output",
-        specs=[held] * 3 + [apart] * 4,
+        specs=[held] + [apart] * 6,
         scratch=[
             pltpu.VMEM((N, INNER), F32),
             pltpu.VMEM((CAP, N), F32),
-            pltpu.VMEM((CAP, INNER), F32),
-            pltpu.VMEM((CAP, INNER), F32),
+            pltpu.VMEM((CAP, HEADS_HERE), F32),
+            pltpu.VMEM((CAP, INNER), BF16),
+            pltpu.VMEM((CAP, INNER), BF16),
+            pltpu.VMEM((INNER,), F32),
             pltpu.VMEM((INNER, D), BF16),
-            pltpu.SemaphoreType.DMA((4,)),
+            dma((6,)),
         ],
         flops=2 * CAP * INNER * D,
         nbytes=6 * 10**6,
-    )(run, state_in, gate_gain, xbc, local, silu, w_out)
+    )(state_in, xbc, run, local, silu, gate_gain, w_out)
 
     parts = lax.all_to_all(partial, "head", 0, 0)
     main, carry = call(
@@ -400,7 +431,13 @@
     )(packed, parts, carry_w, kept)
     carries = lax.all_to_all(carry, "act", 0, 0)
     return call(
-        decode_kernel, shape((BYTES, WIDTH), BF16), "decode", flops=2 * 10**8, nbytes=2 * 10**6
+        decode_kernel,
+        shape((BYTES, WIDTH), BF16),
+        "decode",
+        specs=[apart] + [held] * 5,
+        scratch=[pltpu.VMEM((BYTES, WIDTH), BF16), dma((1,))],
+        flops=2 * 10**8,
+        nbytes=2 * 10**6,
     )(enc_rows, w_hi, w_lo, main, decay, carries)
 
 

time: 113 us -> 107 us (0.947)
  Pallas kernels: 28.6 us -> 20.1 us
  local copies, waits for them, and re-layouts: 1.62 us -> 4.23 us
    pallas_call x5, Pallas kernels: 21.9 us -> 17.8 us  [call(): run(*[pltpu.with_memory_space_constraint(a, pltpu.HBM) if spec.memory_spa...]
    unnamed x4 -> x18, local copies, waits for them, and re-layouts: 1.62 us -> 4.23 us
    pallas_call x1, Pallas kernels: 2.05 us -> 0.27 us  [body(): call(main_kernel, (shape((CAP, WIDTH), BF16), shape((act, 2, WIDTH))), 'm...]
    pallas_call x1, Pallas kernels: 2.92 us -> 1.23 us  [body(): call(weights_kernel, (shape((BYTES, CAP), BF16), shape((BYTES, CAP), BF16...]
    all_to_all x1, waiting for transfers between devices: 9.23 us -> 10.9 us  [body(): parts = lax.all_to_all(partial, 'head', 0, 0)]
    all_gather x1, blocking collectives: 18 us -> 16.7 us  [body(): rows = lax.all_gather(packed, 'head', axis=1, tiled=True)]
  transfers between devices with their start and end apart: 2 -> 2, of which waited for: 2 -> 2; matrix products, arithmetic and copies ran while one was open for 0% -> 0% of each run, Pallas kernels for 9% -> 7%
where the time goes in v5:
time: 107 us; the launch traced here: 106 us
  blocking collectives  56 us (52%)
  Pallas kernels  20.1 us (19%)
  waiting for transfers between devices  15.6 us (15%)
  starting transfers between devices  9.67 us (9%)
  local copies, waits for them, and re-layouts  4.23 us (4%)
    all_to_all x1, blocking collectives, body(): got = lax.all_to_all(pieces, 'act', 0, 0)  23.8 us
    pallas_call x5, Pallas kernels, call(): run(*[pltpu.with_memory_space_constraint(a, pltpu.HBM) if spec.memory_spa...  17.8 us
    all_gather x1, blocking collectives, body(): rows = lax.all_gather(packed, 'head', axis=1, tiled=True)  16.7 us
    all_to_all x1, blocking collectives, body(): carries = lax.all_to_all(carry, 'act', 0, 0)  15.5 us
    all_to_all x1, waiting for transfers between devices, body(): parts = lax.all_to_all(partial, 'head', 0, 0)  10.9 us
    all_to_all x1, starting transfers between devices, body(): state_in = lax.all_to_all(before, 'act', 0, 0)  4.87 us
    all_to_all x1, starting transfers between devices, body(): parts = lax.all_to_all(partial, 'head', 0, 0)  4.8 us
    all_to_all x1, waiting for transfers between devices, body(): state_in = lax.all_to_all(before, 'act', 0, 0)  4.67 us
  transfers between devices with their start and end apart: 2, of which 2 were waited for; matrix products, arithmetic and copies ran while one was open for 0% of the time, Pallas kernels for 7%

profile of v5, /device:TPU:6, one launch (start us, length us, event | category | flops | bytes accessed | tf_op | source)
XLA Modules:
  0.0 105.6 jit_solution(679088242404198778)
XLA Ops:
  0.0 1.5 %select.1.packed_ref = bf16[432,128]{1,0:T(8,128)(2,1)S(1)} custom-call(s32[576]{0:T(1024)} %refs_0_.1, bf16[576,128]{1,0:T(8,128)(2,1)} %enc_hbm.3), custom_call_target="tpu_custom_call" | custom-call | flops 100000000 | tf_op jit(solution)/shard_map/select/pallas_call | solution.py:322
  1.5 16.7 %all_gather.3.rows_ref = bf16[432,1024]{1,0:T(8,128)(2,1)S(1)} all-gather(bf16[432,128]{1,0:T(8,128)(2,1)S(1)} %select.1.packed_ref), channel_id=1, replica_groups=mesh['half'=2,'act'=32,'head'=8] {'head'}, dimensions={1}, use_global_device_ids=true | all-gather | bytes 995328 | tf_op jit(solution)/shard_map/all_gather | solution.py:357
  18.2 4.9 %project.1 = (f32[432,768]{1,0:T(8,128)S(1)}, bf16[432,1024]{1,0:T(8,128)(2,1)S(1)}, f32[432,1]{1,0:T(8,128)S(1)}, f32[432,8]{1,0:T(8,128)S(1)}, f32[432,8]{1,0:T(8,128)S(1)}, /*index=5*/f32[32,4,640]{2,1,0:T(4,128)S(1)}) custom-call(bf16[432,1024]{1,0:T(8,128)(2,1)S(1)} %all_gather.3.rows_ref, bf16[1024,1280]{1,0:T(8,128)(2,1)} %refs_8_.1, s32[576]{0:T(1024)} %refs_0_.1, ...), custom_call_target="tpu_custom_call" | custom-call | flops 679477248 | bytes 8000000 | tf_op jit(solution)/shard_map/project/pallas_call | solution.py:322
  23.1 0.0 copy-start
  23.1 1.1 %copy-done = f32[432,768]{1,0:T(8,128)} copy-done((f32[432,768]{1,0:T(8,128)}, f32[432,768]{1,0:T(8,128)S(1)}, u32[]{:S(2)}) %copy-start) | copy-done | bytes 1327128
  24.2 0.9 copy-done.5
  25.1 0.0 copy-start.7
  25.1 0.7 copy-done.7
  25.8 0.0 copy-start.3
  25.8 0.0 copy-start.6
  25.8 23.8 %all_to_all.20.got_ref = f32[32,4,640]{2,1,0:T(4,128)S(1)} all-to-all(f32[32,4,640]{2,1,0:T(4,128)S(1)} %get-tuple-element.22), channel_id=1, replica_groups=mesh['half'=2,'act'=32,'head'=8] {'act'}, dimensions={0} | all-to-all | bytes 655360 | tf_op jit(solution)/shard_map/all_to_all | solution.py:393
  49.6 0.0 copy-done.3
  49.6 0.0 copy-done.6
  49.6 0.8 scan.1
  50.4 4.9 %all-to-all-start.1 = ((f32[32,4,512]{2,1,0:T(4,128)}), f32[32,4,512]{2,1,0:T(4,128)S(1)}, u32[]{:S(2)}, u32[]{:S(2)}) async-start(f32[32,4,512]{2,1,0:T(4,128)} %scan.1), calls=%async_computation.1 | async-start | bytes 524288 | tf_op jit(solution)/shard_map/all_to_all | solution.py:407
  55.3 5.8 %local.1 = (bf16[432,512]{1,0:T(8,128)(2,1)S(1)}, bf16[432,512]{1,0:T(8,128)(2,1)S(1)}) custom-call(f32[432,768]{1,0:T(8,128)} %copy-done, bf16[432,1024]{1,0:T(8,128)(2,1)} %copy-done.5, f32[432,1]{1,0:T(8,128)} %copy-done.6, f32[432,8]{1,0:T(8,128)} %copy-done.7, f32[432,8]{1,0:T(8,128)} %copy-done.3, f32[1280]{0:T(1024)} %refs_5_.3, f32[8]{0:T(128)} %refs_6_.3, ...), custom_call_target="tpu_custom_call" | custom-call | flops 2000000000 | bytes 6000000 | tf_op jit(solution)/shard_map/local/pallas_call | solution.py:322
  61.1 0.0 copy-start.1
  61.1 0.8 copy-done.1
  61.9 0.0 copy-start.2
  61.9 0.8 copy-done.2
  62.6 4.7 %all-to-all-done.1.state_ref = f32[32,4,512]{2,1,0:T(4,128)S(1)} async-done(((f32[32,4,512]{2,1,0:T(4,128)}), f32[32,4,512]{2,1,0:T(4,128)S(1)}, u32[]{:S(2)}, u32[]{:S(2)}) %all-to-all-start.1) | async-done | bytes 262176 | tf_op jit(solution)/shard_map/all_to_all | solution.py:407
  67.3 0.0 copy-start.4
  67.3 0.0 copy-start.8
  67.3 3.6 %output.1 = bf16[8,432,128]{2,1,0:T(8,128)(2,1)} custom-call(f32[32,4,512]{2,1,0:T(4,128)S(1)} %all-to-all-done.1.state_ref, f32[432,768]{1,0:T(8,128)} %copy-done, f32[432,8]{1,0:T(8,128)} %copy-done.3, bf16[432,512]{1,0:T(8,128)(2,1)} %copy-done.1, bf16[432,512]{1,0:T(8,128)(2,1)} %copy-done.2, f32[512]{0:T(512)} %gain_hbm.1, bf16[512,1024]{1,0:T(8,128)(2,1)} %w_out_hbm.1), custom_call_target="tpu_custom_call" | custom-call | flops 452984832 | bytes 6000000 | tf_op jit(solution)/shard_map/output/pallas_call | solution.py:322
  71.0 4.8 %all-to-all-start.2 = ((bf16[8,432,128]{2,1,0:T(8,128)(2,1)}), bf16[8,432,128]{2,1,0:T(8,128)(2,1)S(1)}, u32[]{:S(2)}, u32[]{:S(2)}) async-start(bf16[8,432,128]{2,1,0:T(8,128)(2,1)} %output.1), calls=%async_computation.2 | async-start | bytes 1769472 | tf_op jit(solution)/shard_map/all_to_all | solution.py:428
  75.8 0.0 copy-done.4
  75.8 0.0 copy-done.8
  75.8 1.2 %weights.1 = (bf16[576,432]{1,0:T(8,128)(2,1)S(1)}, bf16[576,432]{1,0:T(8,128)(2,1)S(1)}, f32[1,432]{1,0:T(1,128)S(1)}, f32[1,128]{1,0:T(1,128)S(1)}, f32[576,1]{1,0:T(8,128)S(1)}) custom-call(s32[576]{0:T(1024)S(1)} %copy-done.4, bf16[576]{0:T(1024)(128)(2,1)S(1)} %copy-done.8), custom_call_target="tpu_custom_call" | custom-call | flops 7464960 | bytes 1000000 | tf_op jit(solution)/shard_map/weights/pallas_call | solution.py:359
  77.0 10.9 %all-to-all-done.2.parts_ref = bf16[8,432,128]{2,1,0:T(8,128)(2,1)S(1)} async-done(((bf16[8,432,128]{2,1,0:T(8,128)(2,1)}), bf16[8,432,128]{2,1,0:T(8,128)(2,1)S(1)}, u32[]{:S(2)}, u32[]{:S(2)}) %all-to-all-start.2) | async-done | bytes 884768 | tf_op jit(solution)/shard_map/all_to_all | solution.py:428
  87.9 0.3 main.1
  88.2 15.5 %all_to_all.21.carries_ref = f32[32,2,128]{2,1,0:T(2,128)S(1)} all-to-all(f32[32,2,128]{2,1,0:T(2,128)S(1)} %get-tuple-element.34), channel_id=1, replica_groups=mesh['half'=2,'act'=32,'head'=8] {'act'}, dimensions={0} | all-to-all | bytes 65536 | tf_op jit(solution)/shard_map/all_to_all | solution.py:432
  103.6 2.0 %decode.1 = bf16[576,128]{1,0:T(8,128)(2,1)} custom-call(bf16[576,128]{1,0:T(8,128)(2,1)} %enc_hbm.3, bf16[576,432]{1,0:T(8,128)(2,1)S(1)} %get-tuple-element.20.w_hi_ref, bf16[576,432]{1,0:T(8,128)(2,1)S(1)} %get-tuple-element.21.w_lo_ref, bf16[432,128]{1,0:T(8,128)(2,1)S(1)} %get-tuple-element.32.main_ref, f32[576,1]{1,0:T(8,128)S(1)} %get-tuple-element.33.decay_ref, ...), custom_call_target="tpu_custom_call" | custom-call | flops 200000000 | bytes 2000000 | tf_op jit(solution)/shard_map/decode/pallas_call | solution.py:322
  (1 shorter events, 0.0 us)
Async XLA Ops:
  23.1 1.1 %copy-start = (f32[432,768]{1,0:T(8,128)}, f32[432,768]{1,0:T(8,128)S(1)}, u32[]{:S(2)}) copy-start(f32[432,768]{1,0:T(8,128)S(1)} %get-tuple-element.23.refs_0_.c_hbm) | copy-start | bytes 3981316
  24.1 0.9 copy-start.5
  25.1 0.7 copy-start.7
  25.8 23.8 %copy-start.3 = (f32[432,8]{1,0:T(8,128)}, f32[432,8]{1,0:T(8,128)S(1)}, u32[]{:S(2)}) copy-start(f32[432,8]{1,0:T(8,128)S(1)} %get-tuple-element.24.refs_4_.run_hbm) | copy-start | bytes 41476
  25.8 23.8 %copy-start.6 = (f32[432,1]{1,0:T(8,128)}, f32[432,1]{1,0:T(8,128)S(1)}, u32[]{:S(2)}) copy-start(f32[432,1]{1,0:T(8,128)S(1)} %get-tuple-element.26.refs_2_) | copy-start | bytes 5188
  50.4 16.9 %all-to-all-start.1 = ((f32[32,4,512]{2,1,0:T(4,128)}), f32[32,4,512]{2,1,0:T(4,128)S(1)}, u32[]{:S(2)}, u32[]{:S(2)}) async-start(f32[32,4,512]{2,1,0:T(4,128)} %scan.1), calls=%async_computation.1 | async-start | bytes 524288 | tf_op jit(solution)/shard_map/all_to_all | solution.py:407
  61.1 0.8 copy-start.1
  61.9 0.8 copy-start.2
  67.3 8.5 %copy-start.4 = (s32[576]{0:T(1024)S(1)}, s32[576]{0:T(1024)}, u32[]{:S(2)}) copy-start(s32[576]{0:T(1024)} %refs_0_.1) | copy-start | bytes 6916
  67.3 8.5 %copy-start.8 = (bf16[576]{0:T(1024)(128)(2,1)S(1)}, bf16[576]{0:T(1024)(128)(2,1)}, u32[]{:S(2)}) copy-start(bf16[576]{0:T(1024)(128)(2,1)} %prob_ref.1) | copy-start | bytes 3460
  71.0 16.9 %all-to-all-start.2 = ((bf16[8,432,128]{2,1,0:T(8,128)(2,1)}), bf16[8,432,128]{2,1,0:T(8,128)(2,1)S(1)}, u32[]{:S(2)}, u32[]{:S(2)}) async-start(bf16[8,432,128]{2,1,0:T(8,128)(2,1)} %output.1), calls=%async_computation.2 | async-start | bytes 1769472 | tf_op jit(solution)/shard_map/all_to_all | solution.py:428

commit v6 on v5

--- a/solution.py
+++ b/solution.py
@@ -64,8 +64,10 @@
     return ref[...].reshape(1, ref.shape[0])
 
 
-def fetch(given, held, sems):
-    copies = [pltpu.make_async_copy(a, b, sems.at[i]) for i, (a, b) in enumerate(zip(given, held))]
+def fetch(given, held, sems, first=0):
+    copies = [
+        pltpu.make_async_copy(a, b, sems.at[first + i]) for i, (a, b) in enumerate(zip(given, held))
+    ]
     for copy in copies:
         copy.start()
     return copies
@@ -132,8 +134,8 @@
     rows_ref, w_in_ref, *refs,
 ):
     given, refs = refs[:8], refs[8:]
-    (xbc_ref, normed_ref, inverse_ref, step_ref, run_ref, pieces_ref), refs = refs[:6], refs[6:]
-    held, (w_ref, sems, small_sems) = refs[:8], refs[8:]
+    (xbc_hbm, normed_hbm, aux_hbm, pieces_ref), refs = refs[:4], refs[4:]
+    held, (xbc_ref, normed_ref, aux_ref, w_ref, sems, small_sems, out_sems) = refs[:8], refs[8:]
     flags_ref, pad_ref, gain_ref, w_dt_ref, pad_proj_ref, pad_dt_ref, bias_ref, a_log_ref = held
     small = fetch(given, held, small_sems)
     tiles = range(XBC // 256)
@@ -153,21 +155,22 @@
     pad = line(pad_ref)
     power = jnp.sum(energy, axis=1, keepdims=True) + jnp.sum(pad * pad)
     inverse = lax.rsqrt(power / E + eps)
-    inverse_ref[...] = inverse
     gain = line(gain_ref)
     for i in range(HEAD_PARTS):
         lanes = slice(i * WIDTH, (i + 1) * WIDTH)
         normed_ref[:, lanes] = (rows_ref[:, lanes].astype(F32) * inverse * gain[:, lanes]).astype(BF16)
+    kept = [pltpu.make_async_copy(normed_ref, normed_hbm, out_sems.at[0])]
+    kept[0].start()
     h = HEADS_HERE
     raw = dot(normed_ref[...], w_dt_ref[...], ((1,), (1,))) + inverse * line(pad_dt_ref) + line(bias_ref)
     soft = jnp.maximum(raw, 0.0) + jnp.log1p(jnp.exp(-jnp.abs(raw)))
     count = jnp.sum(line(flags_ref).astype(F32), axis=1, keepdims=True)
     step = jnp.where(iota((CAP, h), 0).astype(F32) < count, soft, 0.0)
-    step_ref[...] = step
     split = jnp.concatenate(thirds(log_decays(step, a_log_ref)), axis=1)
     lower = (iota((CAP, CAP), 1) <= iota((CAP, CAP), 0)).astype(BF16)
     run = sum_thirds(dot(lower, split), 1)
-    run_ref[...] = run
+    fill = jnp.zeros((CAP, WIDTH - 2 * h - 1), F32)
+    aux_ref[...] = jnp.concatenate([step, run, inverse, fill], axis=1)
     total = run[CAP - 1 :, :]
     tail = spread_heads(jnp.exp(total - run) * step)
     pad_proj = line(pad_proj_ref)
@@ -176,6 +179,7 @@
         lanes = slice(256 * t, 256 * (t + 1))
         offset = inverse * pad_proj[:, INNER + 256 * t : INNER + 256 * (t + 1)]
         xbc_ref[:, lanes] = dot(normed_ref[...], w_ref[t]) + offset
+    kept += fetch((xbc_ref, aux_ref), (xbc_hbm, aux_hbm), out_sems, 1)
     state = dot3(xbc_ref[:, INNER : INNER + N], xbc_ref[:, :INNER] * tail, ((0,), (0,)))
     total_wide = spread_heads(jnp.broadcast_to(total, (8, h)))[0:1, :]
     spare = jnp.concatenate(
@@ -188,17 +192,20 @@
         pieces_ref[d, 0:4, INNER:] = spare
         if per > 4:
             pieces_ref[d, 4:, INNER:] = jnp.zeros((per - 4, WIDTH), F32)
+    arrived(kept)
 
 
 def local_kernel(*refs):
-    given, w_in_ref, (out_ref, silu_ref), held, (w_ref, sems) = refs[:8], refs[8], refs[9:11], refs[11:19], refs[19:]
-    xbc_ref, normed_ref, inverse_ref, step_ref, run_ref, pad_proj_ref, a_log_ref, skip_ref = held
+    given, w_in_ref, outs_hbm, held = refs[:6], refs[6], refs[7:9], refs[9:15]
+    out_ref, silu_ref, w_ref, sems, out_sems = refs[15:]
+    xbc_ref, normed_ref, aux_ref, pad_proj_ref, a_log_ref, skip_ref = held
+    h = HEADS_HERE
     tiles = range(INNER // 256)
     pieces = [w_in_ref.at[:, 256 * t : 256 * (t + 1)] for t in tiles]
     copies = fetch(given + tuple(pieces), held + tuple(w_ref.at[t] for t in tiles), sems)
-    arrived(copies[:8])
-    copies = copies[8:]
-    split = jnp.concatenate(thirds(log_decays(step_ref[...], a_log_ref)), axis=1)
+    arrived(copies[: len(held)])
+    copies = copies[len(held) :]
+    split = jnp.concatenate(thirds(log_decays(aux_ref[:, :h], a_log_ref)), axis=1)
     upper = (iota((CAP, CAP), 0) <= iota((CAP, CAP), 1)).astype(BF16)
     run_t = sum_thirds(dot(split, upper, ((0,), (0,))), 0)
     state = jnp.zeros((N, INNER), F32)
@@ -209,8 +216,8 @@
         x = xbc_ref[rows, :INNER]
         b = xbc_ref[rows, INNER : INNER + N]
         c = xbc_ref[rows, INNER + N :]
-        run = run_ref[rows, :]
-        step = step_ref[rows, :]
+        step = aux_ref[rows, :h]
+        run = aux_ref[rows, h : 2 * h]
         end_run = run[length - 1 :, :]
         scaled = (x * spread_heads(step)).astype(BF16)
         inter = dot3(c, b, ((1,), (1,)))
@@ -229,12 +236,16 @@
             kept = spread_heads(jnp.broadcast_to(jnp.exp(end_run - start_run), (8, HEADS_HERE)))
             state = state * kept[0:1, :] + dot3(b, weighted, ((0,), (0,)))
         start_run = end_run
+    kept = fetch((out_ref,), outs_hbm[:1], out_sems)
     pad_proj = line(pad_proj_ref)
+    inverse = aux_ref[:, 2 * h : 2 * h + 1]
     for t in range(INNER // 256):
         copies[t].wait()
         lanes = slice(256 * t, 256 * (t + 1))
-        gate = dot(normed_ref[...], w_ref[t]) + inverse_ref[...] * pad_proj[:, lanes]
+        gate = dot(normed_ref[...], w_ref[t]) + inverse * pad_proj[:, lanes]
         silu_ref[:, lanes] = (gate / (1.0 + jnp.exp(-gate))).astype(BF16)
+    kept += fetch((silu_ref,), outs_hbm[1:], out_sems, 1)
+    arrived(kept)
 
 
 def scan_kernel(got_ref, before_ref):
@@ -248,19 +259,19 @@
 
 
 def output_kernel(
-    state_ref, c_hbm, run_hbm, local_hbm, silu_hbm, gain_hbm, w_out_hbm,
-    out_ref, full_ref, c_ref, run_ref, local_ref, silu_ref, gain_ref, w_ref, sems,
+    state_ref, c_hbm, aux_hbm, local_hbm, silu_hbm, gain_hbm, w_out_hbm,
+    out_ref, full_ref, c_ref, aux_ref, local_ref, silu_ref, gain_ref, w_ref, sems,
 ):
     copies = fetch(
-        (c_hbm.at[:, INNER + N :], run_hbm, local_hbm, silu_hbm, gain_hbm, w_out_hbm),
-        (c_ref, run_ref, local_ref, silu_ref, gain_ref, w_ref),
+        (c_hbm.at[:, INNER + N :], aux_hbm, local_hbm, silu_hbm, gain_hbm, w_out_hbm),
+        (c_ref, aux_ref, local_ref, silu_ref, gain_ref, w_ref),
         sems,
     )
     parts, per, _ = state_ref.shape
     for d in range(parts):
         full_ref[d * per : (d + 1) * per, :] = state_ref[d]
     arrived(copies[:2])
-    carried = spread_heads(jnp.exp(run_ref[...])) * dot3(c_ref[...], full_ref[...])
+    carried = spread_heads(jnp.exp(aux_ref[:, HEADS_HERE : 2 * HEADS_HERE])) * dot3(c_ref[...], full_ref[...])
     arrived(copies[2:5])
     gated = (local_ref[...].astype(F32) + carried) * silu_ref[...].astype(F32)
     power = jnp.mean(gated * gated, axis=1, keepdims=True)
@@ -286,8 +297,7 @@
     sent_ref[...] = jnp.broadcast_to(row[None], sent_ref.shape)
 
 
-def decode_kernel(enc_hbm, w_hi_ref, w_lo_ref, main_ref, decay_ref, carries_ref, out_ref, enc_ref, sems):
-    copies = fetch((enc_hbm,), (enc_ref,), sems)
+def decode_kernel(enc_ref, w_hi_ref, w_lo_ref, main_ref, decay_ref, carries_ref, out_ref):
     me = lax.axis_index("act")
     act = carries_ref.shape[0]
     carry = jnp.zeros((1, WIDTH), F32)
@@ -296,7 +306,6 @@
         carry = jnp.where(j < me, after, carry)
     main = main_ref[...]
     smoothed = dot(w_hi_ref[...], main) + dot(w_lo_ref[...], main) + decay_ref[...] * carry
-    arrived(copies)
     out_ref[...] = (enc_ref[...].astype(F32) + smoothed).astype(BF16)
 
 
@@ -304,8 +313,10 @@
     return jax.ShapeDtypeStruct(dims, dtype)
 
 
-def call(kernel, outs, name, specs=None, scratch=(), flops=0, transcendentals=0, nbytes=0):
+def call(kernel, outs, name, specs=None, out_specs=None, scratch=(), flops=0, transcendentals=0, nbytes=0):
     more = {} if specs is None else {"in_specs": specs}
+    if out_specs is not None:
+        more["out_specs"] = out_specs
     run = pl.pallas_call(
         kernel,
         out_shape=outs,
@@ -372,33 +383,31 @@
     )(boundary_flags, boundary_prob)
 
     small = [boundary_flags, pad_vector, norm_gain, w_dt.T, pad_proj, pad_dt, dt_bias, a_log]
-    xbc, normed, inverse, step, run, pieces = call(
+    kept_across = [((CAP, XBC), F32), ((CAP, D), BF16), ((CAP, WIDTH), F32)]
+    xbc, normed, aux, pieces = call(
         project_kernel,
-        (
-            shape((CAP, XBC)),
-            shape((CAP, D), BF16),
-            shape((CAP, 1)),
-            shape((CAP, HEADS_HERE)),
-            shape((CAP, HEADS_HERE)),
-            shape((act, N // act, INNER + WIDTH)),
-        ),
+        [pltpu.HBM(*a) for a in kept_across] + [shape((act, N // act, INNER + WIDTH))],
         "project",
+        out_specs=[apart] * 3 + [held],
         specs=[held] + [apart] * (1 + len(small)),
         scratch=[pltpu.VMEM(a.shape, a.dtype) for a in small]
-        + [pltpu.VMEM((XBC // 256, D, 256), BF16), dma((XBC // 256,)), dma((len(small),))],
+        + [pltpu.VMEM(*a) for a in kept_across]
+        + [pltpu.VMEM((XBC // 256, D, 256), BF16), dma((XBC // 256,)), dma((len(small),)), dma((3,))],
         flops=2 * CAP * D * XBC,
         nbytes=8 * 10**6,
     )(rows, w_in, *small)
 
     got = lax.all_to_all(pieces, "act", 0, 0)
-    needed = [xbc, normed, inverse, step, run, pad_proj, a_log, d_skip]
+    needed = [xbc, normed, aux, pad_proj, a_log, d_skip]
     local, silu = call(
         local_kernel,
-        (shape((CAP, INNER), BF16), shape((CAP, INNER), BF16)),
+        [pltpu.HBM((CAP, INNER), BF16)] * 2,
         "local",
+        out_specs=[apart] * 2,
         specs=[apart] * (len(needed) + 1),
         scratch=[pltpu.VMEM(a.shape, a.dtype) for a in needed]
-        + [pltpu.VMEM((INNER // 256, D, 256), BF16), dma((len(needed) + INNER // 256,))],
+        + [pltpu.VMEM((CAP, INNER), BF16)] * 2
+        + [pltpu.VMEM((INNER // 256, D, 256), BF16), dma((len(needed) + INNER // 256,)), dma((2,))],
         flops=2 * 10**9,
         transcendentals=CAP * 2048,
         nbytes=6 * 10**6,
@@ -414,7 +423,7 @@
         scratch=[
             pltpu.VMEM((N, INNER), F32),
             pltpu.VMEM((CAP, N), F32),
-            pltpu.VMEM((CAP, HEADS_HERE), F32),
+            pltpu.VMEM((CAP, WIDTH), F32),
             pltpu.VMEM((CAP, INNER), BF16),
             pltpu.VMEM((CAP, INNER), BF16),
             pltpu.VMEM((INNER,), F32),
@@ -423,7 +432,7 @@
         ],
         flops=2 * CAP * INNER * D,
         nbytes=6 * 10**6,
-    )(state_in, xbc, run, local, silu, gate_gain, w_out)
+    )(state_in, xbc, aux, local, silu, gate_gain, w_out)
 
     parts = lax.all_to_all(partial, "head", 0, 0)
     main, carry = call(
@@ -434,8 +443,6 @@
         decode_kernel,
         shape((BYTES, WIDTH), BF16),
         "decode",
-        specs=[apart] + [held] * 5,
-        scratch=[pltpu.VMEM((BYTES, WIDTH), BF16), dma((1,))],
         flops=2 * 10**8,
         nbytes=2 * 10**6,
     )(enc_rows, w_hi, w_lo, main, decay, carries)

time: 107 us -> 103 us (0.963)
  local copies, waits for them, and re-layouts: 4.23 us -> 0.01 us
    unnamed x18 -> x6, local copies, waits for them, and re-layouts: 4.23 us -> 0.01 us
    pallas_call x0 -> x1, Pallas kernels: none -> 1.14 us  [body(): call(decode_kernel, shape((BYTES, WIDTH), BF16), 'decode', flops=2 * 10 *...]
    pallas_call x5 -> x4, Pallas kernels: 17.8 us -> 17.1 us  [call(): run(*[pltpu.with_memory_space_constraint(a, pltpu.HBM) if spec.memory_spa...]
  transfers between devices with their start and end apart: 2 -> 2, of which waited for: 2 -> 2; matrix products, arithmetic and copies ran while one was open for 0% -> 0% of each run, Pallas kernels for 7% -> 8%
where the time goes in v6:
time: 103 us; the launch traced here: 102 us
  blocking collectives  55.1 us (53%)
  Pallas kernels  20.5 us (20%)
  waiting for transfers between devices  16.5 us (16%)
  starting transfers between devices  9.79 us (10%)
    all_to_all x1, blocking collectives, body(): got = lax.all_to_all(pieces, 'act', 0, 0)  23.8 us
    pallas_call x4, Pallas kernels, call(): run(*[pltpu.with_memory_space_constraint(a, pltpu.HBM) if spec.memory_spa...  17.1 us
    all_gather x1, blocking collectives, body(): rows = lax.all_gather(packed, 'head', axis=1, tiled=True)  16.7 us
    all_to_all x1, blocking collectives, body(): carries = lax.all_to_all(carry, 'act', 0, 0)  14.6 us
    all_to_all x1, waiting for transfers between devices, body(): parts = lax.all_to_all(partial, 'head', 0, 0)  10.9 us
    all_to_all x1, waiting for transfers between devices, body(): state_in = lax.all_to_all(before, 'act', 0, 0)  5.56 us
    all_to_all x1, starting transfers between devices, body(): parts = lax.all_to_all(partial, 'head', 0, 0)  4.92 us
    all_to_all x1, starting transfers between devices, body(): state_in = lax.all_to_all(before, 'act', 0, 0)  4.87 us
  transfers between devices with their start and end apart: 2, of which 2 were waited for; matrix products, arithmetic and copies ran while one was open for 0% of the time, Pallas kernels for 8%

profile of v6, /device:TPU:6, one launch (start us, length us, event | category | flops | bytes accessed | tf_op | source)
XLA Modules:
  0.0 102.0 jit_solution(13103025118753490251)
XLA Ops:
  0.0 1.5 %select.1.packed_ref = bf16[432,128]{1,0:T(8,128)(2,1)S(1)} custom-call(s32[576]{0:T(1024)} %refs_0_.1, bf16[576,128]{1,0:T(8,128)(2,1)} %enc_ref.1), custom_call_target="tpu_custom_call" | custom-call | flops 100000000 | tf_op jit(solution)/shard_map/select/pallas_call | solution.py:333
  1.5 16.7 %all_gather.3.rows_ref = bf16[432,1024]{1,0:T(8,128)(2,1)S(1)} all-gather(bf16[432,128]{1,0:T(8,128)(2,1)S(1)} %select.1.packed_ref), channel_id=1, replica_groups=mesh['half'=2,'act'=32,'head'=8] {'head'}, dimensions={1}, use_global_device_ids=true | all-gather | bytes 995328 | tf_op jit(solution)/shard_map/all_gather | solution.py:368
  18.2 5.5 %project.1 = (f32[432,768]{1,0:T(8,128)}, bf16[432,1024]{1,0:T(8,128)(2,1)}, f32[432,128]{1,0:T(8,128)}, f32[32,4,640]{2,1,0:T(4,128)S(1)}) custom-call(bf16[432,1024]{1,0:T(8,128)(2,1)S(1)} %all_gather.3.rows_ref, bf16[1024,1280]{1,0:T(8,128)(2,1)} %refs_6_.3, s32[576]{0:T(1024)} %refs_0_.1, f32[1024]{0:T(1024)} %refs_1_.1, f32[1024]{0:T(1024)} %refs_2_.1, ...), custom_call_target="tpu_custom_call" | custom-call | flops 679477248 | bytes 8000000 | tf_op jit(solution)/shard_map/project/pallas_call | solution.py:333
  23.7 23.8 %all_to_all.20.got_ref = f32[32,4,640]{2,1,0:T(4,128)S(1)} all-to-all(f32[32,4,640]{2,1,0:T(4,128)S(1)} %get-tuple-element.20), channel_id=1, replica_groups=mesh['half'=2,'act'=32,'head'=8] {'act'}, dimensions={0} | all-to-all | bytes 655360 | tf_op jit(solution)/shard_map/all_to_all | solution.py:400
  47.5 0.8 scan.1
  48.3 4.9 %all-to-all-start.1 = ((f32[32,4,512]{2,1,0:T(4,128)}), f32[32,4,512]{2,1,0:T(4,128)S(1)}, u32[]{:S(2)}, u32[]{:S(2)}) async-start(f32[32,4,512]{2,1,0:T(4,128)} %scan.1), calls=%async_computation.1 | async-start | bytes 524288 | tf_op jit(solution)/shard_map/all_to_all | solution.py:416
  53.2 6.5 %local.1 = (bf16[432,512]{1,0:T(8,128)(2,1)}, bf16[432,512]{1,0:T(8,128)(2,1)}) custom-call(f32[432,768]{1,0:T(8,128)} %get-tuple-element.21.refs_0_.c_hbm, bf16[432,1024]{1,0:T(8,128)(2,1)} %get-tuple-element.23.refs_1_, f32[432,128]{1,0:T(8,128)} %get-tuple-element.22.refs_2_.aux_hbm, f32[1280]{0:T(1024)} %refs_3_.1, f32[8]{0:T(128)} %refs_4_.3, ...), custom_call_target="tpu_custom_call" | custom-call | flops 2000000000 | bytes 6000000 | tf_op jit(solution)/shard_map/local/pallas_call | solution.py:333
  59.7 5.6 %all-to-all-done.1.state_ref = f32[32,4,512]{2,1,0:T(4,128)S(1)} async-done(((f32[32,4,512]{2,1,0:T(4,128)}), f32[32,4,512]{2,1,0:T(4,128)S(1)}, u32[]{:S(2)}, u32[]{:S(2)}) %all-to-all-start.1) | async-done | bytes 262176 | tf_op jit(solution)/shard_map/all_to_all | solution.py:416
  65.2 0.0 copy-start.1
  65.2 0.0 copy-start.2
  65.3 3.6 %output.1 = bf16[8,432,128]{2,1,0:T(8,128)(2,1)} custom-call(f32[32,4,512]{2,1,0:T(4,128)S(1)} %all-to-all-done.1.state_ref, f32[432,768]{1,0:T(8,128)} %get-tuple-element.21.refs_0_.c_hbm, f32[432,128]{1,0:T(8,128)} %get-tuple-element.22.refs_2_.aux_hbm, bf16[432,512]{1,0:T(8,128)(2,1)} %get-tuple-element.24.local_hbm, ...), custom_call_target="tpu_custom_call" | custom-call | flops 452984832 | bytes 6000000 | tf_op jit(solution)/shard_map/output/pallas_call | solution.py:333
  68.9 0.0 copy-start
  68.9 4.9 %all-to-all-start.2 = ((bf16[8,432,128]{2,1,0:T(8,128)(2,1)}), bf16[8,432,128]{2,1,0:T(8,128)(2,1)S(1)}, u32[]{:S(2)}, u32[]{:S(2)}) async-start(bf16[8,432,128]{2,1,0:T(8,128)(2,1)} %output.1), calls=%async_computation.2 | async-start | bytes 1769472 | tf_op jit(solution)/shard_map/all_to_all | solution.py:437
  73.8 0.0 copy-done.1
  73.8 0.0 copy-done.2
  73.8 1.2 %weights.1 = (bf16[576,432]{1,0:T(8,128)(2,1)S(1)}, bf16[576,432]{1,0:T(8,128)(2,1)S(1)}, f32[1,432]{1,0:T(1,128)S(1)}, f32[1,128]{1,0:T(1,128)S(1)}, f32[576,1]{1,0:T(8,128)S(1)}) custom-call(s32[576]{0:T(1024)S(1)} %copy-done.1, bf16[576]{0:T(1024)(128)(2,1)S(1)} %copy-done.2), custom_call_target="tpu_custom_call" | custom-call | flops 7464960 | bytes 1000000 | tf_op jit(solution)/shard_map/weights/pallas_call | solution.py:370
  75.1 10.9 %all-to-all-done.2.parts_ref = bf16[8,432,128]{2,1,0:T(8,128)(2,1)S(1)} async-done(((bf16[8,432,128]{2,1,0:T(8,128)(2,1)}), bf16[8,432,128]{2,1,0:T(8,128)(2,1)S(1)}, u32[]{:S(2)}, u32[]{:S(2)}) %all-to-all-start.2) | async-done | bytes 884768 | tf_op jit(solution)/shard_map/all_to_all | solution.py:437
  86.0 0.3 main.1
  86.2 14.6 %all_to_all.21.carries_ref = f32[32,2,128]{2,1,0:T(2,128)S(1)} all-to-all(f32[32,2,128]{2,1,0:T(2,128)S(1)} %get-tuple-element.30), channel_id=1, replica_groups=mesh['half'=2,'act'=32,'head'=8] {'act'}, dimensions={0} | all-to-all | bytes 65536 | tf_op jit(solution)/shard_map/all_to_all | solution.py:441
  100.8 0.0 copy-done
  100.8 1.1 %decode.1 = bf16[576,128]{1,0:T(8,128)(2,1)} custom-call(bf16[576,128]{1,0:T(8,128)(2,1)S(1)} %copy-done, bf16[576,432]{1,0:T(8,128)(2,1)S(1)} %get-tuple-element.18.w_hi_ref, bf16[576,432]{1,0:T(8,128)(2,1)S(1)} %get-tuple-element.19.w_lo_ref, bf16[432,128]{1,0:T(8,128)(2,1)S(1)} %get-tuple-element.28.main_ref, f32[576,1]{1,0:T(8,128)S(1)} %get-tuple-element.29.decay_ref, ...), custom_call_target="tpu_custom_call" | custom-call | flops 200000000 | bytes 2000000 | tf_op jit(solution)/shard_map/decode/pallas_call | solution.py:442
Async XLA Ops:
  48.3 16.9 %all-to-all-start.1 = ((f32[32,4,512]{2,1,0:T(4,128)}), f32[32,4,512]{2,1,0:T(4,128)S(1)}, u32[]{:S(2)}, u32[]{:S(2)}) async-start(f32[32,4,512]{2,1,0:T(4,128)} %scan.1), calls=%async_computation.1 | async-start | bytes 524288 | tf_op jit(solution)/shard_map/all_to_all | solution.py:416
  65.2 8.6 %copy-start.1 = (s32[576]{0:T(1024)S(1)}, s32[576]{0:T(1024)}, u32[]{:S(2)}) copy-start(s32[576]{0:T(1024)} %refs_0_.1) | copy-start | bytes 6916
  65.2 8.6 %copy-start.2 = (bf16[576]{0:T(1024)(128)(2,1)S(1)}, bf16[576]{0:T(1024)(128)(2,1)}, u32[]{:S(2)}) copy-start(bf16[576]{0:T(1024)(128)(2,1)} %prob_ref.1) | copy-start | bytes 3460
  68.9 31.9 %copy-start = (bf16[576,128]{1,0:T(8,128)(2,1)S(1)}, bf16[576,128]{1,0:T(8,128)(2,1)}, u32[]{:S(2)}) copy-start(bf16[576,128]{1,0:T(8,128)(2,1)} %enc_ref.1) | copy-start | bytes 442372
  68.9 17.1 %all-to-all-start.2 = ((bf16[8,432,128]{2,1,0:T(8,128)(2,1)}), bf16[8,432,128]{2,1,0:T(8,128)(2,1)S(1)}, u32[]{:S(2)}, u32[]{:S(2)}) async-start(bf16[8,432,128]{2,1,0:T(8,128)(2,1)} %output.1), calls=%async_computation.2 | async-start | bytes 1769472 | tf_op jit(solution)/shard_map/all_to_all | solution.py:437

commit v7 on v6

--- a/solution.py
+++ b/solution.py
@@ -15,6 +15,7 @@
 COLS = 2 * INNER + 2 * N
 CAP = 432
 HEAD_PARTS = 8
+X_CHIPS = 4
 BYTES = 576
 WIDTH = 128
 CHUNKS = ((0, 128), (128, 128), (256, 128), (384, 48))
@@ -89,15 +90,19 @@
     packed_ref[...] = dot(hit, enc_ref[...]).astype(BF16)
 
 
-def weights_kernel(flags_ref, prob_ref, w_hi_ref, w_lo_ref, carry_ref, kept_ref, decay_ref):
+def weights_kernel(flags_ref, prob_ref, packed_ref, w_hi_ref, w_lo_ref, carry_ref, own_ref, decay_ref):
     flags = line(flags_ref).astype(F32)
     prob = prob_ref[...].astype(F32).reshape(1, BYTES)
     logs = jnp.where(flags > 0, jnp.log1p(-prob), 0.0)
     before = iota((BYTES, BYTES), 1) <= iota((BYTES, BYTES), 0)
+    after = iota((BYTES, BYTES), 0) <= iota((BYTES, BYTES), 1)
     same = iota((BYTES, BYTES), 1) == iota((BYTES, BYTES), 0)
 
     def column(mask, row):
         return jnp.sum(jnp.where(mask, row, 0.0), axis=1, keepdims=True)
+
+    def across(mask, col):
+        return jnp.sum(jnp.where(mask, col, 0.0), axis=0, keepdims=True)
 
     rank = column(before, flags)
     kept = column(before, logs)
@@ -105,18 +110,22 @@
     chance = column(same, prob)
     place = iota((BYTES, CAP), 1).astype(F32)
     hit = (place == rank - 1.0) & (flag > 0)
-    kept_k = jnp.sum(jnp.where(hit, kept, 0.0), axis=0, keepdims=True)
-    prob_k = jnp.sum(jnp.where(hit, chance, 0.0), axis=0, keepdims=True)
-    gap = jnp.where(place < rank, kept - kept_k, LOW)
-    hi, lo = halves(jnp.exp(gap) * prob_k)
+    gap = jnp.where(place < rank, kept - across(hit, kept), LOW)
+    hi, lo = halves(jnp.exp(gap) * across(hit, chance))
     w_hi_ref[...] = hi
     w_lo_ref[...] = lo
+    decay_ref[...] = jnp.exp(kept)
+    rank_row = across(after, flag)
+    kept_row = across(after, column(same, logs))
+    place = iota((CAP, BYTES), 0).astype(F32)
+    hit = (place == rank_row - 1.0) & (flags > 0)
     total = jnp.sum(logs, axis=1, keepdims=True)
     count = jnp.sum(flags, axis=1, keepdims=True)
-    real = iota((1, CAP), 1).astype(F32) < count
-    carry_ref[...] = jnp.exp(jnp.where(real, total - kept_k, LOW)) * prob_k
-    kept_ref[...] = jnp.broadcast_to(total, (1, WIDTH))
-    decay_ref[...] = jnp.exp(kept)
+    real = iota((CAP, 1), 0).astype(F32) < count
+    weight = jnp.exp(jnp.where(real, total - column(hit, kept_row), LOW)) * column(hit, prob)
+    wide = jnp.broadcast_to(weight, (CAP, WIDTH))
+    carry_ref[...] = wide
+    own_ref[...] = jnp.sum(wide * packed_ref[...].astype(F32), axis=0, keepdims=True)
 
 
 def log_decays(step, a_log_ref):
@@ -133,10 +142,10 @@
 def project_kernel(
     rows_ref, w_in_ref, *refs,
 ):
-    given, refs = refs[:8], refs[8:]
+    given, refs = refs[:9], refs[9:]
     (xbc_hbm, normed_hbm, aux_hbm, pieces_ref), refs = refs[:4], refs[4:]
-    held, (xbc_ref, normed_ref, aux_ref, w_ref, sems, small_sems, out_sems) = refs[:8], refs[8:]
-    flags_ref, pad_ref, gain_ref, w_dt_ref, pad_proj_ref, pad_dt_ref, bias_ref, a_log_ref = held
+    held, (xbc_ref, normed_ref, aux_ref, w_ref, sems, small_sems, out_sems) = refs[:9], refs[9:]
+    flags_ref, prob_ref, pad_ref, gain_ref, w_dt_ref, pad_proj_ref, pad_dt_ref, bias_ref, a_log_ref = held
     small = fetch(given, held, small_sems)
     tiles = range(XBC // 256)
     copies = [
@@ -181,9 +190,11 @@
         xbc_ref[:, lanes] = dot(normed_ref[...], w_ref[t]) + offset
     kept += fetch((xbc_ref, aux_ref), (xbc_hbm, aux_hbm), out_sems, 1)
     state = dot3(xbc_ref[:, INNER : INNER + N], xbc_ref[:, :INNER] * tail, ((0,), (0,)))
-    total_wide = spread_heads(jnp.broadcast_to(total, (8, h)))[0:1, :]
+    prob = prob_ref[...].astype(F32).reshape(1, BYTES)
+    keeps = jnp.sum(jnp.where(line(flags_ref) > 0, jnp.log1p(-prob), 0.0), axis=1, keepdims=True)
+    head_row = jnp.concatenate([total, jnp.zeros((1, WIDTH - h), F32)], axis=1)
     spare = jnp.concatenate(
-        [total_wide[:, i * WIDTH : (i + 1) * WIDTH] for i in range(INNER // WIDTH)], axis=0
+        [head_row, jnp.broadcast_to(keeps, (1, WIDTH)), jnp.zeros((2, WIDTH), F32)], axis=0
     )
     parts = pieces_ref.shape[0]
     per = N // parts
@@ -248,23 +259,27 @@
     arrived(kept)
 
 
-def scan_kernel(got_ref, before_ref):
+def scan_kernel(got_ref, before_ref, keeps_ref):
     act, per, _ = got_ref.shape
+    logs = jnp.concatenate([got_ref[j, 0:1, INNER:] for j in range(act)], axis=0)
+    keeps_ref[...] = jnp.concatenate([got_ref[j, 1:2, INNER:] for j in range(act)], axis=0)
+    keep = spread_heads(jnp.exp(logs[:, :HEADS_HERE]))
     state = jnp.zeros((per, INNER), F32)
     for j in range(act):
         before_ref[j] = state
-        keep = jnp.exp(got_ref[j, 0:4, INNER:])
-        keep = jnp.concatenate([keep[i : i + 1, :] for i in range(INNER // WIDTH)], axis=1)
-        state = state * keep + got_ref[j, :, :INNER]
+        state = state * keep[j : j + 1, :] + got_ref[j, :, :INNER]
 
 
 def output_kernel(
-    state_ref, c_hbm, aux_hbm, local_hbm, silu_hbm, gain_hbm, w_out_hbm,
-    out_ref, full_ref, c_ref, aux_ref, local_ref, silu_ref, gain_ref, w_ref, sems,
+    state_ref, c_hbm, aux_hbm, local_hbm, silu_hbm, gain_hbm, w_out_hbm, carry_hbm, own_hbm,
+    kept_ref, sent_ref, rows_ref,
+    full_ref, c_ref, aux_ref, local_ref, silu_ref, gain_ref, w_ref, carry_ref, own_ref, sems,
 ):
+    core = lax.axis_index("core")
+    head = lax.axis_index("x") * 2 + core
     copies = fetch(
-        (c_hbm.at[:, INNER + N :], aux_hbm, local_hbm, silu_hbm, gain_hbm, w_out_hbm),
-        (c_ref, aux_ref, local_ref, silu_ref, gain_ref, w_ref),
+        (c_hbm.at[:, INNER + N :], aux_hbm, local_hbm, silu_hbm, gain_hbm, w_out_hbm, carry_hbm, own_hbm),
+        (c_ref, aux_ref, local_ref, silu_ref, gain_ref, w_ref, carry_ref, own_ref),
         sems,
     )
     parts, per, _ = state_ref.shape
@@ -277,34 +292,44 @@
     power = jnp.mean(gated * gated, axis=1, keepdims=True)
     mixed = (gated * lax.rsqrt(power + eps) * line(gain_ref)).astype(BF16)
     arrived(copies[5:])
-    for i in range(HEAD_PARTS // 2):
-        pair = dot(mixed, w_ref[:, i * 2 * WIDTH : (i + 1) * 2 * WIDTH]).astype(BF16)
-        out_ref[2 * i] = pair[:, :WIDTH]
-        out_ref[2 * i + 1] = pair[:, WIDTH:]
-
-
-def main_kernel(packed_ref, parts_ref, carry_ref, kept_ref, main_ref, sent_ref):
-    summed = packed_ref[...].astype(F32)
-    added = parts_ref[0].astype(F32)
+    weight = carry_ref[...]
+    carries = []
+    for i in range(X_CHIPS):
+        pair = dot(mixed, w_ref[:, i * 2 * WIDTH : (i + 1) * 2 * WIDTH])
+        first, second = pair[:, :WIDTH], pair[:, WIDTH:]
+        kept_ref[i] = jnp.where(core == 0, first, second)
+        sent_ref[i] = jnp.where(core == 0, second, first).astype(BF16)
+        carries += [jnp.sum(weight * part, axis=0, keepdims=True) for part in (first, second)]
+    mine = iota((HEAD_PARTS, WIDTH), 0) == head
+    rows = jnp.concatenate(carries, axis=0) + jnp.where(mine, own_ref[...], 0.0)
+    rows_ref[...] = jnp.broadcast_to(rows[None], rows_ref.shape)
+
+
+def pair_kernel(packed_ref, own_ref, got_ref, keep_ref, s1, s2, s3):
+    x = lax.axis_index("x")
+    keep_ref[...] = packed_ref[...].astype(F32) + (own_ref[x] + got_ref[x].astype(F32))
+    for s, out_ref in enumerate((s1, s2, s3), start=1):
+        chip = lax.rem(x + s, X_CHIPS)
+        out_ref[...] = (own_ref[chip] + got_ref[chip].astype(F32)).astype(BF16)
+
+
+def carry_kernel(got_ref, keeps_ref, sent_ref):
+    me = lax.axis_index("act")
+    act, parts, _ = got_ref.shape
+    keep = jnp.exp(keeps_ref[...])
+    carry = jnp.zeros((parts, WIDTH), F32)
+    for j in range(act):
+        carry = jnp.where(j < me, carry * keep[j : j + 1, :] + got_ref[j], carry)
+    for i in range(parts):
+        sent_ref[i] = carry[i : i + 1, :]
+
+
+def decode_kernel(enc_ref, w_hi_ref, w_lo_ref, keep_ref, r1, r2, r3, decay_ref, carries_ref, out_ref):
+    added = r1[...].astype(F32) + r2[...].astype(F32) + r3[...].astype(F32)
+    main = (keep_ref[...] + added).astype(BF16)
+    carry = carries_ref[0]
     for i in range(1, HEAD_PARTS):
-        added = added + parts_ref[i].astype(F32)
-    main = (summed + added).astype(BF16)
-    main_ref[...] = main
-    split = jnp.concatenate([jnp.broadcast_to(p, (8, CAP)) for p in thirds(carry_ref[...])], axis=0)
-    sums = dot(split, main)
-    carry = sums[0:1] + sums[8:9] + sums[16:17]
-    row = jnp.concatenate([carry, kept_ref[...]], axis=0)
-    sent_ref[...] = jnp.broadcast_to(row[None], sent_ref.shape)
-
-
-def decode_kernel(enc_ref, w_hi_ref, w_lo_ref, main_ref, decay_ref, carries_ref, out_ref):
-    me = lax.axis_index("act")
-    act = carries_ref.shape[0]
-    carry = jnp.zeros((1, WIDTH), F32)
-    for j in range(act):
-        after = carry * jnp.exp(carries_ref[j, 1:2, :]) + carries_ref[j, 0:1, :]
-        carry = jnp.where(j < me, after, carry)
-    main = main_ref[...]
+        carry = carry + carries_ref[i]
     smoothed = dot(w_hi_ref[...], main) + dot(w_lo_ref[...], main) + decay_ref[...] * carry
     out_ref[...] = (enc_ref[...].astype(F32) + smoothed).astype(BF16)
 
@@ -355,6 +380,7 @@
     w_out,
 ):
     act = lax.axis_size("act")
+    heads = ("x", "core")
     held, apart = pl.BlockSpec(), pl.BlockSpec(memory_space=pltpu.HBM)
     dma = pltpu.SemaphoreType.DMA
     packed = call(
@@ -365,14 +391,14 @@
         scratch=[pltpu.VMEM((BYTES,), jnp.int32), pltpu.VMEM((BYTES, WIDTH), BF16), dma((2,))],
         flops=10**8,
     )(boundary_flags, enc_rows)
-    rows = lax.all_gather(packed, "head", axis=1, tiled=True)
-
-    w_hi, w_lo, carry_w, kept, decay = call(
+    rows = lax.all_gather(packed, heads, axis=1, tiled=True)
+
+    w_hi, w_lo, carry_w, own_row, decay = call(
         weights_kernel,
         (
             shape((BYTES, CAP), BF16),
             shape((BYTES, CAP), BF16),
-            shape((1, CAP)),
+            shape((CAP, WIDTH)),
             shape((1, WIDTH)),
             shape((BYTES, 1)),
         ),
@@ -380,9 +406,9 @@
         transcendentals=BYTES * CAP,
         flops=BYTES * CAP * 30,
         nbytes=10**6,
-    )(boundary_flags, boundary_prob)
-
-    small = [boundary_flags, pad_vector, norm_gain, w_dt.T, pad_proj, pad_dt, dt_bias, a_log]
+    )(boundary_flags, boundary_prob, packed)
+
+    small = [boundary_flags, boundary_prob, pad_vector, norm_gain, w_dt.T, pad_proj, pad_dt, dt_bias, a_log]
     kept_across = [((CAP, XBC), F32), ((CAP, D), BF16), ((CAP, WIDTH), F32)]
     xbc, normed, aux, pieces = call(
         project_kernel,
@@ -412,14 +438,20 @@
         transcendentals=CAP * 2048,
         nbytes=6 * 10**6,
     )(*needed, w_in)
-    before = call(scan_kernel, shape((act, N // act, INNER)), "scan", nbytes=6 * 10**5)(got)
+    before, keeps = call(
+        scan_kernel, (shape((act, N // act, INNER)), shape((act, WIDTH))), "scan", nbytes=6 * 10**5
+    )(got)
     state_in = lax.all_to_all(before, "act", 0, 0)
 
-    partial = call(
+    own, sent, carry_rows = call(
         output_kernel,
-        shape((HEAD_PARTS, CAP, WIDTH), BF16),
+        (
+            shape((X_CHIPS, CAP, WIDTH)),
+            shape((X_CHIPS, CAP, WIDTH), BF16),
+            shape((act, HEAD_PARTS, WIDTH)),
+        ),
         "output",
-        specs=[held] + [apart] * 6,
+        specs=[held] + [apart] * 8,
         scratch=[
             pltpu.VMEM((N, INNER), F32),
             pltpu.VMEM((CAP, N), F32),
@@ -428,30 +460,36 @@
             pltpu.VMEM((CAP, INNER), BF16),
             pltpu.VMEM((INNER,), F32),
             pltpu.VMEM((INNER, D), BF16),
-            dma((6,)),
+            pltpu.VMEM((CAP, WIDTH), F32),
+            pltpu.VMEM((1, WIDTH), F32),
+            dma((8,)),
         ],
         flops=2 * CAP * INNER * D,
         nbytes=6 * 10**6,
-    )(state_in, xbc, aux, local, silu, gate_gain, w_out)
-
-    parts = lax.all_to_all(partial, "head", 0, 0)
-    main, carry = call(
-        main_kernel, (shape((CAP, WIDTH), BF16), shape((act, 2, WIDTH))), "main", nbytes=6 * 10**5
-    )(packed, parts, carry_w, kept)
-    carries = lax.all_to_all(carry, "act", 0, 0)
+    )(state_in, xbc, aux, local, silu, gate_gain, w_out, carry_w, own_row)
+
+    all_rows = lax.all_to_all(carry_rows, "act", 0, 0)
+    got_sums = lax.ppermute(sent, "core", [(0, 1), (1, 0)])
+    block = shape((CAP, WIDTH), BF16)
+    keep, *parts = call(
+        pair_kernel, (shape((CAP, WIDTH)), block, block, block), "pair", nbytes=2 * 10**6
+    )(packed, own, got_sums)
+    parts = [over_chips(a, s) for s, a in enumerate(parts, start=1)]
+    carry = call(carry_kernel, shape((HEAD_PARTS, 1, WIDTH)), "carry", nbytes=2 * 10**5)(all_rows, keeps)
+    carries = lax.all_to_all(carry, heads, 0, 0)
     return call(
-        decode_kernel,
-        shape((BYTES, WIDTH), BF16),
-        "decode",
-        flops=2 * 10**8,
-        nbytes=2 * 10**6,
-    )(enc_rows, w_hi, w_lo, main, decay, carries)
+        decode_kernel, shape((BYTES, WIDTH), BF16), "decode", flops=2 * 10**8, nbytes=2 * 10**6
+    )(enc_rows, w_hi, w_lo, keep, *parts, decay, carries)
+
+
+def over_chips(a, s):
+    return lax.ppermute(a, "x", [(i, (i + s) % X_CHIPS) for i in range(X_CHIPS)])
 
 
 def solution(mesh):
-    seq, heads = mesh.shape["seq"], mesh.shape["head"]
-    split = Mesh(mesh.devices.reshape(2, seq // 2, heads), ("half", "act", "head"))
-    by_seq, by_head = ("half", "act"), "head"
+    seq = mesh.shape["seq"]
+    split = Mesh(mesh.devices.reshape(2, seq // 2, X_CHIPS, 2), ("half", "act", "x", "core"))
+    by_seq, by_head = ("half", "act"), ("x", "core")
     in_specs = (
         P(by_seq, by_head),
         P(by_seq),

time: 103 us -> 102 us (level)
  the two profiles are of different devices: /device:TPU:6 before, /device:TPU:1 now
where the time goes in v7:
time: 102 us; the launch traced here: 101 us
  blocking collectives  49.6 us (49%)
  starting transfers between devices  25.6 us (25%)
  Pallas kernels  22.3 us (22%)
  waiting for transfers between devices  2.52 us (2%)
  local copies, waits for them, and re-layouts  1.33 us (1%)
    all_to_all x1, blocking collectives, body(): got = lax.all_to_all(pieces, 'act', 0, 0)  21.1 us
    all_gather x1, blocking collectives, body(): rows = lax.all_gather(packed, heads, axis=1, tiled=True)  20 us
    pallas_call x4, Pallas kernels, call(): run(*[pltpu.with_memory_space_constraint(a, pltpu.HBM) if spec.memory_spa...  17.5 us
    ppermute x3, starting transfers between devices, over_chips(): lax.ppermute(a, 'x', [(i, (i + s) % X_CHIPS) for i in range(X_CHIPS)])  9.83 us
    all_to_all x1, blocking collectives, body(): carries = lax.all_to_all(carry, heads, 0, 0)  8.42 us
    all_to_all x1, starting transfers between devices, body(): all_rows = lax.all_to_all(carry_rows, 'act', 0, 0)  6.28 us
    all_to_all x1, starting transfers between devices, body(): state_in = lax.all_to_all(before, 'act', 0, 0)  5.57 us
    ppermute x1, starting transfers between devices, body(): got_sums = lax.ppermute(sent, 'core', [(0, 1), (1, 0)])  3.88 us
  transfers between devices with their start and end apart: 6, of which 1 were waited for; matrix products, arithmetic and copies ran while one was open for 0% of the time, Pallas kernels for 9%

profile of v7, /device:TPU:1, one launch (start us, length us, event | category | flops | bytes accessed | tf_op | source)
XLA Modules:
  0.0 101.4 jit_solution(574539213123329102)
XLA Ops:
  0.0 1.5 %select.1.packed_ref = bf16[432,128]{1,0:T(8,128)(2,1)S(1)} custom-call(s32[576]{0:T(1024)} %refs_0_.1, bf16[576,128]{1,0:T(8,128)(2,1)} %enc_ref.1), custom_call_target="tpu_custom_call" | custom-call | flops 100000000 | tf_op jit(solution)/shard_map/select/pallas_call | solution.py:358
  1.5 20.0 %all_gather.3.rows_ref = bf16[432,1024]{1,0:T(8,128)(2,1)S(1)} all-gather(bf16[432,128]{1,0:T(8,128)(2,1)S(1)} %select.1.packed_ref), channel_id=1, replica_groups=mesh['half'=2,'act'=32,'x'=4,'core'=2] {'x','core'}, dimensions={1}, use_global_device_ids=true | all-gather | bytes 995328 | tf_op jit(solution)/shard_map/all_gather | solution.py:394
  21.5 5.9 %project.1 = (f32[432,768]{1,0:T(8,128)}, bf16[432,1024]{1,0:T(8,128)(2,1)}, f32[432,128]{1,0:T(8,128)}, f32[32,4,640]{2,1,0:T(4,128)S(1)}) custom-call(bf16[432,1024]{1,0:T(8,128)(2,1)S(1)} %all_gather.3.rows_ref, bf16[1024,1280]{1,0:T(8,128)(2,1)} %refs_6_.3, s32[576]{0:T(1024)} %refs_0_.1, bf16[576]{0:T(1024)(128)(2,1)} %refs_1_.1, f32[1024]{0:T(1024)} %refs_2_.1, ...), custom_call_target="tpu_custom_call" | custom-call | flops 679477248 | bytes 8000000 | tf_op jit(solution)/shard_map/project/pallas_call | solution.py:358
  27.4 21.1 %all_to_all.20.got_ref = f32[32,4,640]{2,1,0:T(4,128)S(1)} all-to-all(f32[32,4,640]{2,1,0:T(4,128)S(1)} %get-tuple-element.27), channel_id=1, replica_groups=mesh['half'=2,'act'=32,'x'=4,'core'=2] {'act'}, dimensions={0} | all-to-all | bytes 655360 | tf_op jit(solution)/shard_map/all_to_all | solution.py:426
  48.5 1.0 scan.1
  49.5 0.6 copy-done.2
  50.1 5.6 %all-to-all-start.1 = ((f32[32,4,512]{2,1,0:T(4,128)}), f32[32,4,512]{2,1,0:T(4,128)S(1)}, u32[]{:S(2)}, u32[]{:S(2)}) async-start(f32[32,4,512]{2,1,0:T(4,128)} %get-tuple-element.28), calls=%async_computation.1 | async-start | bytes 524288 | tf_op jit(solution)/shard_map/all_to_all | solution.py:444
  55.7 0.0 copy-done.4
  55.7 0.0 copy-done.5
  55.7 1.8 %weights.1 = (bf16[576,432]{1,0:T(8,128)(2,1)S(1)}, bf16[576,432]{1,0:T(8,128)(2,1)S(1)}, f32[432,128]{1,0:T(8,128)S(1)}, f32[1,128]{1,0:T(1,128)S(1)}, f32[576,1]{1,0:T(8,128)S(1)}) custom-call(s32[576]{0:T(1024)S(1)} %copy-done.4, bf16[576]{0:T(1024)(128)(2,1)S(1)} %copy-done.5, bf16[432,128]{1,0:T(8,128)(2,1)S(1)} %select.1.packed_ref), custom_call_target="tpu_custom_call" | custom-call | flops 7464960 | bytes 1000000 | tf_op jit(solution)/shard_map/weights/pallas_call | solution.py:396
  57.5 0.0 copy-start
  57.5 0.0 copy-start.6
  57.5 6.6 %local.1 = (bf16[432,512]{1,0:T(8,128)(2,1)}, bf16[432,512]{1,0:T(8,128)(2,1)}) custom-call(f32[432,768]{1,0:T(8,128)} %get-tuple-element.29.refs_0_.c_hbm, bf16[432,1024]{1,0:T(8,128)(2,1)} %get-tuple-element.31.refs_1_, f32[432,128]{1,0:T(8,128)} %get-tuple-element.30.refs_2_.aux_hbm, f32[1280]{0:T(1024)} %refs_3_.3, f32[8]{0:T(128)} %refs_4_.1, ...), custom_call_target="tpu_custom_call" | custom-call | flops 2000000000 | bytes 6000000 | tf_op jit(solution)/shard_map/local/pallas_call | solution.py:358
  64.1 0.0 copy-done
  64.1 0.0 copy-done.6
  64.1 2.5 %all-to-all-done.1.state_ref = f32[32,4,512]{2,1,0:T(4,128)S(1)} async-done(((f32[32,4,512]{2,1,0:T(4,128)}), f32[32,4,512]{2,1,0:T(4,128)S(1)}, u32[]{:S(2)}, u32[]{:S(2)}) %all-to-all-start.1) | async-done | bytes 262176 | tf_op jit(solution)/shard_map/all_to_all | solution.py:444
  66.6 3.5 %output.1 = (f32[4,432,128]{2,1,0:T(8,128)S(1)}, bf16[4,432,128]{2,1,0:T(8,128)(2,1)}, f32[32,8,128]{2,1,0:T(8,128)}) custom-call(f32[32,4,512]{2,1,0:T(4,128)S(1)} %all-to-all-done.1.state_ref, f32[432,768]{1,0:T(8,128)} %get-tuple-element.29.refs_0_.c_hbm, f32[432,128]{1,0:T(8,128)} %get-tuple-element.30.refs_2_.aux_hbm, ...), custom_call_target="tpu_custom_call" | custom-call | flops 452984832 | bytes 6000000 | tf_op jit(solution)/shard_map/output/pallas_call | solution.py:358
  70.2 3.9 %collective-permute-start = (bf16[4,432,128]{2,1,0:T(8,128)(2,1)}, bf16[4,432,128]{2,1,0:T(8,128)(2,1)S(1)}, u32[]{:S(2)}, u32[]{:S(2)}) collective-permute-start(bf16[4,432,128]{2,1,0:T(8,128)(2,1)} %get-tuple-element.37), channel_id=1, source_target_pairs={{0,1},{1,0},{2,3},{3,2},{4,5},{5,4},{6,7},{7,6},{8,9},{9,8},{10,11... | collective-permute-start | bytes 1327112 | tf_op jit(solution)/shard_map/ppermute | solution.py:472
  74.1 6.3 %all-to-all-start.2 = ((f32[32,8,128]{2,1,0:T(8,128)}), f32[32,8,128]{2,1,0:T(8,128)S(1)}, u32[]{:S(2)}, u32[]{:S(2)}) async-start(f32[32,8,128]{2,1,0:T(8,128)} %get-tuple-element.43), calls=%async_computation.2 | async-start | bytes 262144 | tf_op jit(solution)/shard_map/all_to_all | solution.py:471
  80.4 0.0 collective-permute-done.got_ref
  80.4 0.8 pair.1
  81.1 3.2 %collective-permute-start.1 = (bf16[432,128]{1,0:T(8,128)(2,1)}, bf16[432,128]{1,0:T(8,128)(2,1)S(1)}, u32[]{:S(2)}, u32[]{:S(2)}) collective-permute-start(bf16[432,128]{1,0:T(8,128)(2,1)} %get-tuple-element.39), channel_id=1, source_target_pairs={{0,2},{2,4},{4,6},{6,0},{1,3},{3,5},{5,7},{7,1},{8,10},{10,12},{12... | collective-permute-start | bytes 331784 | tf_op jit(solution)/shard_map/ppermute | solution.py:486
  84.4 3.5 %collective-permute-start.2 = (bf16[432,128]{1,0:T(8,128)(2,1)}, bf16[432,128]{1,0:T(8,128)(2,1)S(1)}, u32[]{:S(2)}, u32[]{:S(2)}) collective-permute-start(bf16[432,128]{1,0:T(8,128)(2,1)} %get-tuple-element.40), channel_id=1, source_target_pairs={{0,4},{2,6},{4,0},{6,2},{1,5},{3,7},{5,1},{7,3},{8,12},{10,14},{12... | collective-permute-start | bytes 331784 | tf_op jit(solution)/shard_map/ppermute | solution.py:486
  87.9 3.1 %collective-permute-start.3 = (bf16[432,128]{1,0:T(8,128)(2,1)S(1)}, bf16[432,128]{1,0:T(8,128)(2,1)S(1)}, u32[]{:S(2)}, u32[]{:S(2)}) collective-permute-start(bf16[432,128]{1,0:T(8,128)(2,1)S(1)} %get-tuple-element.41), channel_id=1, source_target_pairs={{0,6},{2,0},{4,2},{6,4},{1,7},{3,1},{5,3},{7,5},{8,14},{10,8},{12,... | collective-permute-start | bytes 331784 | tf_op jit(solution)/shard_map/ppermute | solution.py:486
  91.0 0.0 all-to-all-done.2.got_ref
  91.0 0.7 copy-done.3
  91.7 0.1 carry.1
  91.8 8.4 %all_to_all.21.carries_ref = f32[8,1,128]{2,1,0:T(1,128)S(1)} all-to-all(f32[8,1,128]{2,1,0:T(1,128)S(1)} %carry.1), channel_id=1, replica_groups=mesh['half'=2,'act'=32,'x'=4,'core'=2] {'x','core'}, dimensions={0} | all-to-all | bytes 8192 | tf_op jit(solution)/shard_map/all_to_all | solution.py:479
  100.2 0.0 collective-permute-done.1.r1
  100.2 0.0 collective-permute-done.2.r2
  100.2 0.0 collective-permute-done.3.r3
  100.3 1.2 %decode.1 = bf16[576,128]{1,0:T(8,128)(2,1)} custom-call(bf16[576,128]{1,0:T(8,128)(2,1)S(1)} %copy-done.1, bf16[576,432]{1,0:T(8,128)(2,1)S(1)} %get-tuple-element.25.w_hi_ref, bf16[576,432]{1,0:T(8,128)(2,1)S(1)} %get-tuple-element.26.w_lo_ref, f32[432,128]{1,0:T(8,128)S(1)} %get-tuple-element.38.keep_ref, bf16[432,128]{1,0:T(8,128)(2,1)S(1)} %collective-permute-done.1.r1, ...), custom_call_target="tpu_custom_call" | custom-call | flops 200000000 | bytes 2000000 | tf_op jit(solution)/shard_map/decode/pallas_call | solution.py:480
  (6 shorter events, 0.0 us)
Async XLA Ops:
  21.5 34.1 %copy-start.4 = (s32[576]{0:T(1024)S(1)}, s32[576]{0:T(1024)}, u32[]{:S(2)}) copy-start(s32[576]{0:T(1024)} %refs_0_.1) | copy-start | bytes 6916
  21.5 34.2 %copy-start.5 = (bf16[576]{0:T(1024)(128)(2,1)S(1)}, bf16[576]{0:T(1024)(128)(2,1)}, u32[]{:S(2)}) copy-start(bf16[576]{0:T(1024)(128)(2,1)} %refs_1_.1) | copy-start | bytes 3460
  49.5 0.6 copy-start.2
  50.1 16.5 %all-to-all-start.1 = ((f32[32,4,512]{2,1,0:T(4,128)}), f32[32,4,512]{2,1,0:T(4,128)S(1)}, u32[]{:S(2)}, u32[]{:S(2)}) async-start(f32[32,4,512]{2,1,0:T(4,128)} %get-tuple-element.28), calls=%async_computation.1 | async-start | bytes 524288 | tf_op jit(solution)/shard_map/all_to_all | solution.py:444
  57.5 6.6 %copy-start = (f32[432,128]{1,0:T(8,128)}, f32[432,128]{1,0:T(8,128)S(1)}, u32[]{:S(2)}) copy-start(f32[432,128]{1,0:T(8,128)S(1)} %get-tuple-element.34.carry_hbm) | copy-start | bytes 663556
  57.5 6.6 %copy-start.6 = (f32[1,128]{1,0:T(1,128)}, f32[1,128]{1,0:T(1,128)S(1)}, u32[]{:S(2)}) copy-start(f32[1,128]{1,0:T(1,128)S(1)} %get-tuple-element.35.own_hbm) | copy-start | bytes 1540
  66.6 33.6 %copy-start.1 = (bf16[576,128]{1,0:T(8,128)(2,1)S(1)}, bf16[576,128]{1,0:T(8,128)(2,1)}, u32[]{:S(2)}) copy-start(bf16[576,128]{1,0:T(8,128)(2,1)} %enc_ref.1) | copy-start | bytes 442372
  70.2 10.2 %collective-permute-start = (bf16[4,432,128]{2,1,0:T(8,128)(2,1)}, bf16[4,432,128]{2,1,0:T(8,128)(2,1)S(1)}, u32[]{:S(2)}, u32[]{:S(2)}) collective-permute-start(bf16[4,432,128]{2,1,0:T(8,128)(2,1)} %get-tuple-element.37), channel_id=1, source_target_pairs={{0,1},{1,0},{2,3},{3,2},{4,5},{5,4},{6,7},{7,6},{8,9},{9,8},{10,11... | collective-permute-start | bytes 1327112 | tf_op jit(solution)/shard_map/ppermute | solution.py:472
  74.1 16.9 %all-to-all-start.2 = ((f32[32,8,128]{2,1,0:T(8,128)}), f32[32,8,128]{2,1,0:T(8,128)S(1)}, u32[]{:S(2)}, u32[]{:S(2)}) async-start(f32[32,8,128]{2,1,0:T(8,128)} %get-tuple-element.43), calls=%async_computation.2 | async-start | bytes 262144 | tf_op jit(solution)/shard_map/all_to_all | solution.py:471
  81.1 19.1 %collective-permute-start.1 = (bf16[432,128]{1,0:T(8,128)(2,1)}, bf16[432,128]{1,0:T(8,128)(2,1)S(1)}, u32[]{:S(2)}, u32[]{:S(2)}) collective-permute-start(bf16[432,128]{1,0:T(8,128)(2,1)} %get-tuple-element.39), channel_id=1, source_target_pairs={{0,2},{2,4},{4,6},{6,0},{1,3},{3,5},{5,7},{7,1},{8,10},{10,12},{12... | collective-permute-start | bytes 331784 | tf_op jit(solution)/shard_map/ppermute | solution.py:486
  84.4 15.8 %collective-permute-start.2 = (bf16[432,128]{1,0:T(8,128)(2,1)}, bf16[432,128]{1,0:T(8,128)(2,1)S(1)}, u32[]{:S(2)}, u32[]{:S(2)}) collective-permute-start(bf16[432,128]{1,0:T(8,128)(2,1)} %get-tuple-element.40), channel_id=1, source_target_pairs={{0,4},{2,6},{4,0},{6,2},{1,5},{3,7},{5,1},{7,3},{8,12},{10,14},{12... | collective-permute-start | bytes 331784 | tf_op jit(solution)/shard_map/ppermute | solution.py:486
  87.9 12.3 %collective-permute-start.3 = (bf16[432,128]{1,0:T(8,128)(2,1)S(1)}, bf16[432,128]{1,0:T(8,128)(2,1)S(1)}, u32[]{:S(2)}, u32[]{:S(2)}) collective-permute-start(bf16[432,128]{1,0:T(8,128)(2,1)S(1)} %get-tuple-element.41), channel_id=1, source_target_pairs={{0,6},{2,0},{4,2},{6,4},{1,7},{3,1},{5,3},{7,5},{8,14},{10,8},{12,... | collective-permute-start | bytes 331784 | tf_op jit(solution)/shard_map/ppermute | solution.py:486
  91.0 0.7 copy-start.3

commit v8 on v7

--- a/solution.py
+++ b/solution.py
@@ -259,15 +259,17 @@
     arrived(kept)
 
 
-def scan_kernel(got_ref, before_ref, keeps_ref):
+def scan_kernel(got_ref, before_ref, keeps_hbm, keeps_ref, sems):
     act, per, _ = got_ref.shape
     logs = jnp.concatenate([got_ref[j, 0:1, INNER:] for j in range(act)], axis=0)
     keeps_ref[...] = jnp.concatenate([got_ref[j, 1:2, INNER:] for j in range(act)], axis=0)
+    copies = fetch((keeps_ref,), (keeps_hbm,), sems)
     keep = spread_heads(jnp.exp(logs[:, :HEADS_HERE]))
     state = jnp.zeros((per, INNER), F32)
     for j in range(act):
         before_ref[j] = state
         state = state * keep[j : j + 1, :] + got_ref[j, :, :INNER]
+    arrived(copies)
 
 
 def output_kernel(
@@ -313,8 +315,9 @@
         out_ref[...] = (own_ref[chip] + got_ref[chip].astype(F32)).astype(BF16)
 
 
-def carry_kernel(got_ref, keeps_ref, sent_ref):
+def carry_kernel(got_ref, keeps_hbm, sent_ref, keeps_ref, sems):
     me = lax.axis_index("act")
+    arrived(fetch((keeps_hbm,), (keeps_ref,), sems))
     act, parts, _ = got_ref.shape
     keep = jnp.exp(keeps_ref[...])
     carry = jnp.zeros((parts, WIDTH), F32)
@@ -439,7 +442,13 @@
         nbytes=6 * 10**6,
     )(*needed, w_in)
     before, keeps = call(
-        scan_kernel, (shape((act, N // act, INNER)), shape((act, WIDTH))), "scan", nbytes=6 * 10**5
+        scan_kernel,
+        [shape((act, N // act, INNER)), pltpu.HBM((act, WIDTH), F32)],
+        "scan",
+        specs=[held],
+        out_specs=[held, apart],
+        scratch=[pltpu.VMEM((act, WIDTH), F32), dma((1,))],
+        nbytes=6 * 10**5,
     )(got)
     state_in = lax.all_to_all(before, "act", 0, 0)
 
@@ -475,7 +484,14 @@
         pair_kernel, (shape((CAP, WIDTH)), block, block, block), "pair", nbytes=2 * 10**6
     )(packed, own, got_sums)
     parts = [over_chips(a, s) for s, a in enumerate(parts, start=1)]
-    carry = call(carry_kernel, shape((HEAD_PARTS, 1, WIDTH)), "carry", nbytes=2 * 10**5)(all_rows, keeps)
+    carry = call(
+        carry_kernel,
+        shape((HEAD_PARTS, 1, WIDTH)),
+        "carry",
+        specs=[held, apart],
+        scratch=[pltpu.VMEM((act, WIDTH), F32), dma((1,))],
+        nbytes=2 * 10**5,
+    )(all_rows, keeps)
     carries = lax.all_to_all(carry, heads, 0, 0)
     return call(
         decode_kernel, shape((BYTES, WIDTH), BF16), "decode", flops=2 * 10**8, nbytes=2 * 10**6

time: 102 us -> 102 us (level)
  local copies, waits for them, and re-layouts: 1.33 us -> 0.02 us
  Pallas kernels: 22.3 us -> 23.6 us
    pallas_call x4 -> x6, Pallas kernels: 17.5 us -> 19.8 us  [call(): run(*[pltpu.with_memory_space_constraint(a, pltpu.HBM) if spec.memory_spa...]
    unnamed x14 -> x10, local copies, waits for them, and re-layouts: 1.33 us -> 0.02 us
    pallas_call x2 -> x0, Pallas kernels: 1.06 us -> none  [the longest x1 0.97 us: body(): call(scan_kernel, (shape((act, N // act, INNER)), shape((act, WIDTH))), '...]
  transfers between devices with their start and end apart: 6 -> 6, of which waited for: 1 -> 1; matrix products, arithmetic and copies ran while one was open for 0% -> 0% of each run, Pallas kernels for 9% -> 10%
where the time goes in v8:
time: 102 us; the launch traced here: 101 us
  blocking collectives  49.6 us (49%)
  starting transfers between devices  25.6 us (25%)
  Pallas kernels  23.6 us (23%)
  waiting for transfers between devices  2.51 us (2%)
    all_to_all x1, blocking collectives, body(): got = lax.all_to_all(pieces, 'act', 0, 0)  21.1 us
    all_gather x1, blocking collectives, body(): rows = lax.all_gather(packed, heads, axis=1, tiled=True)  20 us
    pallas_call x6, Pallas kernels, call(): run(*[pltpu.with_memory_space_constraint(a, pltpu.HBM) if spec.memory_spa...  19.8 us
    ppermute x3, starting transfers between devices, over_chips(): lax.ppermute(a, 'x', [(i, (i + s) % X_CHIPS) for i in range(X_CHIPS)])  9.82 us
    all_to_all x1, blocking collectives, body(): carries = lax.all_to_all(carry, heads, 0, 0)  8.41 us
    all_to_all x1, starting transfers between devices, body(): all_rows = lax.all_to_all(carry_rows, 'act', 0, 0)  6.3 us
    all_to_all x1, starting transfers between devices, body(): state_in = lax.all_to_all(before, 'act', 0, 0)  5.58 us
    ppermute x1, starting transfers between devices, body(): got_sums = lax.ppermute(sent, 'core', [(0, 1), (1, 0)])  3.87 us
  transfers between devices with their start and end apart: 6, of which 1 were waited for; matrix products, arithmetic and copies ran while one was open for 0% of the time, Pallas kernels for 10%

profile of v8, /device:TPU:1, one launch (start us, length us, event | category | flops | bytes accessed | tf_op | source)
XLA Modules:
  0.0 101.4 jit_solution(10830648288713558549)
XLA Ops:
  0.0 1.5 %select.1.packed_ref = bf16[432,128]{1,0:T(8,128)(2,1)S(1)} custom-call(s32[576]{0:T(1024)} %refs_0_.1, bf16[576,128]{1,0:T(8,128)(2,1)} %enc_ref.1), custom_call_target="tpu_custom_call" | custom-call | flops 100000000 | tf_op jit(solution)/shard_map/select/pallas_call | solution.py:361
  1.5 20.0 %all_gather.3.rows_ref = bf16[432,1024]{1,0:T(8,128)(2,1)S(1)} all-gather(bf16[432,128]{1,0:T(8,128)(2,1)S(1)} %select.1.packed_ref), channel_id=1, replica_groups=mesh['half'=2,'act'=32,'x'=4,'core'=2] {'x','core'}, dimensions={1}, use_global_device_ids=true | all-gather | bytes 995328 | tf_op jit(solution)/shard_map/all_gather | solution.py:397
  21.5 0.0 copy-start.2
  21.5 5.9 %project.1 = (f32[432,768]{1,0:T(8,128)}, bf16[432,1024]{1,0:T(8,128)(2,1)}, f32[432,128]{1,0:T(8,128)}, f32[32,4,640]{2,1,0:T(4,128)S(1)}) custom-call(bf16[432,1024]{1,0:T(8,128)(2,1)S(1)} %all_gather.3.rows_ref, bf16[1024,1280]{1,0:T(8,128)(2,1)} %refs_6_.3, s32[576]{0:T(1024)} %refs_0_.1, bf16[576]{0:T(1024)(128)(2,1)} %refs_1_.1, f32[1024]{0:T(1024)} %refs_2_.1, ...), custom_call_target="tpu_custom_call" | custom-call | flops 679477248 | bytes 8000000 | tf_op jit(solution)/shard_map/project/pallas_call | solution.py:361
  27.4 21.1 %all_to_all.20.got_ref = f32[32,4,640]{2,1,0:T(4,128)S(1)} all-to-all(f32[32,4,640]{2,1,0:T(4,128)S(1)} %get-tuple-element.27), channel_id=1, replica_groups=mesh['half'=2,'act'=32,'x'=4,'core'=2] {'act'}, dimensions={0} | all-to-all | bytes 655360 | tf_op jit(solution)/shard_map/all_to_all | solution.py:429
  48.5 1.6 %scan.1 = (f32[32,4,512]{2,1,0:T(4,128)}, f32[32,128]{1,0:T(8,128)}) custom-call(f32[32,4,640]{2,1,0:T(4,128)S(1)} %all_to_all.20.got_ref), custom_call_target="tpu_custom_call" | custom-call | bytes 600000 | tf_op jit(solution)/shard_map/scan/pallas_call | solution.py:361
  50.1 5.6 %all-to-all-start.1 = ((f32[32,4,512]{2,1,0:T(4,128)}), f32[32,4,512]{2,1,0:T(4,128)S(1)}, u32[]{:S(2)}, u32[]{:S(2)}) async-start(f32[32,4,512]{2,1,0:T(4,128)} %get-tuple-element.28), calls=%async_computation.1 | async-start | bytes 524288 | tf_op jit(solution)/shard_map/all_to_all | solution.py:453
  55.7 0.0 copy-done.2
  55.7 0.0 copy-done.3
  55.7 1.8 %weights.1 = (bf16[576,432]{1,0:T(8,128)(2,1)S(1)}, bf16[576,432]{1,0:T(8,128)(2,1)S(1)}, f32[432,128]{1,0:T(8,128)S(1)}, f32[1,128]{1,0:T(1,128)S(1)}, f32[576,1]{1,0:T(8,128)S(1)}) custom-call(s32[576]{0:T(1024)S(1)} %copy-done.2, bf16[576]{0:T(1024)(128)(2,1)S(1)} %copy-done.3, bf16[432,128]{1,0:T(8,128)(2,1)S(1)} %select.1.packed_ref), custom_call_target="tpu_custom_call" | custom-call | flops 7464960 | bytes 1000000 | tf_op jit(solution)/shard_map/weights/pallas_call | solution.py:399
  57.5 0.0 copy-start
  57.5 0.0 copy-start.4
  57.5 6.6 %local.1 = (bf16[432,512]{1,0:T(8,128)(2,1)}, bf16[432,512]{1,0:T(8,128)(2,1)}) custom-call(f32[432,768]{1,0:T(8,128)} %get-tuple-element.29.refs_0_.c_hbm, bf16[432,1024]{1,0:T(8,128)(2,1)} %get-tuple-element.31.refs_1_, f32[432,128]{1,0:T(8,128)} %get-tuple-element.30.refs_2_.aux_hbm, f32[1280]{0:T(1024)} %refs_3_.3, f32[8]{0:T(128)} %refs_4_.1, ...), custom_call_target="tpu_custom_call" | custom-call | flops 2000000000 | bytes 6000000 | tf_op jit(solution)/shard_map/local/pallas_call | solution.py:361
  64.1 0.0 copy-done
  64.1 0.0 copy-done.4
  64.1 2.5 %all-to-all-done.1.state_ref = f32[32,4,512]{2,1,0:T(4,128)S(1)} async-done(((f32[32,4,512]{2,1,0:T(4,128)}), f32[32,4,512]{2,1,0:T(4,128)S(1)}, u32[]{:S(2)}, u32[]{:S(2)}) %all-to-all-start.1) | async-done | bytes 262176 | tf_op jit(solution)/shard_map/all_to_all | solution.py:453
  66.6 3.6 %output.1 = (f32[4,432,128]{2,1,0:T(8,128)S(1)}, bf16[4,432,128]{2,1,0:T(8,128)(2,1)}, f32[32,8,128]{2,1,0:T(8,128)}) custom-call(f32[32,4,512]{2,1,0:T(4,128)S(1)} %all-to-all-done.1.state_ref, f32[432,768]{1,0:T(8,128)} %get-tuple-element.29.refs_0_.c_hbm, f32[432,128]{1,0:T(8,128)} %get-tuple-element.30.refs_2_.aux_hbm, ...), custom_call_target="tpu_custom_call" | custom-call | flops 452984832 | bytes 6000000 | tf_op jit(solution)/shard_map/output/pallas_call | solution.py:361
  70.2 3.9 %collective-permute-start = (bf16[4,432,128]{2,1,0:T(8,128)(2,1)}, bf16[4,432,128]{2,1,0:T(8,128)(2,1)S(1)}, u32[]{:S(2)}, u32[]{:S(2)}) collective-permute-start(bf16[4,432,128]{2,1,0:T(8,128)(2,1)} %get-tuple-element.37), channel_id=1, source_target_pairs={{0,1},{1,0},{2,3},{3,2},{4,5},{5,4},{6,7},{7,6},{8,9},{9,8},{10,11... | collective-permute-start | bytes 1327112 | tf_op jit(solution)/shard_map/ppermute | solution.py:481
  74.1 6.3 %all-to-all-start.2 = ((f32[32,8,128]{2,1,0:T(8,128)}), f32[32,8,128]{2,1,0:T(8,128)S(1)}, u32[]{:S(2)}, u32[]{:S(2)}) async-start(f32[32,8,128]{2,1,0:T(8,128)} %get-tuple-element.43), calls=%async_computation.2 | async-start | bytes 262144 | tf_op jit(solution)/shard_map/all_to_all | solution.py:480
  80.4 0.0 collective-permute-done.got_ref
  80.4 0.8 pair.1
  81.2 3.3 %collective-permute-start.1 = (bf16[432,128]{1,0:T(8,128)(2,1)}, bf16[432,128]{1,0:T(8,128)(2,1)S(1)}, u32[]{:S(2)}, u32[]{:S(2)}) collective-permute-start(bf16[432,128]{1,0:T(8,128)(2,1)} %get-tuple-element.39), channel_id=1, source_target_pairs={{0,2},{2,4},{4,6},{6,0},{1,3},{3,5},{5,7},{7,1},{8,10},{10,12},{12... | collective-permute-start | bytes 331784 | tf_op jit(solution)/shard_map/ppermute | solution.py:502
  84.4 3.5 %collective-permute-start.2 = (bf16[432,128]{1,0:T(8,128)(2,1)}, bf16[432,128]{1,0:T(8,128)(2,1)S(1)}, u32[]{:S(2)}, u32[]{:S(2)}) collective-permute-start(bf16[432,128]{1,0:T(8,128)(2,1)} %get-tuple-element.40), channel_id=1, source_target_pairs={{0,4},{2,6},{4,0},{6,2},{1,5},{3,7},{5,1},{7,3},{8,12},{10,14},{12... | collective-permute-start | bytes 331784 | tf_op jit(solution)/shard_map/ppermute | solution.py:502
  87.9 3.1 %collective-permute-start.3 = (bf16[432,128]{1,0:T(8,128)(2,1)S(1)}, bf16[432,128]{1,0:T(8,128)(2,1)S(1)}, u32[]{:S(2)}, u32[]{:S(2)}) collective-permute-start(bf16[432,128]{1,0:T(8,128)(2,1)S(1)} %get-tuple-element.41), channel_id=1, source_target_pairs={{0,6},{2,0},{4,2},{6,4},{1,7},{3,1},{5,3},{7,5},{8,14},{10,8},{12,... | collective-permute-start | bytes 331784 | tf_op jit(solution)/shard_map/ppermute | solution.py:502
  91.0 0.0 all-to-all-done.2.got_ref
  91.0 0.8 carry.1
  91.8 8.4 %all_to_all.21.carries_ref = f32[8,1,128]{2,1,0:T(1,128)S(1)} all-to-all(f32[8,1,128]{2,1,0:T(1,128)S(1)} %carry.1), channel_id=1, replica_groups=mesh['half'=2,'act'=32,'x'=4,'core'=2] {'x','core'}, dimensions={0} | all-to-all | bytes 8192 | tf_op jit(solution)/shard_map/all_to_all | solution.py:495
  100.3 0.0 collective-permute-done.1.r1
  100.3 0.0 collective-permute-done.2.r2
  100.3 0.0 collective-permute-done.3.r3
  100.3 0.0 copy-done.1
  100.3 1.2 %decode.1 = bf16[576,128]{1,0:T(8,128)(2,1)} custom-call(bf16[576,128]{1,0:T(8,128)(2,1)S(1)} %copy-done.1, bf16[576,432]{1,0:T(8,128)(2,1)S(1)} %get-tuple-element.25.w_hi_ref, bf16[576,432]{1,0:T(8,128)(2,1)S(1)} %get-tuple-element.26.w_lo_ref, f32[432,128]{1,0:T(8,128)S(1)} %get-tuple-element.38.keep_ref, bf16[432,128]{1,0:T(8,128)(2,1)S(1)} %collective-permute-done.1.r1, ...), custom_call_target="tpu_custom_call" | custom-call | flops 200000000 | bytes 2000000 | tf_op jit(solution)/shard_map/decode/pallas_call | solution.py:496
  (2 shorter events, 0.0 us)
Async XLA Ops:
  21.5 34.1 %copy-start.2 = (s32[576]{0:T(1024)S(1)}, s32[576]{0:T(1024)}, u32[]{:S(2)}) copy-start(s32[576]{0:T(1024)} %refs_0_.1) | copy-start | bytes 6916
  21.5 34.2 %copy-start.3 = (bf16[576]{0:T(1024)(128)(2,1)S(1)}, bf16[576]{0:T(1024)(128)(2,1)}, u32[]{:S(2)}) copy-start(bf16[576]{0:T(1024)(128)(2,1)} %refs_1_.1) | copy-start | bytes 3460
  50.1 16.6 %all-to-all-start.1 = ((f32[32,4,512]{2,1,0:T(4,128)}), f32[32,4,512]{2,1,0:T(4,128)S(1)}, u32[]{:S(2)}, u32[]{:S(2)}) async-start(f32[32,4,512]{2,1,0:T(4,128)} %get-tuple-element.28), calls=%async_computation.1 | async-start | bytes 524288 | tf_op jit(solution)/shard_map/all_to_all | solution.py:453
  57.5 6.6 %copy-start = (f32[432,128]{1,0:T(8,128)}, f32[432,128]{1,0:T(8,128)S(1)}, u32[]{:S(2)}) copy-start(f32[432,128]{1,0:T(8,128)S(1)} %get-tuple-element.34.carry_hbm) | copy-start | bytes 663556
  57.5 6.6 %copy-start.4 = (f32[1,128]{1,0:T(1,128)}, f32[1,128]{1,0:T(1,128)S(1)}, u32[]{:S(2)}) copy-start(f32[1,128]{1,0:T(1,128)S(1)} %get-tuple-element.35.own_hbm) | copy-start | bytes 1540
  66.6 33.7 %copy-start.1 = (bf16[576,128]{1,0:T(8,128)(2,1)S(1)}, bf16[576,128]{1,0:T(8,128)(2,1)}, u32[]{:S(2)}) copy-start(bf16[576,128]{1,0:T(8,128)(2,1)} %enc_ref.1) | copy-start | bytes 442372
  70.2 10.2 %collective-permute-start = (bf16[4,432,128]{2,1,0:T(8,128)(2,1)}, bf16[4,432,128]{2,1,0:T(8,128)(2,1)S(1)}, u32[]{:S(2)}, u32[]{:S(2)}) collective-permute-start(bf16[4,432,128]{2,1,0:T(8,128)(2,1)} %get-tuple-element.37), channel_id=1, source_target_pairs={{0,1},{1,0},{2,3},{3,2},{4,5},{5,4},{6,7},{7,6},{8,9},{9,8},{10,11... | collective-permute-start | bytes 1327112 | tf_op jit(solution)/shard_map/ppermute | solution.py:481
  74.1 16.9 %all-to-all-start.2 = ((f32[32,8,128]{2,1,0:T(8,128)}), f32[32,8,128]{2,1,0:T(8,128)S(1)}, u32[]{:S(2)}, u32[]{:S(2)}) async-start(f32[32,8,128]{2,1,0:T(8,128)} %get-tuple-element.43), calls=%async_computation.2 | async-start | bytes 262144 | tf_op jit(solution)/shard_map/all_to_all | solution.py:480
  81.2 19.1 %collective-permute-start.1 = (bf16[432,128]{1,0:T(8,128)(2,1)}, bf16[432,128]{1,0:T(8,128)(2,1)S(1)}, u32[]{:S(2)}, u32[]{:S(2)}) collective-permute-start(bf16[432,128]{1,0:T(8,128)(2,1)} %get-tuple-element.39), channel_id=1, source_target_pairs={{0,2},{2,4},{4,6},{6,0},{1,3},{3,5},{5,7},{7,1},{8,10},{10,12},{12... | collective-permute-start | bytes 331784 | tf_op jit(solution)/shard_map/ppermute | solution.py:502
  84.4 15.8 %collective-permute-start.2 = (bf16[432,128]{1,0:T(8,128)(2,1)}, bf16[432,128]{1,0:T(8,128)(2,1)S(1)}, u32[]{:S(2)}, u32[]{:S(2)}) collective-permute-start(bf16[432,128]{1,0:T(8,128)(2,1)} %get-tuple-element.40), channel_id=1, source_target_pairs={{0,4},{2,6},{4,0},{6,2},{1,5},{3,7},{5,1},{7,3},{8,12},{10,14},{12... | collective-permute-start | bytes 331784 | tf_op jit(solution)/shard_map/ppermute | solution.py:502
  87.9 12.3 %collective-permute-start.3 = (bf16[432,128]{1,0:T(8,128)(2,1)S(1)}, bf16[432,128]{1,0:T(8,128)(2,1)S(1)}, u32[]{:S(2)}, u32[]{:S(2)}) collective-permute-start(bf16[432,128]{1,0:T(8,128)(2,1)S(1)} %get-tuple-element.41), channel_id=1, source_target_pairs={{0,6},{2,0},{4,2},{6,4},{1,7},{3,1},{5,3},{7,5},{8,14},{10,8},{12,... | collective-permute-start | bytes 331784 | tf_op jit(solution)/shard_map/ppermute | solution.py:502
